TPU v7x, 256 devices: a whole 4x4x8 slice. The times are simulated.
256 devices in a mesh: wide: 32 (over x, y, core), narrow: 8 (over z).
Axes of the slice: x: 4, y: 4, z: 8, core: 2. Of those that a mesh axis runs over, the one named last changes fastest.
Arguments:
- test_matrix: bfloat16 [64, 1048576], P(None, ('wide', 'narrow')), may hold values from -6 to 6
- weights: bfloat16 [8192, 8, 128, 128], P(('wide', 'narrow'))
- block_cols: int32 [8192, 8], P(('wide', 'narrow')), may hold values from 0 to 49
- export_rows: int32 [256, 2], replicated, may hold values from 0 to 31, as said below
- row_count: int32 [256], P(('wide', 'narrow')), may hold values from 1024 to 4096, as said below
Outputs:
- range_basis: float32 [64, 1048576], P(None, ('wide', 'narrow'))
Inputs may be any that keep to these rules, and one draw needn't show every extreme that they name: `export_rows`: the 2 entries of one part are distinct. The present nodes of a part are its first row_count node slots.
All inputs are finite; a program needn't handle non-finite values.
Results may differ from a plain program's by a relative error of at most 0.0041.
Values may be sent and summed in bfloat16 or wider, within the bound.
No kernel may reach another device: no remote copies, remote signals or barrier semaphores. Data moves between devices by JAX's collectives and lax.ppermute only.
A program may use at most 64 MiB of HBM per device.

v0:
```python
import math

import jax
import jax.numpy as jnp
from jax import lax
from jax.sharding import PartitionSpec as P

EPSILON = 1e-06
AXES = ("wide", "narrow")


def shifted(value, axis, step):
    count = lax.axis_size(axis)
    return lax.ppermute(value, axis, [(i, (i + step) % count) for i in range(count)])


def swapped(value, axis, partner):
    return lax.ppermute(value, axis, [(i, partner(i)) for i in range(lax.axis_size(axis))])


def halo_blocks(exports):
    count = lax.axis_size("wide")
    column = jnp.concatenate([shifted(exports, "narrow", 1), exports, shifted(exports, "narrow", -1)], axis=0)
    chip = swapped(column, "wide", lambda i: i ^ 1)
    other = swapped(column, "wide", lambda i: (i + 1) % count if i % 2 else (i - 1) % count)
    return jnp.concatenate([column, chip, other], axis=0)


def summed(value):
    wide_steps = [lambda i: i ^ 1, lambda i: i ^ 2, lambda i: i ^ 6, lambda i: i ^ 8, lambda i: i ^ 24]
    for step in wide_steps:
        value = value + swapped(value, "wide", step)
    for step in [lambda i: i ^ 1, lambda i: i ^ 3]:
        value = value + swapped(value, "narrow", step)
    return value + swapped(value, "narrow", lambda i: (i + 2 if i % 4 >= 2 else i - 2) % 8)


def local(test_matrix, weights, block_cols, export_rows, row_count):
    row_blocks = weights.shape[0]
    block_size = weights.shape[2]
    columns = test_matrix.shape[0]
    exports_each = export_rows.shape[1]
    degree = jnp.sum(jnp.abs(weights), axis=(1, 3), dtype=jnp.float32) + EPSILON
    positions = jnp.arange(row_blocks * block_size, dtype=jnp.int32).reshape(row_blocks, block_size)
    live_rows = (positions < row_count[0]).astype(jnp.float32)
    inverse_root = lax.rsqrt(degree)
    wide_pos = lax.axis_index("wide")
    part = wide_pos * lax.axis_size("narrow") + lax.axis_index("narrow")
    own_exports = lax.dynamic_index_in_dim(export_rows, part, 0, keepdims=False)
    group = 3 * exports_each
    offset = jnp.maximum(block_cols - row_blocks, 0)
    wide_spot = offset // group
    on_chip = (wide_spot == 2) == (wide_pos % 2 == 0)
    source = jnp.where(wide_spot == 1, 0, jnp.where(on_chip, 1, 2))
    slot_index = jnp.where(block_cols < row_blocks, block_cols, row_blocks + source * group + offset % group)

    def apply_blocks(vectors):
        exports = jnp.take(vectors, own_exports, axis=0)
        block_table = jnp.concatenate([vectors, halo_blocks(exports)], axis=0)
        gathered = jnp.take(block_table, slot_index, axis=0)
        return jnp.einsum("rskc,rsic->rki", gathered, weights, preferred_element_type=jnp.float32)

    probe = test_matrix.reshape(columns, row_blocks, block_size).transpose(1, 0, 2)
    first_input = (probe * (inverse_root * live_rows)[:, None]).astype(jnp.bfloat16)
    first_out = apply_blocks(first_input)
    second_input = (first_out / degree[:, None] * live_rows[:, None]).astype(jnp.bfloat16)
    second_out = apply_blocks(second_input)
    sketch = second_out * (inverse_root * live_rows)[:, None]
    sketch = sketch.transpose(1, 0, 2).reshape(columns, row_blocks * block_size)
    gram = summed(jnp.dot(sketch, sketch.T, precision=lax.Precision.HIGHEST))
    lower_factor = jnp.linalg.cholesky(gram)
    node_total = lax.axis_size(AXES) * row_blocks * block_size
    solved = jax.scipy.linalg.solve_triangular(lower_factor, sketch, lower=True)
    return solved * math.sqrt(node_total)


def solution(mesh):
    in_specs = (
        P(None, AXES),
        P(AXES, None, None, None),
        P(AXES, None),
        P(),
        P(AXES),
    )
    return jax.shard_map(local, mesh=mesh, in_specs=in_specs, out_specs=P(None, AXES), check_vma=False)
```

profile of v0, /device:TPU:8, one launch (start us, length us, event | category | flops | bytes accessed | tf_op | source)
XLA Modules:
  0.0 108.5 jit_solution(14156871802223329516)
XLA Ops:
  1.6 5.2 %convert_reduce_fusion = f32[32,128]{1,0:T(8,128)S(1)} fusion(bf16[32,8,128,128]{3,2,1,0:T(8,128)(2,1)} %param.10), kind=kLoop, calls=%fused_computation.4 | loop fusion | flops 12578816 | bytes 8404992 | tf_op jit(solution)/shard_map/reduce_sum | solution.py:43
  7.7 5.9 %collective-permute-start.1 = (bf16[2,64,128]{2,1,0:T(8,128)(2,1)S(1)}, bf16[2,64,128]{2,1,0:T(8,128)(2,1)S(1)}, u32[]{:S(2)}, u32[]{:S(2)}) collective-permute-start(bf16[2,64,128]{2,1,0:T(8,128)(2,1)S(1)} %broadcast_select_fusion.1), channel_id=1, source_target_pairs={{0,7},{1,0},{2,1},{3,2},{4,3},{5,4},{6,5},{7,6},{8,15},{9,8},{10,9... | collective-permute-start | bytes 98312 | tf_op jit(solution)/shard_map/ppermute | solution.py:14
  15.1 3.5 %collective-permute-done = bf16[2,64,128]{2,1,0:T(8,128)(2,1)S(1)} collective-permute-done((bf16[2,64,128]{2,1,0:T(8,128)(2,1)S(1)}, bf16[2,64,128]{2,1,0:T(8,128)(2,1)S(1)}, u32[]{:S(2)}, u32[]{:S(2)}) %collective-permute-start) | collective-permute-done | bytes 32800 | tf_op jit(solution)/shard_map/ppermute | solution.py:14
  18.8 1.7 %collective-permute-start.2 = (bf16[6,64,128]{2,1,0:T(8,128)(2,1)S(1)}, bf16[6,64,128]{2,1,0:T(8,128)(2,1)S(1)}, u32[]{:S(2)}, u32[]{:S(2)}) collective-permute-start(bf16[6,64,128]{2,1,0:T(8,128)(2,1)S(1)} %pad_maximum_fusion), channel_id=1, source_target_pairs={{0,8},{8,0},{16,24},{24,16},{32,40},{40,32},{48,56},{56,48},{64,72... | collective-permute-start | bytes 294920 | tf_op jit(solution)/shard_map/ppermute | solution.py:18
  21.4 1.4 %collective-permute-done.3 = bf16[6,64,128]{2,1,0:T(8,128)(2,1)S(1)} collective-permute-done((bf16[6,64,128]{2,1,0:T(8,128)(2,1)S(1)}, bf16[6,64,128]{2,1,0:T(8,128)(2,1)S(1)}, u32[]{:S(2)}, u32[]{:S(2)}) %collective-permute-start.3) | collective-permute-done | bytes 98336 | tf_op jit(solution)/shard_map/ppermute | solution.py:18
  22.8 3.0 %gather_fusion.1 = bf16[256,64,128]{2,1,0:T(8,128)(2,1)} fusion(bf16[50,64,128]{2,1,0:T(8,128)(2,1)S(1)} %constant_dynamic-update-slice_fusion, s32[1024]{0:T(1024)S(1)} %pad_clamp_fusion), kind=kCustom, calls=%fused_computation.1.clone | custom fusion | bytes 8389632 | tf_op jit(solution)/shard_map/jit(_take)/gather | solution.py:60
  25.9 7.7 %constant_dynamic-update-slice_fusion.11 = (bf16[50,64,128]{2,1,0:T(8,128)(2,1)S(1)}, bf16[32,64,128]{2,1,0:T(8,128)(2,1)S(1)}) fusion(f32[32,128]{1,0:T(8,128)S(1)} %fusion.27, f32[32,128]{1,0:T(8,128)S(1)} %get-tuple-element.11, bf16[32,8,128,128]{3,2,1,0:T(8,128)(2,1)} %param.10, bf16[32,8,64,128]{3,2,1,0:T(8,128)(2,1)} %bitcast.53, ...), kind=kOutput, calls=%fused_computation.49 | convolution fusion | flops 539754496 | bytes 13664512 | tf_op jit(solution)/shard_map/rskc,rsic->rki/dot_general | solution.py:61
  34.3 2.0 %collective-permute-start.4 = (bf16[2,64,128]{2,1,0:T(8,128)(2,1)S(1)}, bf16[2,64,128]{2,1,0:T(8,128)(2,1)S(1)}, u32[]{:S(2)}, u32[]{:S(2)}) collective-permute-start(bf16[2,64,128]{2,1,0:T(8,128)(2,1)S(1)} %broadcast_select_fusion), channel_id=1, source_target_pairs={{0,1},{1,2},{2,3},{3,4},{4,5},{5,6},{6,7},{7,0},{8,9},{9,10},{10,1... | collective-permute-start | bytes 98312 | tf_op jit(solution)/shard_map/ppermute | solution.py:14
  36.3 1.9 %collective-permute-done.5 = bf16[2,64,128]{2,1,0:T(8,128)(2,1)S(1)} collective-permute-done((bf16[2,64,128]{2,1,0:T(8,128)(2,1)S(1)}, bf16[2,64,128]{2,1,0:T(8,128)(2,1)S(1)}, u32[]{:S(2)}, u32[]{:S(2)}) %collective-permute-start.5) | collective-permute-done | bytes 32800 | tf_op jit(solution)/shard_map/ppermute | solution.py:14
  39.6 1.7 %collective-permute-start.6 = (bf16[6,64,128]{2,1,0:T(8,128)(2,1)S(1)}, bf16[6,64,128]{2,1,0:T(8,128)(2,1)S(1)}, u32[]{:S(2)}, u32[]{:S(2)}) collective-permute-start(bf16[6,64,128]{2,1,0:T(8,128)(2,1)S(1)} %pad_maximum_fusion.1), channel_id=1, source_target_pairs={{0,8},{8,0},{16,24},{24,16},{32,40},{40,32},{48,56},{56,48},{64,72... | collective-permute-start | bytes 294920 | tf_op jit(solution)/shard_map/ppermute | solution.py:18
  42.2 1.4 %collective-permute-done.7 = bf16[6,64,128]{2,1,0:T(8,128)(2,1)S(1)} collective-permute-done((bf16[6,64,128]{2,1,0:T(8,128)(2,1)S(1)}, bf16[6,64,128]{2,1,0:T(8,128)(2,1)S(1)}, u32[]{:S(2)}, u32[]{:S(2)}) %collective-permute-start.7) | collective-permute-done | bytes 98336 | tf_op jit(solution)/shard_map/ppermute | solution.py:18
  43.6 3.0 %gather_fusion.3 = bf16[256,64,128]{2,1,0:T(8,128)(2,1)} fusion(bf16[50,64,128]{2,1,0:T(8,128)(2,1)S(1)} %constant_dynamic-update-slice_fusion.6, s32[1024]{0:T(1024)S(1)} %pad_clamp_fusion), kind=kCustom, calls=%fused_computation.3.clone | custom fusion | bytes 8389632 | tf_op jit(solution)/shard_map/jit(_take)/gather | solution.py:60
  46.7 7.7 %fusion.14 = f32[32,64,128]{2,1,0:T(8,128)S(1)} fusion(bf16[32,8,128,128]{3,2,1,0:T(8,128)(2,1)} %param.10, bf16[32,8,64,128]{3,2,1,0:T(8,128)(2,1)} %bitcast.54, pred[32,8]{1,0:T(8,128)(4,1)S(1)} %copy.20, f32[32,128]{1,0:T(8,128)S(1)} %get-tuple-element.12), kind=kOutput, calls=%fused_computation.16 | convolution fusion | flops 539230208 | bytes 13648128 | tf_op jit(solution)/shard_map/rskc,rsic->rki/dot_general | solution.py:61
  56.7 7.1 %collective-permute-start.9 = (f32[64,64]{0,1:T(8,128)S(1)}, f32[64,64]{0,1:T(8,128)S(1)}, u32[]{:S(2)}, u32[]{:S(2)}) collective-permute-start(f32[64,64]{0,1:T(8,128)S(1)} %add.99), channel_id=1, source_target_pairs={{0,16},{8,24},{16,0},{24,8},{32,48},{40,56},{48,32},{56,40},{64,80... | collective-permute-start | bytes 49160 | tf_op jit(solution)/shard_map/ppermute | solution.py:18
  63.8 1.9 %collective-permute-done.9 = f32[64,64]{0,1:T(8,128)S(1)} collective-permute-done((f32[64,64]{0,1:T(8,128)S(1)}, f32[64,64]{0,1:T(8,128)S(1)}, u32[]{:S(2)}, u32[]{:S(2)}) %collective-permute-start.9) | collective-permute-done | bytes 16416 | tf_op jit(solution)/shard_map/ppermute | solution.py:18
  65.7 3.9 %collective-permute-done.10 = f32[64,64]{0,1:T(8,128)S(1)} collective-permute-done((f32[64,64]{0,1:T(8,128)S(1)}, f32[64,64]{0,1:T(8,128)S(1)}, u32[]{:S(2)}, u32[]{:S(2)}) %collective-permute-start.10) | collective-permute-done | bytes 16416 | tf_op jit(solution)/shard_map/ppermute | solution.py:18
  69.6 3.9 %collective-permute-done.11 = f32[64,64]{0,1:T(8,128)S(1)} collective-permute-done((f32[64,64]{0,1:T(8,128)S(1)}, f32[64,64]{0,1:T(8,128)S(1)}, u32[]{:S(2)}, u32[]{:S(2)}) %collective-permute-start.11) | collective-permute-done | bytes 16416 | tf_op jit(solution)/shard_map/ppermute | solution.py:18
  73.8 4.8 %collective-permute-done.12 = f32[64,64]{0,1:T(8,128)S(1)} collective-permute-done((f32[64,64]{0,1:T(8,128)S(1)}, f32[64,64]{0,1:T(8,128)S(1)}, u32[]{:S(2)}, u32[]{:S(2)}) %collective-permute-start.12) | collective-permute-done | bytes 16416 | tf_op jit(solution)/shard_map/ppermute | solution.py:18
  79.4 3.2 %collective-permute-done.13 = f32[64,64]{0,1:T(8,128)S(1)} collective-permute-done((f32[64,64]{0,1:T(8,128)S(1)}, f32[64,64]{0,1:T(8,128)S(1)}, u32[]{:S(2)}, u32[]{:S(2)}) %collective-permute-start.13) | collective-permute-done | bytes 16416 | tf_op jit(solution)/shard_map/ppermute | solution.py:18
  82.6 5.7 %collective-permute-done.14 = f32[64,64]{0,1:T(8,128)S(1)} collective-permute-done((f32[64,64]{0,1:T(8,128)S(1)}, f32[64,64]{0,1:T(8,128)S(1)}, u32[]{:S(2)}, u32[]{:S(2)}) %collective-permute-start.14) | collective-permute-done | bytes 16416 | tf_op jit(solution)/shard_map/ppermute | solution.py:18
  88.3 6.0 %collective-permute-done.15 = f32[64,64]{0,1:T(8,128)S(1)} collective-permute-done((f32[64,64]{0,1:T(8,128)S(1)}, f32[64,64]{0,1:T(8,128)S(1)}, u32[]{:S(2)}, u32[]{:S(2)}) %collective-permute-start.15) | collective-permute-done | bytes 16416 | tf_op jit(solution)/shard_map/ppermute | solution.py:18
  94.4 5.8 %cholesky.16 = f32[64,64]{1,0:T(8,128)S(1)} custom-call(f32[64,64]{1,0:T(8,128)S(1)} %fusion.26), custom_call_target="Cholesky" | custom-call | tf_op jit(solution)/shard_map/jit(cholesky)/cholesky | solution.py:71
  101.6 4.9 %custom-call.7 = f32[1,64,64]{1,2,0:T(8,128)S(1)} custom-call(f32[1,64,64]{2,1,0:T(8,128)S(1)} %fusion.24), custom_call_target="InvertDiagBlocksLowerTriangular" | custom-call | tf_op jit(solution)/shard_map/jit(_solve_triangular)/triangular_solve | solution.py:73
  106.5 2.0 %convolution_multiply_fusion = f32[64,4096]{1,0:T(8,128)} fusion(f32[1,64,64]{1,2,0:T(8,128)S(1)} %custom-call.7, f32[32,64,128]{2,1,0:T(8,128)S(1)} %fusion.14), kind=kOutput, calls=%fused_computation.5 | convolution fusion | flops 201588736 | bytes 2113536 | tf_op jit(solution)/shard_map/jit(_solve_triangular)/triangular_solve | solution.py:73
  (64 shorter events, 12.3 us)
Async XLA Ops:
  0.0 0.7 copy-start
  1.6 5.2 %copy-start.1 = (bf16[64,4096]{1,0:T(8,128)(2,1)S(1)}, bf16[64,4096]{1,0:T(8,128)(2,1)}, u32[]{:S(2)}) copy-start(bf16[64,4096]{1,0:T(8,128)(2,1)} %param.9) | copy-start | bytes 1572868
  1.6 12.0 %copy-start.2 = (s32[32,8]{0,1:T(8,128)S(1)}, s32[32,8]{0,1:T(8,128)}, u32[]{:S(2)}) copy-start(s32[32,8]{0,1:T(8,128)} %param.11) | copy-start | bytes 3076
  7.7 7.5 %collective-permute-start.1 = (bf16[2,64,128]{2,1,0:T(8,128)(2,1)S(1)}, bf16[2,64,128]{2,1,0:T(8,128)(2,1)S(1)}, u32[]{:S(2)}, u32[]{:S(2)}) collective-permute-start(bf16[2,64,128]{2,1,0:T(8,128)(2,1)S(1)} %broadcast_select_fusion.1), channel_id=1, source_target_pairs={{0,7},{1,0},{2,1},{3,2},{4,3},{5,4},{6,5},{7,6},{8,15},{9,8},{10,9... | collective-permute-start | bytes 98312 | tf_op jit(solution)/shard_map/ppermute | solution.py:14
  13.5 5.1 %collective-permute-start = (bf16[2,64,128]{2,1,0:T(8,128)(2,1)S(1)}, bf16[2,64,128]{2,1,0:T(8,128)(2,1)S(1)}, u32[]{:S(2)}, u32[]{:S(2)}) collective-permute-start(bf16[2,64,128]{2,1,0:T(8,128)(2,1)S(1)} %broadcast_select_fusion.1), channel_id=1, source_target_pairs={{0,1},{1,2},{2,3},{3,4},{4,5},{5,6},{6,7},{7,0},{8,9},{9,10},{10,1... | collective-permute-start | bytes 98312 | tf_op jit(solution)/shard_map/ppermute | solution.py:14
  18.7 4.1 %collective-permute-start.3 = (bf16[6,64,128]{2,1,0:T(8,128)(2,1)S(1)}, bf16[6,64,128]{2,1,0:T(8,128)(2,1)S(1)}, u32[]{:S(2)}, u32[]{:S(2)}) collective-permute-start(bf16[6,64,128]{2,1,0:T(8,128)(2,1)S(1)} %pad_maximum_fusion), channel_id=1, source_target_pairs={{0,248},{8,16},{16,8},{24,32},{32,24},{40,48},{48,40},{56,64},{64,... | collective-permute-start | bytes 294920 | tf_op jit(solution)/shard_map/ppermute | solution.py:18
  18.8 2.6 %collective-permute-start.2 = (bf16[6,64,128]{2,1,0:T(8,128)(2,1)S(1)}, bf16[6,64,128]{2,1,0:T(8,128)(2,1)S(1)}, u32[]{:S(2)}, u32[]{:S(2)}) collective-permute-start(bf16[6,64,128]{2,1,0:T(8,128)(2,1)S(1)} %pad_maximum_fusion), channel_id=1, source_target_pairs={{0,8},{8,0},{16,24},{24,16},{32,40},{40,32},{48,56},{56,48},{64,72... | collective-permute-start | bytes 294920 | tf_op jit(solution)/shard_map/ppermute | solution.py:18
  34.2 3.9 %collective-permute-start.5 = (bf16[2,64,128]{2,1,0:T(8,128)(2,1)S(1)}, bf16[2,64,128]{2,1,0:T(8,128)(2,1)S(1)}, u32[]{:S(2)}, u32[]{:S(2)}) collective-permute-start(bf16[2,64,128]{2,1,0:T(8,128)(2,1)S(1)} %broadcast_select_fusion), channel_id=1, source_target_pairs={{0,7},{1,0},{2,1},{3,2},{4,3},{5,4},{6,5},{7,6},{8,15},{9,8},{10,9... | collective-permute-start | bytes 98312 | tf_op jit(solution)/shard_map/ppermute | solution.py:14
  34.3 5.2 %collective-permute-start.4 = (bf16[2,64,128]{2,1,0:T(8,128)(2,1)S(1)}, bf16[2,64,128]{2,1,0:T(8,128)(2,1)S(1)}, u32[]{:S(2)}, u32[]{:S(2)}) collective-permute-start(bf16[2,64,128]{2,1,0:T(8,128)(2,1)S(1)} %broadcast_select_fusion), channel_id=1, source_target_pairs={{0,1},{1,2},{2,3},{3,4},{4,5},{5,6},{6,7},{7,0},{8,9},{9,10},{10,1... | collective-permute-start | bytes 98312 | tf_op jit(solution)/shard_map/ppermute | solution.py:14
  39.5 4.1 %collective-permute-start.7 = (bf16[6,64,128]{2,1,0:T(8,128)(2,1)S(1)}, bf16[6,64,128]{2,1,0:T(8,128)(2,1)S(1)}, u32[]{:S(2)}, u32[]{:S(2)}) collective-permute-start(bf16[6,64,128]{2,1,0:T(8,128)(2,1)S(1)} %pad_maximum_fusion.1), channel_id=1, source_target_pairs={{0,248},{8,16},{16,8},{24,32},{32,24},{40,48},{48,40},{56,64},{64,... | collective-permute-start | bytes 294920 | tf_op jit(solution)/shard_map/ppermute | solution.py:18
  39.6 2.6 %collective-permute-start.6 = (bf16[6,64,128]{2,1,0:T(8,128)(2,1)S(1)}, bf16[6,64,128]{2,1,0:T(8,128)(2,1)S(1)}, u32[]{:S(2)}, u32[]{:S(2)}) collective-permute-start(bf16[6,64,128]{2,1,0:T(8,128)(2,1)S(1)} %pad_maximum_fusion.1), channel_id=1, source_target_pairs={{0,8},{8,0},{16,24},{24,16},{32,40},{40,32},{48,56},{56,48},{64,72... | collective-permute-start | bytes 294920 | tf_op jit(solution)/shard_map/ppermute | solution.py:18
  55.4 1.3 %collective-permute-start.8 = (f32[64,64]{0,1:T(8,128)S(1)}, f32[64,64]{0,1:T(8,128)S(1)}, u32[]{:S(2)}, u32[]{:S(2)}) collective-permute-start(f32[64,64]{0,1:T(8,128)S(1)} %convolution_bitcast_fusion), channel_id=1, source_target_pairs={{0,8},{8,0},{16,24},{24,16},{32,40},{40,32},{48,56},{56,48},{64,72... | collective-permute-start | bytes 49160 | tf_op jit(solution)/shard_map/ppermute | solution.py:18
  56.7 9.0 %collective-permute-start.9 = (f32[64,64]{0,1:T(8,128)S(1)}, f32[64,64]{0,1:T(8,128)S(1)}, u32[]{:S(2)}, u32[]{:S(2)}) collective-permute-start(f32[64,64]{0,1:T(8,128)S(1)} %add.99), channel_id=1, source_target_pairs={{0,16},{8,24},{16,0},{24,8},{32,48},{40,56},{48,32},{56,40},{64,80... | collective-permute-start | bytes 49160 | tf_op jit(solution)/shard_map/ppermute | solution.py:18
  65.7 3.9 %collective-permute-start.10 = (f32[64,64]{0,1:T(8,128)S(1)}, f32[64,64]{0,1:T(8,128)S(1)}, u32[]{:S(2)}, u32[]{:S(2)}) collective-permute-start(f32[64,64]{0,1:T(8,128)S(1)} %add.100), channel_id=1, source_target_pairs={{0,48},{8,56},{16,32},{24,40},{32,16},{40,24},{48,0},{56,8},{64,11... | collective-permute-start | bytes 49160 | tf_op jit(solution)/shard_map/ppermute | solution.py:18
  69.6 3.9 %collective-permute-start.11 = (f32[64,64]{0,1:T(8,128)S(1)}, f32[64,64]{0,1:T(8,128)S(1)}, u32[]{:S(2)}, u32[]{:S(2)}) collective-permute-start(f32[64,64]{0,1:T(8,128)S(1)} %add.101), channel_id=1, source_target_pairs={{0,64},{8,72},{16,80},{24,88},{32,96},{40,104},{48,112},{56,120},{... | collective-permute-start | bytes 49160 | tf_op jit(solution)/shard_map/ppermute | solution.py:18
  73.5 5.1 %collective-permute-start.12 = (f32[64,64]{0,1:T(8,128)S(1)}, f32[64,64]{0,1:T(8,128)S(1)}, u32[]{:S(2)}, u32[]{:S(2)}) collective-permute-start(f32[64,64]{0,1:T(8,128)S(1)} %add.102), channel_id=1, source_target_pairs={{0,192},{8,200},{16,208},{24,216},{32,224},{40,232},{48,240},{56,2... | collective-permute-start | bytes 49160 | tf_op jit(solution)/shard_map/ppermute | solution.py:18
  78.6 3.9 %collective-permute-start.13 = (f32[64,64]{0,1:T(8,128)S(1)}, f32[64,64]{0,1:T(8,128)S(1)}, u32[]{:S(2)}, u32[]{:S(2)}) collective-permute-start(f32[64,64]{0,1:T(8,128)S(1)} %add.103), channel_id=1, source_target_pairs={{0,1},{1,0},{2,3},{3,2},{4,5},{5,4},{6,7},{7,6},{8,9},{9,8},{10,11... | collective-permute-start | bytes 49160 | tf_op jit(solution)/shard_map/ppermute | solution.py:18
  82.5 5.7 %collective-permute-start.14 = (f32[64,64]{0,1:T(8,128)S(1)}, f32[64,64]{0,1:T(8,128)S(1)}, u32[]{:S(2)}, u32[]{:S(2)}) collective-permute-start(f32[64,64]{0,1:T(8,128)S(1)} %add.104), channel_id=1, source_target_pairs={{0,3},{1,2},{2,1},{3,0},{4,7},{5,6},{6,5},{7,4},{8,11},{9,10},{10,... | collective-permute-start | bytes 49160 | tf_op jit(solution)/shard_map/ppermute | solution.py:18
  88.3 6.0 %collective-permute-start.15 = (f32[64,64]{0,1:T(8,128)S(1)}, f32[64,64]{0,1:T(8,128)S(1)}, u32[]{:S(2)}, u32[]{:S(2)}) collective-permute-start(f32[64,64]{0,1:T(8,128)S(1)} %add.105), channel_id=1, source_target_pairs={{0,6},{1,7},{2,4},{3,5},{4,2},{5,3},{6,0},{7,1},{8,14},{9,15},{10,... | collective-permute-start | bytes 49160 | tf_op jit(solution)/shard_map/ppermute | solution.py:18
where the time goes:
time: 110 us; the launch traced here: 109 us
  waiting for transfers between devices  42.9 us (39%)
  starting transfers between devices  19.8 us (18%)
  matrix products  18.4 us (17%)
  other arithmetic  17.9 us (16%)
  local copies, waits for them, and re-layouts  8.53 us (8%)
    ppermute x12, waiting for transfers between devices, swapped(): lax.ppermute(value, axis, [(i, partner(i)) for i in range(lax.axis_size(a...  34.9 us
    dot_general x2, matrix products, apply_blocks(): jnp.einsum('rskc,rsic->rki', gathered, weights, preferred_element_type=jn...  15.4 us
    ppermute x12, starting transfers between devices, swapped(): lax.ppermute(value, axis, [(i, partner(i)) for i in range(lax.axis_size(a...  11.9 us
    ppermute x4, waiting for transfers between devices, shifted(): lax.ppermute(value, axis, [(i, (i + step) % count) for i in range(count)])  7.99 us
    ppermute x4, starting transfers between devices, shifted(): lax.ppermute(value, axis, [(i, (i + step) % count) for i in range(count)])  7.92 us
    another operation x3, other arithmetic, local(): lower_factor = jnp.linalg.cholesky(gram)  6.52 us
    gather x2, local copies, waits for them, and re-layouts, apply_blocks(): gathered = jnp.take(block_table, slot_index, axis=0)  6.1 us
    another operation x2, other arithmetic, local(): solved = jax.scipy.linalg.solve_triangular(lower_factor, sketch, lower=True)  5.55 us
  transfers between devices with their start and end apart: 16, of which 16 were waited for; matrix products, arithmetic and copies ran while one was open for 0% of the time, Pallas kernels for 0%

commit v1 on v0

v1 whole, which is shorter than its diff:
```python
import functools
import math

import jax
import jax.numpy as jnp
from jax import lax
from jax.experimental import pallas as pl
from jax.experimental.pallas import tpu as pltpu
from jax.sharding import PartitionSpec as P

EPSILON = 1e-06
AXES = ("wide", "narrow")
ROWS_STEP = 8
VMEM = pl.BlockSpec(memory_space=pltpu.VMEM)
LIMIT = 24 * 1024 * 1024
LAST = (((1,), (1,)), ((), ()))


def lanes(blocks):
    return jnp.concatenate([blocks[i] for i in range(blocks.shape[0])], axis=1)


def block_degree(blocks):
    ones = jnp.ones((8, blocks.shape[0] * blocks.shape[2]), blocks.dtype)
    sums = lax.dot_general(ones, lanes(jnp.abs(blocks)), LAST, preferred_element_type=jnp.float32)
    return sums[0:1] + EPSILON


def live_mask(row, block_size, present):
    position = lax.broadcasted_iota(jnp.int32, (1, block_size), 1) + row * block_size
    return (position < present).astype(jnp.float32)


def scaled(probe, degree, live):
    return (probe.astype(jnp.float32) * lax.rsqrt(degree) * live).astype(jnp.bfloat16)


def export_first_kernel(exports, count, probe, weights, out):
    row = exports[pl.program_id(0)]
    live = live_mask(row, probe.shape[1], count[0])
    out[0] = scaled(probe[...], block_degree(weights[0]), live)


def first_kernel(count, probe, weights, degree_out, out):
    step, rows = pl.program_id(0), weights.shape[0]
    size = weights.shape[2]
    for i in range(rows):
        degree = block_degree(weights[i])
        degree_out[i : i + 1, :] = degree
        live = live_mask(step * rows + i, size, count[0])
        out[i] = scaled(probe[:, i * size : (i + 1) * size], degree, live)


def fill_table(table, parts):
    start = 0
    for part in parts:
        table[start : start + part.shape[0]] = part[...]
        start += part.shape[0]


def applied(table, slots, row, blocks):
    vectors = jnp.concatenate([table[slots[row, s]] for s in range(blocks.shape[0])], axis=1)
    return lax.dot_general(vectors, lanes(blocks), LAST, preferred_element_type=jnp.float32)


def export_second_kernel(exports, count, slots, own, column, chip, other, degree, weights, out, table):
    @pl.when(pl.program_id(0) == 0)
    def _():
        fill_table(table, (own, column, chip, other))

    row = exports[pl.program_id(0)]
    live = live_mask(row, weights.shape[2], count[0])
    product = applied(table, slots, row, weights[0])
    out[0] = (product / degree[pl.ds(row, 1), :] * live).astype(jnp.bfloat16)


def second_kernel(count, slots, own, column, chip, other, degree, weights, out, table):
    step, rows = pl.program_id(0), weights.shape[0]

    @pl.when(step == 0)
    def _():
        fill_table(table, (own, column, chip, other))

    for i in range(rows):
        row = step * rows + i
        live = live_mask(row, weights.shape[2], count[0])
        product = applied(table, slots, row, weights[i])
        out[i] = (product / degree[i : i + 1, :] * live).astype(jnp.bfloat16)


def halves(value):
    high = value.astype(jnp.bfloat16)
    return high, (value - high.astype(jnp.float32)).astype(jnp.bfloat16)


def sketch_kernel(count, slots, own, column, chip, other, degree, weights, sketch, gram, table, main, cross):
    step, rows = pl.program_id(0), weights.shape[0]
    size = weights.shape[2]

    @pl.when(step == 0)
    def _():
        fill_table(table, (own, column, chip, other))
        main[...] = jnp.zeros_like(main)
        cross[...] = jnp.zeros_like(cross)

    for i in range(rows):
        row = step * rows + i
        live = live_mask(row, size, count[0])
        product = applied(table, slots, row, weights[i])
        sketch[:, i * size : (i + 1) * size] = product * lax.rsqrt(degree[i : i + 1, :]) * live
    high, low = halves(sketch[...])
    main[...] += lax.dot_general(high, high, LAST, preferred_element_type=jnp.float32)
    cross[...] += lax.dot_general(high, low, LAST, preferred_element_type=jnp.float32)

    @pl.when(step == pl.num_programs(0) - 1)
    def _():
        total = main[...] + cross[...] + cross[...].T
        half = total.shape[0] // 2
        gram[...] = jnp.concatenate([total[:half], total[half:]], axis=1)


def factor_kernel(scale, grams, sketch, out, inverse):
    packed = grams[0]
    for i in range(1, grams.shape[0]):
        packed = packed + grams[i]
    half = packed.shape[0]
    count = 2 * half
    total = jnp.concatenate([packed[:, :count], packed[:, count:]], axis=0)
    identity = (
        lax.broadcasted_iota(jnp.int32, (count, count), 0) == lax.broadcasted_iota(jnp.int32, (count, count), 1)
    ).astype(jnp.float32)
    rest = jnp.concatenate([identity, total], axis=1)
    width = 8
    for start in range(0, count, width):
        height = rest.shape[0]
        sides = [
            jnp.broadcast_to(rest[:, count + start + j : count + start + j + 1], rest.shape) for j in range(width)
        ]
        below = lax.broadcasted_iota(jnp.int32, rest.shape, 0)
        for j in range(width):
            pivot = sides[j][j : j + 1, :]
            factors = jnp.where(below > j, sides[j] * (1.0 / pivot), 0.0)
            line = rest[j : j + 1, :]
            inverse[start + j : start + j + 1, :] = line * (lax.rsqrt(pivot) * scale)
            rest = rest - factors * line
            for k in range(j + 1, width):
                sides[k] = sides[k] - factors * sides[k][j : j + 1, :]
        if start + width < count:
            rest = rest[width:, :]
    high, low = halves(inverse[:, :count])
    value_high, value_low = halves(sketch[...])
    out[...] = (
        jnp.dot(high, value_high, preferred_element_type=jnp.float32)
        + jnp.dot(high, value_low, preferred_element_type=jnp.float32)
        + jnp.dot(low, value_high, preferred_element_type=jnp.float32)
    )


def cost(flops, moved):
    return pl.CostEstimate(flops=flops, bytes_accessed=moved, transcendentals=0)


def call(kernel, prefetch, grid, in_specs, out_specs, out_shape, scratch, flops, moved):
    return pl.pallas_call(
        kernel,
        grid_spec=pltpu.PrefetchScalarGridSpec(
            num_scalar_prefetch=prefetch, grid=grid, in_specs=in_specs, out_specs=out_specs, scratch_shapes=scratch
        ),
        out_shape=out_shape,
        compiler_params=pltpu.CompilerParams(vmem_limit_bytes=LIMIT, dimension_semantics=("arbitrary",) * len(grid)),
        cost_estimate=cost(flops, moved),
    )


def whole(shape):
    return pl.BlockSpec(shape, lambda *_: (0,) * len(shape))


class Kernels:
    def __init__(self, columns, row_blocks, slots, size, exports, halo):
        self.k, self.rb, self.nb, self.bs, self.eb = columns, row_blocks, slots, size, exports
        self.halo = halo
        self.step = min(ROWS_STEP, row_blocks)
        self.bytes_weights = row_blocks * slots * size * size * 2
        self.flops = 2 * columns * row_blocks * slots * size * size
        self.tables = [whole((row_blocks, columns, size))] + [whole((halo // 3, columns, size))] * 3
        self.table = pltpu.VMEM((row_blocks + halo, columns, size), jnp.bfloat16)

    def weights(self):
        return pl.BlockSpec((self.step, self.nb, self.bs, self.bs), lambda i, *_: (i, 0, 0, 0))

    def one_weights(self):
        return pl.BlockSpec((1, self.nb, self.bs, self.bs), lambda i, exports, *_: (exports[i], 0, 0, 0))

    def export_first(self, exports, count, probe, weights):
        return call(
            export_first_kernel,
            2,
            (self.eb,),
            [pl.BlockSpec((self.k, self.bs), lambda i, exports, *_: (0, exports[i])), self.one_weights()],
            pl.BlockSpec((1, self.k, self.bs), lambda i, *_: (i, 0, 0)),
            jax.ShapeDtypeStruct((self.eb, self.k, self.bs), jnp.bfloat16),
            [],
            self.flops // 16,
            self.bytes_weights // 16,
        )(exports, count, probe, weights)

    def first(self, count, probe, weights):
        return call(
            first_kernel,
            1,
            (self.rb // self.step,),
            [pl.BlockSpec((self.k, self.step * self.bs), lambda i, *_: (0, i)), self.weights()],
            [
                pl.BlockSpec((self.step, self.bs), lambda i, *_: (i, 0)),
                pl.BlockSpec((self.step, self.k, self.bs), lambda i, *_: (i, 0, 0)),
            ],
            [
                jax.ShapeDtypeStruct((self.rb, self.bs), jnp.float32),
                jax.ShapeDtypeStruct((self.rb, self.k, self.bs), jnp.bfloat16),
            ],
            [],
            self.flops,
            self.bytes_weights,
        )(count, probe, weights)

    def export_second(self, exports, count, slots, tables, degree, weights):
        return call(
            export_second_kernel,
            3,
            (self.eb,),
            self.tables + [whole((self.rb, self.bs)), self.one_weights()],
            pl.BlockSpec((1, self.k, self.bs), lambda i, *_: (i, 0, 0)),
            jax.ShapeDtypeStruct((self.eb, self.k, self.bs), jnp.bfloat16),
            [self.table],
            self.flops // 16,
            self.bytes_weights // 16,
        )(exports, count, slots, *tables, degree, weights)

    def second(self, count, slots, tables, degree, weights):
        return call(
            second_kernel,
            2,
            (self.rb // self.step,),
            self.tables + [pl.BlockSpec((self.step, self.bs), lambda i, *_: (i, 0)), self.weights()],
            pl.BlockSpec((self.step, self.k, self.bs), lambda i, *_: (i, 0, 0)),
            jax.ShapeDtypeStruct((self.rb, self.k, self.bs), jnp.bfloat16),
            [self.table],
            self.flops,
            self.bytes_weights,
        )(count, slots, *tables, degree, weights)

    def sketch(self, count, slots, tables, degree, weights):
        k = self.k
        return call(
            sketch_kernel,
            2,
            (self.rb // self.step,),
            self.tables + [pl.BlockSpec((self.step, self.bs), lambda i, *_: (i, 0)), self.weights()],
            [pl.BlockSpec((k, self.step * self.bs), lambda i, *_: (0, i)), whole((k // 2, 2 * k))],
            [
                jax.ShapeDtypeStruct((k, self.rb * self.bs), jnp.float32),
                jax.ShapeDtypeStruct((k // 2, 2 * k), jnp.float32),
            ],
            [self.table, pltpu.VMEM((k, k), jnp.float32), pltpu.VMEM((k, k), jnp.float32)],
            self.flops,
            self.bytes_weights,
        )(count, slots, *tables, degree, weights)

    def factor(self, scale, grams, sketch):
        return pl.pallas_call(
            functools.partial(factor_kernel, scale),
            in_specs=[VMEM, VMEM],
            out_specs=VMEM,
            out_shape=jax.ShapeDtypeStruct(sketch.shape, jnp.float32),
            scratch_shapes=[pltpu.VMEM((self.k, 2 * self.k), jnp.float32)],
            compiler_params=pltpu.CompilerParams(vmem_limit_bytes=LIMIT),
            cost_estimate=cost(6 * self.k * sketch.size, 8 * sketch.size),
        )(grams, sketch)


def shifted(value, axis, step):
    count = lax.axis_size(axis)
    return lax.ppermute(value, axis, [(i, (i + step) % count) for i in range(count)])


def swapped(value, axis, partner):
    return lax.ppermute(value, axis, [(i, partner(i)) for i in range(lax.axis_size(axis))])


def halo_blocks(exports):
    count = lax.axis_size("wide")
    column = jnp.concatenate([shifted(exports, "narrow", 1), exports, shifted(exports, "narrow", -1)], axis=0)
    chip = swapped(column, "wide", lambda i: i ^ 1)
    other = swapped(column, "wide", lambda i: (i + 1) % count if i % 2 else (i - 1) % count)
    return column, chip, other


def from_all(value, axis, groups=None):
    count = len(groups[0]) if groups else lax.axis_size(axis)
    copies = jnp.broadcast_to(value[None], (count, *value.shape))
    return lax.all_to_all(copies, axis, 0, 0, axis_index_groups=groups, tiled=True)


def gathered_grams(gram):
    chip = gram + swapped(gram, "wide", lambda i: i ^ 1)
    count = lax.axis_size("wide")
    groups = [list(range(core, count, 2)) for core in range(2)]
    return from_all(jnp.sum(from_all(chip, "wide", groups), axis=0), "narrow")


def local(test_matrix, weights, block_cols, export_rows, row_count):
    row_blocks, slots, size, _ = weights.shape
    columns, exports_each = test_matrix.shape[0], export_rows.shape[1]
    group = 3 * exports_each
    kernels = Kernels(columns, row_blocks, slots, size, exports_each, 3 * group)

    wide_pos = lax.axis_index("wide")
    part = wide_pos * lax.axis_size("narrow") + lax.axis_index("narrow")
    own_exports = lax.dynamic_index_in_dim(export_rows, part, 0, keepdims=False)
    offset = jnp.maximum(block_cols - row_blocks, 0)
    wide_spot = offset // group
    on_chip = (wide_spot == 2) == (wide_pos % 2 == 0)
    source = jnp.where(wide_spot == 1, 0, jnp.where(on_chip, 1, 2))
    slot_index = jnp.where(block_cols < row_blocks, block_cols, row_blocks + source * group + offset % group)

    first_exports = kernels.export_first(own_exports, row_count, test_matrix, weights)
    first_halo = halo_blocks(first_exports)
    degree, first_input = kernels.first(row_count, test_matrix, weights)
    tables = (first_input, *first_halo)
    second_exports = kernels.export_second(own_exports, row_count, slot_index, tables, degree, weights)
    second_halo = halo_blocks(second_exports)
    second_input = kernels.second(row_count, slot_index, tables, degree, weights)
    sketch, gram = kernels.sketch(row_count, slot_index, (second_input, *second_halo), degree, weights)
    grams = gathered_grams(gram)
    node_total = lax.axis_size(AXES) * row_blocks * size
    return kernels.factor(math.sqrt(node_total), grams, sketch)


def solution(mesh):
    in_specs = (
        P(None, AXES),
        P(AXES, None, None, None),
        P(AXES, None),
        P(),
        P(AXES),
    )
    return jax.shard_map(local, mesh=mesh, in_specs=in_specs, out_specs=P(None, AXES), check_vma=False)
```

time: 110 us -> 75 us (0.68); the launches traced: 109 us -> 74.6 us
  waiting for transfers between devices: 42.9 us -> 9.37 us
  blocking collectives: 0 us -> 26.4 us
  matrix products: 18.4 us -> 0 us
  other arithmetic: 17.9 us -> 0.09 us
  Pallas kernels: 0 us -> 17.8 us
  starting transfers between devices: 19.8 us -> 11.4 us
    ppermute x12 -> x5, waiting for transfers between devices: 34.9 us -> 1.14 us  [swapped(): lax.ppermute(value, axis, [(i, partner(i)) for i in range(lax.axis_size(a...]
    all_to_all x0 -> x2, blocking collectives: none -> 26.4 us  [from_all(): lax.all_to_all(copies, axis, 0, 0, axis_index_groups=groups, tiled=True)]
    pallas_call x0 -> x6, Pallas kernels: none -> 17.8 us  [the longest x1 5.21 us: sketch(): call(sketch_kernel, 2, (self.rb // self.step,), self.tables + [pl.BlockSp...]
    dot_general x3 -> x0, matrix products: 16.4 us -> none  [the longest x2 15.4 us: apply_blocks(): jnp.einsum('rskc,rsic->rki', gathered, weights, preferred_element_type=jn...]
    another operation x5 -> x0, other arithmetic: 12.1 us -> none  [the longest x3 6.52 us: local(): lower_factor = jnp.linalg.cholesky(gram)]
    ppermute x12 -> x5, starting transfers between devices: 11.9 us -> 3.4 us  [swapped(): lax.ppermute(value, axis, [(i, partner(i)) for i in range(lax.axis_size(a...]
    unnamed x12 -> x15, local copies, waits for them, and re-layouts: 0.76 us -> 8.49 us
    gather x4 -> x0, local copies, waits for them, and re-layouts: 7.22 us -> none  [the longest x2 6.1 us: apply_blocks(): gathered = jnp.take(block_table, slot_index, axis=0)]
  transfers between devices with their start and end apart: 16 -> 9, of which waited for: 16 -> 5; matrix products, arithmetic and copies ran while one was open for 0% -> 0% of each run, Pallas kernels for 0% -> 9%
where the time goes in v1:
time: 75 us; the launch traced here: 74.6 us
  blocking collectives  26.4 us (35%)
  Pallas kernels  17.8 us (24%)
  starting transfers between devices  11.4 us (15%)
  waiting for transfers between devices  9.37 us (12%)
  local copies, waits for them, and re-layouts  8.71 us (12%)
  between operations  0.83 us (1%)
    all_to_all x2, blocking collectives, from_all(): lax.all_to_all(copies, axis, 0, 0, axis_index_groups=groups, tiled=True)  26.4 us
    unnamed x15, local copies, waits for them, and re-layouts  8.49 us
    ppermute x4, waiting for transfers between devices, shifted(): lax.ppermute(value, axis, [(i, (i + step) % count) for i in range(count)])  8.23 us
    ppermute x4, starting transfers between devices, shifted(): lax.ppermute(value, axis, [(i, (i + step) % count) for i in range(count)])  8.03 us
    pallas_call x1, Pallas kernels, sketch(): call(sketch_kernel, 2, (self.rb // self.step,), self.tables + [pl.BlockSp...  5.21 us
    pallas_call x1, Pallas kernels, second(): call(second_kernel, 2, (self.rb // self.step,), self.tables + [pl.BlockSp...  4.23 us
    ppermute x5, starting transfers between devices, swapped(): lax.ppermute(value, axis, [(i, partner(i)) for i in range(lax.axis_size(a...  3.4 us
    pallas_call x1, Pallas kernels, factor(): pl.pallas_call(functools.partial(factor_kernel, scale), in_specs=[VMEM, V...  3.3 us
  transfers between devices with their start and end apart: 9, of which 5 were waited for; matrix products, arithmetic and copies ran while one was open for 0% of the time, Pallas kernels for 9%

profile of v1, /device:TPU:8, one launch (start us, length us, event | category | flops | bytes accessed | tf_op | source)
XLA Modules:
  0.0 74.6 jit_solution(9173502768350849412)
XLA Ops:
  0.7 0.2 dynamic-slice_reduce_fusion.exports
  0.9 3.4 %copy-done.1 = bf16[32,8,128,128]{3,2,1,0:T(8,128)(2,1)S(1)} copy-done((bf16[32,8,128,128]{3,2,1,0:T(8,128)(2,1)S(1)}, bf16[32,8,128,128]{3,2,1,0:T(8,128)(2,1)}, u32[]{:S(2)}) %copy-start.1) | copy-done | bytes 8388632
  4.3 1.0 %copy-done.4 = bf16[64,4096]{1,0:T(8,128)(2,1)S(1)} copy-done((bf16[64,4096]{1,0:T(8,128)(2,1)S(1)}, bf16[64,4096]{1,0:T(8,128)(2,1)}, u32[]{:S(2)}) %copy-start.4) | copy-done | bytes 524312
  5.3 1.0 %shard_map.56 = bf16[2,64,128]{2,1,0:T(8,128)(2,1)S(1)} custom-call(s32[2]{0:T(128)S(1)} %dynamic-slice_reduce_fusion.exports, s32[1]{0:T(128)S(6)} %copy.12.count, bf16[64,4096]{1,0:T(8,128)(2,1)S(1)} %copy-done.4, bf16[32,8,128,128]{3,2,1,0:T(8,128)(2,1)S(1)} %copy-done.1), custom_call_target="tpu_custom_call" | custom-call | flops 33554432 | bytes 524288 | tf_op jit(solution)/shard_map/pallas_call | solution.py:196
  6.3 5.9 %collective-permute-start.1 = (bf16[2,64,128]{2,1,0:T(8,128)(2,1)S(1)}, bf16[2,64,128]{2,1,0:T(8,128)(2,1)S(1)}, u32[]{:S(2)}, u32[]{:S(2)}) collective-permute-start(bf16[2,64,128]{2,1,0:T(8,128)(2,1)S(1)} %shard_map.56), channel_id=1, source_target_pairs={{0,7},{1,0},{2,1},{3,2},{4,3},{5,4},{6,5},{7,6},{8,15},{9,8},{10,9... | collective-permute-start | bytes 98312 | tf_op jit(solution)/shard_map/ppermute | solution.py:284
  12.3 1.5 %collective-permute-done.1 = bf16[2,64,128]{2,1,0:T(8,128)(2,1)S(1)} collective-permute-done((bf16[2,64,128]{2,1,0:T(8,128)(2,1)S(1)}, bf16[2,64,128]{2,1,0:T(8,128)(2,1)S(1)}, u32[]{:S(2)}, u32[]{:S(2)}) %collective-permute-start.1) | collective-permute-done | bytes 32800 | tf_op jit(solution)/shard_map/ppermute | solution.py:284
  13.8 3.5 %collective-permute-done = bf16[2,64,128]{2,1,0:T(8,128)(2,1)S(1)} collective-permute-done((bf16[2,64,128]{2,1,0:T(8,128)(2,1)S(1)}, bf16[2,64,128]{2,1,0:T(8,128)(2,1)S(1)}, u32[]{:S(2)}, u32[]{:S(2)}) %collective-permute-start) | collective-permute-done | bytes 32800 | tf_op jit(solution)/shard_map/ppermute | solution.py:284
  17.5 1.7 %collective-permute-start.2 = (bf16[6,64,128]{2,1,0:T(8,128)(2,1)S(1)}, bf16[6,64,128]{2,1,0:T(8,128)(2,1)S(1)}, u32[]{:S(2)}, u32[]{:S(2)}) collective-permute-start(bf16[6,64,128]{2,1,0:T(8,128)(2,1)S(1)} %pad_maximum_fusion.column), channel_id=1, source_target_pairs={{0,8},{8,0},{16,24},{24,16},{32,40},{40,32},{48,56},{56,48},{64,72... | collective-permute-start | bytes 294920 | tf_op jit(solution)/shard_map/ppermute | solution.py:288
  19.2 3.4 %copy-done.2 = bf16[32,8,128,128]{3,2,1,0:T(8,128)(2,1)S(1)} copy-done((bf16[32,8,128,128]{3,2,1,0:T(8,128)(2,1)S(1)}, bf16[32,8,128,128]{3,2,1,0:T(8,128)(2,1)}, u32[]{:S(2)}) %copy-start.2) | copy-done | bytes 8388632
  22.6 2.7 %shard_map.55 = (f32[32,128]{1,0:T(8,128)S(1)}, bf16[32,64,128]{2,1,0:T(8,128)(2,1)S(1)}) custom-call(s32[1]{0:T(128)S(6)} %copy.12.count, bf16[64,4096]{1,0:T(8,128)(2,1)S(1)} %copy-done.5, bf16[32,8,128,128]{3,2,1,0:T(8,128)(2,1)S(1)} %copy-done.2), custom_call_target="tpu_custom_call" | custom-call | flops 536870912 | bytes 8388608 | tf_op jit(solution)/shard_map/pallas_call | solution.py:209
  25.4 0.6 copy-done.3
  26.0 1.3 %shard_map.58 = bf16[2,64,128]{2,1,0:T(8,128)(2,1)S(1)} custom-call(s32[2]{0:T(128)S(1)} %dynamic-slice_reduce_fusion.exports, s32[1]{0:T(128)S(6)} %copy.12.count, s32[32,8]{1,0:T(8,128)S(1)} %compare_select_fusion.slots, bf16[32,64,128]{2,1,0:T(8,128)(2,1)S(1)} %get-tuple-element.9.own, bf16[6,64,128]{2,1,0:T(8,128)(2,1)S(1)} %pad_maximum_fusion.column, ...), custom_call_target="tpu_custom_call" | custom-call | flops 33554432 | bytes 524288 | tf_op jit(solution)/shard_map/pallas_call | solution.py:228
  27.4 2.0 %collective-permute-start.4 = (bf16[2,64,128]{2,1,0:T(8,128)(2,1)S(1)}, bf16[2,64,128]{2,1,0:T(8,128)(2,1)S(1)}, u32[]{:S(2)}, u32[]{:S(2)}) collective-permute-start(bf16[2,64,128]{2,1,0:T(8,128)(2,1)S(1)} %shard_map.58), channel_id=1, source_target_pairs={{0,1},{1,2},{2,3},{3,4},{4,5},{5,6},{6,7},{7,0},{8,9},{9,10},{10,1... | collective-permute-start | bytes 98312 | tf_op jit(solution)/shard_map/ppermute | solution.py:284
  29.4 1.9 %collective-permute-done.5 = bf16[2,64,128]{2,1,0:T(8,128)(2,1)S(1)} collective-permute-done((bf16[2,64,128]{2,1,0:T(8,128)(2,1)S(1)}, bf16[2,64,128]{2,1,0:T(8,128)(2,1)S(1)}, u32[]{:S(2)}, u32[]{:S(2)}) %collective-permute-start.5) | collective-permute-done | bytes 32800 | tf_op jit(solution)/shard_map/ppermute | solution.py:284
  31.3 1.3 %collective-permute-done.4 = bf16[2,64,128]{2,1,0:T(8,128)(2,1)S(1)} collective-permute-done((bf16[2,64,128]{2,1,0:T(8,128)(2,1)S(1)}, bf16[2,64,128]{2,1,0:T(8,128)(2,1)S(1)}, u32[]{:S(2)}, u32[]{:S(2)}) %collective-permute-start.4) | collective-permute-done | bytes 32800 | tf_op jit(solution)/shard_map/ppermute | solution.py:284
  32.6 1.0 %collective-permute-start.7 = (bf16[6,64,128]{2,1,0:T(8,128)(2,1)S(1)}, bf16[6,64,128]{2,1,0:T(8,128)(2,1)S(1)}, u32[]{:S(2)}, u32[]{:S(2)}) collective-permute-start(bf16[6,64,128]{2,1,0:T(8,128)(2,1)S(1)} %pad_maximum_fusion.1.column), channel_id=1, source_target_pairs={{0,248},{8,16},{16,8},{24,32},{32,24},{40,48},{48,40},{56,64},{64,... | collective-permute-start | bytes 294920 | tf_op jit(solution)/shard_map/ppermute | solution.py:288
  33.6 0.5 collective-permute-start.6
  34.1 4.2 %shard_map.57.own = bf16[32,64,128]{2,1,0:T(8,128)(2,1)S(1)} custom-call(s32[1]{0:T(128)S(6)} %copy.12.count, s32[32,8]{1,0:T(8,128)S(1)} %compare_select_fusion.slots, bf16[32,64,128]{2,1,0:T(8,128)(2,1)S(1)} %get-tuple-element.9.own, bf16[6,64,128]{2,1,0:T(8,128)(2,1)S(1)} %pad_maximum_fusion.column, bf16[6,64,128]{2,1,0:T(8,128)(2,1)S(1)} %collective-permute-done.2.chip, ...), custom_call_target="tpu_custom_call" | custom-call | flops 536870912 | bytes 8388608 | tf_op jit(solution)/shard_map/pallas_call | solution.py:241
  38.3 5.2 %shard_map.59 = (f32[64,4096]{1,0:T(8,128)S(1)}, f32[32,128]{1,0:T(8,128)S(1)}) custom-call(s32[1]{0:T(128)S(6)} %copy.12.count, s32[32,8]{1,0:T(8,128)S(1)} %compare_select_fusion.slots, bf16[32,64,128]{2,1,0:T(8,128)(2,1)S(1)} %shard_map.57.own, bf16[6,64,128]{2,1,0:T(8,128)(2,1)S(1)} %pad_maximum_fusion.1.column, ...), custom_call_target="tpu_custom_call" | custom-call | flops 536870912 | bytes 8388608 | tf_op jit(solution)/shard_map/pallas_call | solution.py:255
  43.6 0.1 collective-permute-start.8
  43.7 1.1 %collective-permute-done.8 = f32[32,128]{1,0:T(8,128)S(1)} collective-permute-done((f32[32,128]{1,0:T(8,128)S(1)}, f32[32,128]{1,0:T(8,128)S(1)}, u32[]{:S(2)}, u32[]{:S(2)}) %collective-permute-start.8) | collective-permute-done | bytes 16416 | tf_op jit(solution)/shard_map/ppermute | solution.py:288
  44.9 14.7 %all_to_all.10 = f32[16,32,128]{2,1,0:T(8,128)S(1)} all-to-all(f32[16,32,128]{2,1,0:T(8,128)S(1)} %broadcast_in_dim.10), channel_id=1, replica_groups={{0,16,32,48,64,80,96,112,128,144,160,176,192,208,224,240},{8,24,40,56,7..., dimensions={0} | all-to-all | bytes 524288 | tf_op jit(solution)/shard_map/all_to_all | solution.py:302
  59.6 11.8 %all_to_all.11.grams = f32[8,32,128]{2,1,0:T(8,128)S(1)} all-to-all(f32[8,32,128]{2,1,0:T(8,128)S(1)} %broadcast_in_dim.11), channel_id=1, replica_groups=mesh['wide'=32,'narrow'=8] {'narrow'}, dimensions={0} | all-to-all | bytes 262144 | tf_op jit(solution)/shard_map/all_to_all | solution.py:302
  71.3 3.3 %shard_map.60 = f32[64,4096]{1,0:T(8,128)} custom-call(f32[8,32,128]{2,1,0:T(8,128)S(1)} %all_to_all.11.grams, f32[64,4096]{1,0:T(8,128)S(1)} %get-tuple-element.12.sketch), custom_call_target="tpu_custom_call" | custom-call | flops 100663296 | bytes 2097152 | tf_op jit(solution)/shard_map/pallas_call | solution.py:271
  (25 shorter events, 0.4 us)
Async XLA Ops:
  0.0 0.7 copy-start
  0.0 12.2 %copy-start.6 = (s32[32,8]{0,1:T(8,128)S(1)}, s32[32,8]{0,1:T(8,128)}, u32[]{:S(2)}) copy-start(s32[32,8]{0,1:T(8,128)} %param.7) | copy-start | bytes 3076
  0.9 3.4 %copy-start.1 = (bf16[32,8,128,128]{3,2,1,0:T(8,128)(2,1)S(1)}, bf16[32,8,128,128]{3,2,1,0:T(8,128)(2,1)}, u32[]{:S(2)}) copy-start(bf16[32,8,128,128]{3,2,1,0:T(8,128)(2,1)} %weights.9) | copy-start | bytes 25165828
  4.3 1.0 %copy-start.4 = (bf16[64,4096]{1,0:T(8,128)(2,1)S(1)}, bf16[64,4096]{1,0:T(8,128)(2,1)}, u32[]{:S(2)}) copy-start(bf16[64,4096]{1,0:T(8,128)(2,1)} %probe.3) | copy-start | bytes 1572868
  5.3 13.9 %copy-start.5 = (bf16[64,4096]{1,0:T(8,128)(2,1)S(1)}, bf16[64,4096]{1,0:T(8,128)(2,1)}, u32[]{:S(2)}) copy-start(bf16[64,4096]{1,0:T(8,128)(2,1)} %probe.3) | copy-start | bytes 1572868
  6.3 7.5 %collective-permute-start.1 = (bf16[2,64,128]{2,1,0:T(8,128)(2,1)S(1)}, bf16[2,64,128]{2,1,0:T(8,128)(2,1)S(1)}, u32[]{:S(2)}, u32[]{:S(2)}) collective-permute-start(bf16[2,64,128]{2,1,0:T(8,128)(2,1)S(1)} %shard_map.56), channel_id=1, source_target_pairs={{0,7},{1,0},{2,1},{3,2},{4,3},{5,4},{6,5},{7,6},{8,15},{9,8},{10,9... | collective-permute-start | bytes 98312 | tf_op jit(solution)/shard_map/ppermute | solution.py:284
  12.2 5.1 %collective-permute-start = (bf16[2,64,128]{2,1,0:T(8,128)(2,1)S(1)}, bf16[2,64,128]{2,1,0:T(8,128)(2,1)S(1)}, u32[]{:S(2)}, u32[]{:S(2)}) collective-permute-start(bf16[2,64,128]{2,1,0:T(8,128)(2,1)S(1)} %shard_map.56), channel_id=1, source_target_pairs={{0,1},{1,2},{2,3},{3,4},{4,5},{5,6},{6,7},{7,0},{8,9},{9,10},{10,1... | collective-permute-start | bytes 98312 | tf_op jit(solution)/shard_map/ppermute | solution.py:284
  17.4 8.0 %collective-permute-start.3 = (bf16[6,64,128]{2,1,0:T(8,128)(2,1)S(1)}, bf16[6,64,128]{2,1,0:T(8,128)(2,1)S(1)}, u32[]{:S(2)}, u32[]{:S(2)}) collective-permute-start(bf16[6,64,128]{2,1,0:T(8,128)(2,1)S(1)} %pad_maximum_fusion.column), channel_id=1, source_target_pairs={{0,248},{8,16},{16,8},{24,32},{32,24},{40,48},{48,40},{56,64},{64,... | collective-permute-start | bytes 294920 | tf_op jit(solution)/shard_map/ppermute | solution.py:288
  17.5 7.9 %collective-permute-start.2 = (bf16[6,64,128]{2,1,0:T(8,128)(2,1)S(1)}, bf16[6,64,128]{2,1,0:T(8,128)(2,1)S(1)}, u32[]{:S(2)}, u32[]{:S(2)}) collective-permute-start(bf16[6,64,128]{2,1,0:T(8,128)(2,1)S(1)} %pad_maximum_fusion.column), channel_id=1, source_target_pairs={{0,8},{8,0},{16,24},{24,16},{32,40},{40,32},{48,56},{56,48},{64,72... | collective-permute-start | bytes 294920 | tf_op jit(solution)/shard_map/ppermute | solution.py:288
  19.2 3.4 %copy-start.2 = (bf16[32,8,128,128]{3,2,1,0:T(8,128)(2,1)S(1)}, bf16[32,8,128,128]{3,2,1,0:T(8,128)(2,1)}, u32[]{:S(2)}) copy-start(bf16[32,8,128,128]{3,2,1,0:T(8,128)(2,1)} %weights.9) | copy-start | bytes 25165828
  22.6 3.4 %copy-start.3 = (bf16[32,8,128,128]{3,2,1,0:T(8,128)(2,1)S(1)}, bf16[32,8,128,128]{3,2,1,0:T(8,128)(2,1)}, u32[]{:S(2)}) copy-start(bf16[32,8,128,128]{3,2,1,0:T(8,128)(2,1)} %weights.9) | copy-start | bytes 25165828
  27.3 4.0 %collective-permute-start.5 = (bf16[2,64,128]{2,1,0:T(8,128)(2,1)S(1)}, bf16[2,64,128]{2,1,0:T(8,128)(2,1)S(1)}, u32[]{:S(2)}, u32[]{:S(2)}) collective-permute-start(bf16[2,64,128]{2,1,0:T(8,128)(2,1)S(1)} %shard_map.58), channel_id=1, source_target_pairs={{0,7},{1,0},{2,1},{3,2},{4,3},{5,4},{6,5},{7,6},{8,15},{9,8},{10,9... | collective-permute-start | bytes 98312 | tf_op jit(solution)/shard_map/ppermute | solution.py:284
  27.4 5.2 %collective-permute-start.4 = (bf16[2,64,128]{2,1,0:T(8,128)(2,1)S(1)}, bf16[2,64,128]{2,1,0:T(8,128)(2,1)S(1)}, u32[]{:S(2)}, u32[]{:S(2)}) collective-permute-start(bf16[2,64,128]{2,1,0:T(8,128)(2,1)S(1)} %shard_map.58), channel_id=1, source_target_pairs={{0,1},{1,2},{2,3},{3,4},{4,5},{5,6},{6,7},{7,0},{8,9},{9,10},{10,1... | collective-permute-start | bytes 98312 | tf_op jit(solution)/shard_map/ppermute | solution.py:284
  32.6 5.7 %collective-permute-start.7 = (bf16[6,64,128]{2,1,0:T(8,128)(2,1)S(1)}, bf16[6,64,128]{2,1,0:T(8,128)(2,1)S(1)}, u32[]{:S(2)}, u32[]{:S(2)}) collective-permute-start(bf16[6,64,128]{2,1,0:T(8,128)(2,1)S(1)} %pad_maximum_fusion.1.column), channel_id=1, source_target_pairs={{0,248},{8,16},{16,8},{24,32},{32,24},{40,48},{48,40},{56,64},{64,... | collective-permute-start | bytes 294920 | tf_op jit(solution)/shard_map/ppermute | solution.py:288
  33.6 4.7 %collective-permute-start.6 = (bf16[6,64,128]{2,1,0:T(8,128)(2,1)S(1)}, bf16[6,64,128]{2,1,0:T(8,128)(2,1)S(1)}, u32[]{:S(2)}, u32[]{:S(2)}) collective-permute-start(bf16[6,64,128]{2,1,0:T(8,128)(2,1)S(1)} %pad_maximum_fusion.1.column), channel_id=1, source_target_pairs={{0,8},{8,0},{16,24},{24,16},{32,40},{40,32},{48,56},{56,48},{64,72... | collective-permute-start | bytes 294920 | tf_op jit(solution)/shard_map/ppermute | solution.py:288
  43.6 1.3 %collective-permute-start.8 = (f32[32,128]{1,0:T(8,128)S(1)}, f32[32,128]{1,0:T(8,128)S(1)}, u32[]{:S(2)}, u32[]{:S(2)}) collective-permute-start(f32[32,128]{1,0:T(8,128)S(1)} %get-tuple-element.11), channel_id=1, source_target_pairs={{0,8},{8,0},{16,24},{24,16},{32,40},{40,32},{48,56},{56,48},{64,72... | collective-permute-start | bytes 49160 | tf_op jit(solution)/shard_map/ppermute | solution.py:288

commit v2 on v1

v2 whole, which is shorter than its diff:
```python
import functools
import math

import jax
import jax.numpy as jnp
from jax import lax
from jax.experimental import pallas as pl
from jax.experimental.pallas import tpu as pltpu
from jax.sharding import PartitionSpec as P

EPSILON = 1e-06
AXES = ("wide", "narrow")
ROWS_STEP = 8
VMEM = pl.BlockSpec(memory_space=pltpu.VMEM)
LIMIT = 24 * 1024 * 1024
LAST = (((1,), (1,)), ((), ()))


def lanes(blocks):
    return jnp.concatenate([blocks[i] for i in range(blocks.shape[0])], axis=1)


def block_degree(blocks):
    ones = jnp.ones((8, blocks.shape[0] * blocks.shape[2]), blocks.dtype)
    sums = lax.dot_general(ones, lanes(jnp.abs(blocks)), LAST, preferred_element_type=jnp.float32)
    return sums[0:1] + EPSILON


def live_mask(row, block_size, present):
    position = lax.broadcasted_iota(jnp.int32, (1, block_size), 1) + row * block_size
    return (position < present).astype(jnp.float32)


def scaled(probe, degree, live):
    return (probe.astype(jnp.float32) * lax.rsqrt(degree) * live).astype(jnp.bfloat16)


def export_first_kernel(
    exports, count, probe, weights, out, probe_here, weights_here, probe_sems, weights_sems
):
    pieces = weights_sems.shape[1]
    slots, size = weights.shape[1] // pieces, weights.shape[2]
    rows = [exports[i] for i in range(exports.shape[0])]
    copies = []
    for i, row in enumerate(rows):
        start = pl.multiple_of(row * size, size)
        copies.append(pltpu.make_async_copy(probe.at[:, pl.ds(start, size)], probe_here.at[i], probe_sems.at[i]))
        for j in range(pieces):
            some = pl.ds(j * slots, slots)
            copies.append(
                pltpu.make_async_copy(weights.at[row, some], weights_here.at[i, some], weights_sems.at[i, j])
            )
    for copy in copies:
        copy.start()
    for copy in copies:
        copy.wait()
    for i, row in enumerate(rows):
        live = live_mask(row, size, count[0])
        out[i] = scaled(probe_here[i], block_degree(weights_here[i]), live)


def first_kernel(count, probe, weights, passed, degree_out, live_out, out, passed_out):
    rows, size = weights.shape[0], weights.shape[2]
    passed_out[...] = passed[...]

    @pl.loop(0, rows // ROWS_STEP)
    def _(step):
        for i in range(ROWS_STEP):
            row = step * ROWS_STEP + i
            degree = block_degree(weights[row])
            degree_out[pl.ds(row, 1), :] = degree
            live = live_mask(row, size, count[0])
            live_out[pl.ds(row, 1), :] = live
            out[row] = scaled(probe[:, pl.ds(pl.multiple_of(row * size, size), size)], degree, live)


def fill_table(table, owns, column, chip, other):
    start = 0
    for own in owns:
        table[start : start + own.shape[0]] = own[...]
        start += own.shape[0]
    group = column.shape[0]
    odd = lax.axis_index("wide") & 1
    table[start + group : start + 2 * group] = column[...]
    table[pl.ds(start + 2 * group * (1 - odd), group)] = chip[...]
    table[pl.ds(start + 2 * group * odd, group)] = other[...]


def applied(table, slots, row, blocks):
    vectors = jnp.concatenate([table[slots[s, row]] for s in range(blocks.shape[0])], axis=1)
    return lax.dot_general(vectors, lanes(blocks), LAST, preferred_element_type=jnp.float32)


def export_second_kernel(exports, slots, own, column, chip, other, degree, live, weights, out, table):
    fill_table(table, (own,), column, chip, other)
    for i in range(out.shape[0]):
        row = exports[i]
        product = applied(table, slots, row, weights[row])
        out[i] = (product / degree[pl.ds(row, 1), :] * live[pl.ds(row, 1), :]).astype(jnp.bfloat16)


def second_kernel(begin, slots, own, column, chip, other, degree, live, weights, passed, out, passed_out, table):
    fill_table(table, (own,), column, chip, other)
    passed_out[...] = passed[...]

    @pl.loop(0, out.shape[0] // ROWS_STEP)
    def _(step):
        for i in range(ROWS_STEP):
            place = step * ROWS_STEP + i
            row = begin + place
            product = applied(table, slots, row, weights[row])
            out[place] = (product / degree[pl.ds(row, 1), :] * live[pl.ds(row, 1), :]).astype(jnp.bfloat16)


def halves(value):
    high = value.astype(jnp.bfloat16)
    return high, (value - high.astype(jnp.float32)).astype(jnp.bfloat16)


def sketch_kernel(slots, low_own, high_own, column, chip, other, degree, live, weights, sketch, gram, table, sums):
    fill_table(table, (low_own, high_own), column, chip, other)
    row_blocks, _, size, _ = weights.shape
    columns = table.shape[1]
    sums[...] = jnp.zeros_like(sums)

    @pl.loop(0, row_blocks // ROWS_STEP)
    def _(step):
        highs, lows = [], []
        for i in range(ROWS_STEP):
            row = step * ROWS_STEP + i
            product = applied(table, slots, row, weights[row])
            value = product * lax.rsqrt(degree[pl.ds(row, 1), :]) * live[pl.ds(row, 1), :]
            sketch[:, pl.ds(pl.multiple_of(row * size, size), size)] = value
            high, low = halves(value)
            highs.append(high)
            lows.append(low)
        high = jnp.concatenate(highs, axis=1)
        both = jnp.concatenate([high, jnp.concatenate(lows, axis=1)], axis=0)
        sums[...] += lax.dot_general(both, high, LAST, preferred_element_type=jnp.float32)

    cross = sums[columns:]
    result = sums[:columns] + cross + cross.T
    gram[...] = jnp.concatenate([result[: columns // 2], result[columns // 2 :]], axis=1)


def factor_kernel(scale, grams, sketch, out, inverse):
    packed = grams[0]
    for i in range(1, grams.shape[0]):
        packed = packed + grams[i]
    half = packed.shape[0]
    count = 2 * half
    total = jnp.concatenate([packed[:, :count], packed[:, count:]], axis=0)
    identity = (
        lax.broadcasted_iota(jnp.int32, (count, count), 0) == lax.broadcasted_iota(jnp.int32, (count, count), 1)
    ).astype(jnp.float32)
    rest = jnp.concatenate([identity, total], axis=1)
    width = 8
    for start in range(0, count, width):
        height = rest.shape[0]
        sides = [
            jnp.broadcast_to(rest[:, count + start + j : count + start + j + 1], rest.shape) for j in range(width)
        ]
        below = lax.broadcasted_iota(jnp.int32, rest.shape, 0)
        for j in range(width):
            pivot = sides[j][j : j + 1, :]
            factors = jnp.where(below > j, sides[j] * (1.0 / pivot), 0.0)
            line = rest[j : j + 1, :]
            inverse[start + j : start + j + 1, :] = line * (lax.rsqrt(pivot) * scale)
            rest = rest - factors * line
            for k in range(j + 1, width):
                sides[k] = sides[k] - factors * sides[k][j : j + 1, :]
        if start + width < count:
            rest = rest[width:, :]
    high, low = halves(inverse[:, :count])
    value_high, value_low = halves(sketch[...])
    out[...] = (
        jnp.dot(high, value_high, preferred_element_type=jnp.float32)
        + jnp.dot(high, value_low, preferred_element_type=jnp.float32)
        + jnp.dot(low, value_high, preferred_element_type=jnp.float32)
    )


def cost(flops, moved):
    return pl.CostEstimate(flops=flops, bytes_accessed=moved, transcendentals=0)


SMEM = pl.BlockSpec(memory_space=pltpu.SMEM)
ANY = pl.BlockSpec(memory_space=pl.ANY)


def plain(kernel, in_specs, out_specs, out_shape, scratch, flops, moved):
    return pl.pallas_call(
        kernel,
        in_specs=in_specs,
        out_specs=out_specs,
        out_shape=out_shape,
        scratch_shapes=scratch,
        compiler_params=pltpu.CompilerParams(vmem_limit_bytes=LIMIT),
        cost_estimate=cost(flops, moved),
    )


def in_hbm(value):
    return pltpu.with_memory_space_constraint(value, pltpu.HBM)


class Kernels:
    def __init__(self, columns, row_blocks, slots, size, exports, halo):
        self.k, self.rb, self.nb, self.bs, self.eb = columns, row_blocks, slots, size, exports
        self.bytes_weights = row_blocks * slots * size * size * 2
        self.flops = 2 * columns * row_blocks * slots * size * size
        self.table = pltpu.VMEM((row_blocks + halo, columns, size), jnp.bfloat16)

    def export_first(self, exports, count, probe, weights):
        pieces = 4
        return plain(
            export_first_kernel,
            [SMEM, SMEM, ANY, ANY],
            VMEM,
            jax.ShapeDtypeStruct((self.eb, self.k, self.bs), jnp.bfloat16),
            [
                pltpu.VMEM((self.eb, self.k, self.bs), jnp.bfloat16),
                pltpu.VMEM((self.eb, self.nb, self.bs, self.bs), jnp.bfloat16),
                pltpu.SemaphoreType.DMA((self.eb,)),
                pltpu.SemaphoreType.DMA((self.eb, pieces)),
            ],
            self.flops // 16,
            self.bytes_weights // 16,
        )(exports, count, in_hbm(probe), in_hbm(weights))

    def first(self, count, probe, weights, passed):
        return plain(
            first_kernel,
            [SMEM, VMEM, VMEM, VMEM],
            [VMEM] * 4,
            [
                jax.ShapeDtypeStruct((self.rb, self.bs), jnp.float32),
                jax.ShapeDtypeStruct((self.rb, self.bs), jnp.float32),
                jax.ShapeDtypeStruct((self.rb, self.k, self.bs), jnp.bfloat16),
                jax.ShapeDtypeStruct(passed.shape, passed.dtype),
            ],
            [],
            self.flops,
            self.bytes_weights,
        )(count, probe, weights, passed)

    def export_second(self, exports, slots, tables, degree, live, weights):
        return plain(
            export_second_kernel,
            [SMEM] * 2 + [VMEM] * 7,
            VMEM,
            jax.ShapeDtypeStruct((self.eb, self.k, self.bs), jnp.bfloat16),
            [self.table],
            self.flops // 16,
            self.bytes_weights // 16,
        )(exports, slots, *tables, degree, live, weights)

    def second(self, begin, rows, slots, tables, degree, live, weights, passed):
        return plain(
            functools.partial(second_kernel, begin),
            [SMEM] + [VMEM] * 8,
            [VMEM, VMEM],
            [
                jax.ShapeDtypeStruct((rows, self.k, self.bs), jnp.bfloat16),
                jax.ShapeDtypeStruct(passed.shape, passed.dtype),
            ],
            [self.table],
            self.flops // 2,
            self.bytes_weights // 2,
        )(slots, *tables, degree, live, weights, passed)

    def sketch(self, slots, owns, halo, degree, live, weights):
        return plain(
            sketch_kernel,
            [SMEM] + [VMEM] * 8,
            [VMEM, VMEM],
            [
                jax.ShapeDtypeStruct((self.k, self.rb * self.bs), jnp.float32),
                jax.ShapeDtypeStruct((self.k // 2, 2 * self.k), jnp.float32),
            ],
            [self.table, pltpu.VMEM((2 * self.k, self.k), jnp.float32)],
            self.flops,
            self.bytes_weights,
        )(slots, *owns, *halo, degree, live, weights)

    def factor(self, scale, grams, sketch):
        return plain(
            functools.partial(factor_kernel, scale),
            [VMEM, VMEM],
            VMEM,
            jax.ShapeDtypeStruct(sketch.shape, jnp.float32),
            [pltpu.VMEM((self.k, 2 * self.k), jnp.float32)],
            6 * self.k * sketch.size,
            8 * sketch.size,
        )(grams, sketch)


def shifted(value, axis, step):
    count = lax.axis_size(axis)
    return lax.ppermute(value, axis, [(i, (i + step) % count) for i in range(count)])


def swapped(value, axis, partner):
    return lax.ppermute(value, axis, [(i, partner(i)) for i in range(lax.axis_size(axis))])


def along_narrow(exports):
    return shifted(exports, "narrow", 1), shifted(exports, "narrow", -1)


def halo_blocks(before, exports, after):
    count = lax.axis_size("wide")
    column = jnp.concatenate([before, exports, after], axis=0)
    chip = swapped(column, "wide", lambda i: i ^ 1)
    other = swapped(column, "wide", lambda i: (i + 1) % count if i % 2 else (i - 1) % count)
    return column, chip, other


def from_all(value, axis, groups=None):
    count = len(groups[0]) if groups else lax.axis_size(axis)
    copies = jnp.broadcast_to(value[None], (count, *value.shape))
    return lax.all_to_all(copies, axis, 0, 0, axis_index_groups=groups, tiled=True)


def gathered_grams(gram):
    chip = gram + swapped(gram, "wide", lambda i: i ^ 1)
    count = lax.axis_size("wide")
    groups = [list(range(core, count, 2)) for core in range(2)]
    return from_all(jnp.sum(from_all(chip, "wide", groups), axis=0), "narrow")


def local(test_matrix, weights, block_cols, export_rows, row_count):
    row_blocks, slots, size, _ = weights.shape
    columns, exports_each = test_matrix.shape[0], export_rows.shape[1]
    kernels = Kernels(columns, row_blocks, slots, size, exports_each, 9 * exports_each)
    part = lax.axis_index("wide") * lax.axis_size("narrow") + lax.axis_index("narrow")
    exports, slots_of = lax.dynamic_index_in_dim(export_rows, part, 0, keepdims=False), block_cols.T

    first_exports = kernels.export_first(exports, row_count, test_matrix, weights)
    before, after = along_narrow(first_exports)
    degree, live, first_input, passed = kernels.first(row_count, test_matrix, weights, first_exports)
    tables = (first_input, *halo_blocks(before, passed, after))
    second_exports = kernels.export_second(exports, slots_of, tables, degree, live, weights)
    before, after = along_narrow(second_exports)
    half = row_blocks // 2
    low, passed = kernels.second(0, half, slots_of, tables, degree, live, weights, second_exports)
    halo = halo_blocks(before, passed, after)
    high, _ = kernels.second(half, half, slots_of, tables, degree, live, weights, second_exports)
    sketch, gram = kernels.sketch(slots_of, (low, high), halo, degree, live, weights)
    grams = gathered_grams(gram)
    node_total = lax.axis_size(AXES) * row_blocks * size
    return kernels.factor(math.sqrt(node_total), grams, sketch)


def solution(mesh):
    in_specs = (
        P(None, AXES),
        P(AXES, None, None, None),
        P(AXES, None),
        P(),
        P(AXES),
    )
    return jax.shard_map(local, mesh=mesh, in_specs=in_specs, out_specs=P(None, AXES), check_vma=False)
```

time: 75 us -> 69.2 us (0.923)
  local copies, waits for them, and re-layouts: 8.71 us -> 0.29 us
  blocking collectives: 26.4 us -> 29.9 us
  waiting for transfers between devices: 9.37 us -> 5.95 us
  starting transfers between devices: 11.4 us -> 12.8 us
  Pallas kernels: 17.8 us -> 19.2 us
    unnamed x15 -> x12, local copies, waits for them, and re-layouts: 8.49 us -> 0.05 us
    ppermute x4, waiting for transfers between devices: 8.23 us -> 2.43 us  [shifted(): lax.ppermute(value, axis, [(i, (i + step) % count) for i in range(count)])]
    all_to_all x2, blocking collectives: 26.4 us -> 29.9 us  [from_all(): lax.all_to_all(copies, axis, 0, 0, axis_index_groups=groups, tiled=True)]
    ppermute x5, waiting for transfers between devices: 1.14 us -> 3.53 us  [swapped(): lax.ppermute(value, axis, [(i, partner(i)) for i in range(lax.axis_size(a...]
    pallas_call x6 -> x7, Pallas kernels: 17.8 us -> 19.2 us  [the longest x2 5.15 us: second(): plain(functools.partial(second_kernel, begin), [SMEM] + [VMEM] * 8, [VMEM...]
    ppermute x4, starting transfers between devices: 8.03 us -> 9.24 us  [shifted(): lax.ppermute(value, axis, [(i, (i + step) % count) for i in range(count)])]
  transfers between devices with their start and end apart: 9 -> 9, of which waited for: 5 -> 3; matrix products, arithmetic and copies ran while one was open for 0% -> 0% of each run, Pallas kernels for 9% -> 11%
where the time goes in v2:
time: 69.2 us; the launch traced here: 69 us
  blocking collectives  29.9 us (43%)
  Pallas kernels  19.2 us (28%)
  starting transfers between devices  12.8 us (18%)
  waiting for transfers between devices  5.95 us (9%)
  between operations  0.85 us (1%)
    all_to_all x2, blocking collectives, from_all(): lax.all_to_all(copies, axis, 0, 0, axis_index_groups=groups, tiled=True)  29.9 us
    ppermute x4, starting transfers between devices, shifted(): lax.ppermute(value, axis, [(i, (i + step) % count) for i in range(count)])  9.24 us
    pallas_call x2, Pallas kernels, second(): plain(functools.partial(second_kernel, begin), [SMEM] + [VMEM] * 8, [VMEM...  5.15 us
    pallas_call x1, Pallas kernels, sketch(): plain(sketch_kernel, [SMEM] + [VMEM] * 8, [VMEM, VMEM], [jax.ShapeDtypeSt...  4.81 us
    ppermute x5, starting transfers between devices, swapped(): lax.ppermute(value, axis, [(i, partner(i)) for i in range(lax.axis_size(a...  3.59 us
    ppermute x5, waiting for transfers between devices, swapped(): lax.ppermute(value, axis, [(i, partner(i)) for i in range(lax.axis_size(a...  3.53 us
    pallas_call x1, Pallas kernels, factor(): plain(functools.partial(factor_kernel, scale), [VMEM, VMEM], VMEM, jax.Sh...  3.3 us
    pallas_call x1, Pallas kernels, first(): plain(first_kernel, [SMEM, VMEM, VMEM, VMEM], [VMEM] * 4, [jax.ShapeDtype...  2.7 us
  transfers between devices with their start and end apart: 9, of which 3 were waited for; matrix products, arithmetic and copies ran while one was open for 0% of the time, Pallas kernels for 11%

profile of v2, /device:TPU:8, one launch (start us, length us, event | category | flops | bytes accessed | tf_op | source)
XLA Modules:
  0.0 69.0 jit_solution(13237456676118185439)
XLA Ops:
  0.7 0.0 copy-start.1
  0.7 0.2 dynamic-slice_reduce_fusion.exports
  0.9 2.3 %shard_map.55.passed = bf16[2,64,128]{2,1,0:T(8,128)(2,1)S(1)} custom-call(s32[2]{0:T(128)S(1)} %dynamic-slice_reduce_fusion.exports, s32[1]{0:T(128)S(6)} %copy.10.count, bf16[64,4096]{1,0:T(8,128)(2,1)} %probe.3, bf16[32,8,128,128]{3,2,1,0:T(8,128)(2,1)} %weights.11), custom_call_target="tpu_custom_call" | custom-call | flops 33554432 | bytes 524288 | tf_op jit(solution)/shard_map/pallas_call | solution.py:216
  3.2 5.9 %collective-permute-start.1 = (bf16[2,64,128]{2,1,0:T(8,128)(2,1)S(1)}, bf16[2,64,128]{2,1,0:T(8,128)(2,1)S(1)}, u32[]{:S(2)}, u32[]{:S(2)}) collective-permute-start(bf16[2,64,128]{2,1,0:T(8,128)(2,1)S(1)} %shard_map.55.passed), channel_id=1, source_target_pairs={{0,7},{1,0},{2,1},{3,2},{4,3},{5,4},{6,5},{7,6},{8,15},{9,8},{10,9... | collective-permute-start | bytes 98312 | tf_op jit(solution)/shard_map/ppermute | solution.py:300
  9.2 2.7 %shard_map.56 = (f32[32,128]{1,0:T(8,128)S(1)}, f32[32,128]{1,0:T(8,128)S(1)}, bf16[32,64,128]{2,1,0:T(8,128)(2,1)S(1)}, bf16[2,64,128]{2,1,0:T(8,128)(2,1)S(1)}) custom-call(s32[1]{0:T(128)S(6)} %copy.10.count, bf16[64,4096]{1,0:T(8,128)(2,1)S(1)} %copy-done.2, bf16[32,8,128,128]{3,2,1,0:T(8,128)(2,1)S(1)} %copy-done.1, ...), custom_call_target="tpu_custom_call" | custom-call | flops 536870912 | bytes 8388608 | tf_op jit(solution)/shard_map/pallas_call | solution.py:232
  11.8 2.4 %collective-permute-done = bf16[2,64,128]{2,1,0:T(8,128)(2,1)S(1)} collective-permute-done((bf16[2,64,128]{2,1,0:T(8,128)(2,1)S(1)}, bf16[2,64,128]{2,1,0:T(8,128)(2,1)S(1)}, u32[]{:S(2)}, u32[]{:S(2)}) %collective-permute-start) | collective-permute-done | bytes 32800 | tf_op jit(solution)/shard_map/ppermute | solution.py:300
  14.3 0.0 collective-permute-done.1
  14.3 0.1 collective-permute-start.3
  14.4 1.7 %collective-permute-start.2 = (bf16[6,64,128]{2,1,0:T(8,128)(2,1)S(1)}, bf16[6,64,128]{2,1,0:T(8,128)(2,1)S(1)}, u32[]{:S(2)}, u32[]{:S(2)}) collective-permute-start(bf16[6,64,128]{2,1,0:T(8,128)(2,1)S(1)} %constant_dynamic-update-slice_fusion.column), channel_id=1, source_target_pairs={{0,8},{8,0},{16,24},{24,16},{32,40},{40,32},{48,56},{56,48},{64,72... | collective-permute-start | bytes 294920 | tf_op jit(solution)/shard_map/ppermute | solution.py:304
  16.1 2.3 %collective-permute-done.3.other = bf16[6,64,128]{2,1,0:T(8,128)(2,1)S(1)} collective-permute-done((bf16[6,64,128]{2,1,0:T(8,128)(2,1)S(1)}, bf16[6,64,128]{2,1,0:T(8,128)(2,1)S(1)}, u32[]{:S(2)}, u32[]{:S(2)}) %collective-permute-start.3) | collective-permute-done | bytes 98336 | tf_op jit(solution)/shard_map/ppermute | solution.py:304
  18.4 0.9 %shard_map.57.passed = bf16[2,64,128]{2,1,0:T(8,128)(2,1)S(1)} custom-call(s32[2]{0:T(128)S(1)} %dynamic-slice_reduce_fusion.exports, s32[8,32]{1,0:T(8,128)S(1)} %bitcast.1, bf16[32,64,128]{2,1,0:T(8,128)(2,1)S(1)} %get-tuple-element.14.own, bf16[6,64,128]{2,1,0:T(8,128)(2,1)S(1)} %constant_dynamic-update-slice_fusion.column, ...), custom_call_target="tpu_custom_call" | custom-call | flops 33554432 | bytes 524288 | tf_op jit(solution)/shard_map/pallas_call | solution.py:248
  19.4 0.1 collective-permute-start.4
  19.5 3.2 %collective-permute-start.5 = (bf16[2,64,128]{2,1,0:T(8,128)(2,1)S(1)}, bf16[2,64,128]{2,1,0:T(8,128)(2,1)S(1)}, u32[]{:S(2)}, u32[]{:S(2)}) collective-permute-start(bf16[2,64,128]{2,1,0:T(8,128)(2,1)S(1)} %shard_map.57.passed), channel_id=1, source_target_pairs={{0,7},{1,0},{2,1},{3,2},{4,3},{5,4},{6,5},{7,6},{8,15},{9,8},{10,9... | collective-permute-start | bytes 98312 | tf_op jit(solution)/shard_map/ppermute | solution.py:300
  22.7 2.3 %shard_map.58 = (bf16[16,64,128]{2,1,0:T(8,128)(2,1)S(1)}, bf16[2,64,128]{2,1,0:T(8,128)(2,1)S(1)}) custom-call(s32[8,32]{1,0:T(8,128)S(1)} %bitcast.2, bf16[32,64,128]{2,1,0:T(8,128)(2,1)S(1)} %get-tuple-element.14.own, bf16[6,64,128]{2,1,0:T(8,128)(2,1)S(1)} %constant_dynamic-update-slice_fusion.column, ...), custom_call_target="tpu_custom_call" | custom-call | flops 268435456 | bytes 4194304 | tf_op jit(solution)/shard_map/pallas_call | solution.py:259
  25.1 0.2 collective-permute-start.7
  25.3 1.6 %collective-permute-start.6 = (bf16[6,64,128]{2,1,0:T(8,128)(2,1)S(1)}, bf16[6,64,128]{2,1,0:T(8,128)(2,1)S(1)}, u32[]{:S(2)}, u32[]{:S(2)}) collective-permute-start(bf16[6,64,128]{2,1,0:T(8,128)(2,1)S(1)} %constant_dynamic-update-slice_fusion.3.column), channel_id=1, source_target_pairs={{0,8},{8,0},{16,24},{24,16},{32,40},{40,32},{48,56},{56,48},{64,72... | collective-permute-start | bytes 294920 | tf_op jit(solution)/shard_map/ppermute | solution.py:304
  26.9 2.8 %shard_map.59 = (bf16[16,64,128]{2,1,0:T(8,128)(2,1)S(1)}, bf16[2,64,128]{2,1,0:T(8,128)(2,1)}) custom-call(s32[8,32]{1,0:T(8,128)S(1)} %bitcast.3, bf16[32,64,128]{2,1,0:T(8,128)(2,1)S(1)} %get-tuple-element.14.own, bf16[6,64,128]{2,1,0:T(8,128)(2,1)S(1)} %constant_dynamic-update-slice_fusion.column, bf16[6,64,128]{2,1,0:T(8,128)(2,1)S(1)} %collective-permute-done.2.chip, ...), custom_call_target="tpu_custom_call" | custom-call | flops 268435456 | bytes 4194304 | tf_op jit(solution)/shard_map/pallas_call | solution.py:259
  29.7 0.0 collective-permute-done.7.other
  29.7 4.8 %shard_map.60 = (f32[64,4096]{1,0:T(8,128)S(1)}, f32[32,128]{1,0:T(8,128)S(1)}) custom-call(s32[8,32]{1,0:T(8,128)S(1)} %bitcast.4, bf16[16,64,128]{2,1,0:T(8,128)(2,1)S(1)} %get-tuple-element.18.low_own, bf16[16,64,128]{2,1,0:T(8,128)(2,1)S(1)} %get-tuple-element.19.high_own, bf16[6,64,128]{2,1,0:T(8,128)(2,1)S(1)} %constant_dynamic-update-slice_fusion.3.column, ...), custom_call_target="tpu_custom_call" | custom-call | flops 536870912 | bytes 8388608 | tf_op jit(solution)/shard_map/pallas_call | solution.py:273
  34.5 0.0 collective-permute-start.8
  34.6 1.2 %collective-permute-done.8 = f32[32,128]{1,0:T(8,128)S(1)} collective-permute-done((f32[32,128]{1,0:T(8,128)S(1)}, f32[32,128]{1,0:T(8,128)S(1)}, u32[]{:S(2)}, u32[]{:S(2)}) %collective-permute-start.8) | collective-permute-done | bytes 16416 | tf_op jit(solution)/shard_map/ppermute | solution.py:304
  35.8 17.9 %all_to_all.10 = f32[16,32,128]{2,1,0:T(8,128)S(1)} all-to-all(f32[16,32,128]{2,1,0:T(8,128)S(1)} %broadcast_in_dim.4), channel_id=1, replica_groups={{0,16,32,48,64,80,96,112,128,144,160,176,192,208,224,240},{8,24,40,56,7..., dimensions={0} | all-to-all | bytes 524288 | tf_op jit(solution)/shard_map/all_to_all | solution.py:322
  53.7 12.0 %all_to_all.11.grams = f32[8,32,128]{2,1,0:T(8,128)S(1)} all-to-all(f32[8,32,128]{2,1,0:T(8,128)S(1)} %broadcast_in_dim.5), channel_id=1, replica_groups=mesh['wide'=32,'narrow'=8] {'narrow'}, dimensions={0} | all-to-all | bytes 262144 | tf_op jit(solution)/shard_map/all_to_all | solution.py:322
  65.7 3.3 %shard_map.61 = f32[64,4096]{1,0:T(8,128)} custom-call(f32[8,32,128]{2,1,0:T(8,128)S(1)} %all_to_all.11.grams, f32[64,4096]{1,0:T(8,128)S(1)} %get-tuple-element.22.sketch), custom_call_target="tpu_custom_call" | custom-call | flops 100663296 | bytes 2097152 | tf_op jit(solution)/shard_map/pallas_call | solution.py:287
  (22 shorter events, 0.1 us)
Async XLA Ops:
  0.0 0.7 %copy-start = (s32[256,2]{0,1:T(2,128)S(1)}, s32[256,2]{0,1:T(2,128)}, u32[]{:S(2)}) copy-start(s32[256,2]{0,1:T(2,128)} %param.8) | copy-start | bytes 6148
  0.0 9.1 %copy-start.2 = (bf16[64,4096]{1,0:T(8,128)(2,1)S(1)}, bf16[64,4096]{1,0:T(8,128)(2,1)}, u32[]{:S(2)}) copy-start(bf16[64,4096]{1,0:T(8,128)(2,1)} %probe.3) | copy-start | bytes 1572868
  0.7 8.4 %copy-start.1 = (bf16[32,8,128,128]{3,2,1,0:T(8,128)(2,1)S(1)}, bf16[32,8,128,128]{3,2,1,0:T(8,128)(2,1)}, u32[]{:S(2)}) copy-start(bf16[32,8,128,128]{3,2,1,0:T(8,128)(2,1)} %weights.11) | copy-start | bytes 25165828
  0.9 17.5 %copy-start.3 = (s32[32,8]{0,1:T(8,128)S(1)}, s32[32,8]{0,1:T(8,128)}, u32[]{:S(2)}) copy-start(s32[32,8]{0,1:T(8,128)} %param.7) | copy-start | bytes 3076
  3.2 11.1 %collective-permute-start.1 = (bf16[2,64,128]{2,1,0:T(8,128)(2,1)S(1)}, bf16[2,64,128]{2,1,0:T(8,128)(2,1)S(1)}, u32[]{:S(2)}, u32[]{:S(2)}) collective-permute-start(bf16[2,64,128]{2,1,0:T(8,128)(2,1)S(1)} %shard_map.55.passed), channel_id=1, source_target_pairs={{0,7},{1,0},{2,1},{3,2},{4,3},{5,4},{6,5},{7,6},{8,15},{9,8},{10,9... | collective-permute-start | bytes 98312 | tf_op jit(solution)/shard_map/ppermute | solution.py:300
  9.1 5.1 %collective-permute-start = (bf16[2,64,128]{2,1,0:T(8,128)(2,1)S(1)}, bf16[2,64,128]{2,1,0:T(8,128)(2,1)S(1)}, u32[]{:S(2)}, u32[]{:S(2)}) collective-permute-start(bf16[2,64,128]{2,1,0:T(8,128)(2,1)S(1)} %shard_map.55.passed), channel_id=1, source_target_pairs={{0,1},{1,2},{2,3},{3,4},{4,5},{5,6},{6,7},{7,0},{8,9},{9,10},{10,1... | collective-permute-start | bytes 98312 | tf_op jit(solution)/shard_map/ppermute | solution.py:300
  14.3 4.1 %collective-permute-start.3 = (bf16[6,64,128]{2,1,0:T(8,128)(2,1)S(1)}, bf16[6,64,128]{2,1,0:T(8,128)(2,1)S(1)}, u32[]{:S(2)}, u32[]{:S(2)}) collective-permute-start(bf16[6,64,128]{2,1,0:T(8,128)(2,1)S(1)} %constant_dynamic-update-slice_fusion.column), channel_id=1, source_target_pairs={{0,248},{8,16},{16,8},{24,32},{32,24},{40,48},{48,40},{56,64},{64,... | collective-permute-start | bytes 294920 | tf_op jit(solution)/shard_map/ppermute | solution.py:304
  14.4 4.0 %collective-permute-start.2 = (bf16[6,64,128]{2,1,0:T(8,128)(2,1)S(1)}, bf16[6,64,128]{2,1,0:T(8,128)(2,1)S(1)}, u32[]{:S(2)}, u32[]{:S(2)}) collective-permute-start(bf16[6,64,128]{2,1,0:T(8,128)(2,1)S(1)} %constant_dynamic-update-slice_fusion.column), channel_id=1, source_target_pairs={{0,8},{8,0},{16,24},{24,16},{32,40},{40,32},{48,56},{56,48},{64,72... | collective-permute-start | bytes 294920 | tf_op jit(solution)/shard_map/ppermute | solution.py:304
  19.4 5.7 %collective-permute-start.4 = (bf16[2,64,128]{2,1,0:T(8,128)(2,1)S(1)}, bf16[2,64,128]{2,1,0:T(8,128)(2,1)S(1)}, u32[]{:S(2)}, u32[]{:S(2)}) collective-permute-start(bf16[2,64,128]{2,1,0:T(8,128)(2,1)S(1)} %shard_map.57.passed), channel_id=1, source_target_pairs={{0,1},{1,2},{2,3},{3,4},{4,5},{5,6},{6,7},{7,0},{8,9},{9,10},{10,1... | collective-permute-start | bytes 98312 | tf_op jit(solution)/shard_map/ppermute | solution.py:300
  19.5 5.6 %collective-permute-start.5 = (bf16[2,64,128]{2,1,0:T(8,128)(2,1)S(1)}, bf16[2,64,128]{2,1,0:T(8,128)(2,1)S(1)}, u32[]{:S(2)}, u32[]{:S(2)}) collective-permute-start(bf16[2,64,128]{2,1,0:T(8,128)(2,1)S(1)} %shard_map.57.passed), channel_id=1, source_target_pairs={{0,7},{1,0},{2,1},{3,2},{4,3},{5,4},{6,5},{7,6},{8,15},{9,8},{10,9... | collective-permute-start | bytes 98312 | tf_op jit(solution)/shard_map/ppermute | solution.py:300
  25.1 4.6 %collective-permute-start.7 = (bf16[6,64,128]{2,1,0:T(8,128)(2,1)S(1)}, bf16[6,64,128]{2,1,0:T(8,128)(2,1)S(1)}, u32[]{:S(2)}, u32[]{:S(2)}) collective-permute-start(bf16[6,64,128]{2,1,0:T(8,128)(2,1)S(1)} %constant_dynamic-update-slice_fusion.3.column), channel_id=1, source_target_pairs={{0,248},{8,16},{16,8},{24,32},{32,24},{40,48},{48,40},{56,64},{64,... | collective-permute-start | bytes 294920 | tf_op jit(solution)/shard_map/ppermute | solution.py:304
  25.3 4.4 %collective-permute-start.6 = (bf16[6,64,128]{2,1,0:T(8,128)(2,1)S(1)}, bf16[6,64,128]{2,1,0:T(8,128)(2,1)S(1)}, u32[]{:S(2)}, u32[]{:S(2)}) collective-permute-start(bf16[6,64,128]{2,1,0:T(8,128)(2,1)S(1)} %constant_dynamic-update-slice_fusion.3.column), channel_id=1, source_target_pairs={{0,8},{8,0},{16,24},{24,16},{32,40},{40,32},{48,56},{56,48},{64,72... | collective-permute-start | bytes 294920 | tf_op jit(solution)/shard_map/ppermute | solution.py:304
  34.5 1.2 %collective-permute-start.8 = (f32[32,128]{1,0:T(8,128)S(1)}, f32[32,128]{1,0:T(8,128)S(1)}, u32[]{:S(2)}, u32[]{:S(2)}) collective-permute-start(f32[32,128]{1,0:T(8,128)S(1)} %get-tuple-element.21), channel_id=1, source_target_pairs={{0,8},{8,0},{16,24},{24,16},{32,40},{40,32},{48,56},{56,48},{64,72... | collective-permute-start | bytes 49160 | tf_op jit(solution)/shard_map/ppermute | solution.py:304

commit v3 on v2

--- a/solution.py
+++ b/solution.py
@@ -22,8 +22,8 @@
 
 def block_degree(blocks):
     ones = jnp.ones((8, blocks.shape[0] * blocks.shape[2]), blocks.dtype)
-    sums = lax.dot_general(ones, lanes(jnp.abs(blocks)), LAST, preferred_element_type=jnp.float32)
-    return sums[0:1] + EPSILON
+    sums = lax.dot_general(lanes(jnp.abs(blocks)), ones, LAST, preferred_element_type=jnp.float32)
+    return sums.T[0:1] + EPSILON
 
 
 def live_mask(row, block_size, present):
@@ -59,9 +59,8 @@
         out[i] = scaled(probe_here[i], block_degree(weights_here[i]), live)
 
 
-def first_kernel(count, probe, weights, passed, degree_out, live_out, out, passed_out):
+def first_kernel(count, probe, weights, degree_out, live_out, out):
     rows, size = weights.shape[0], weights.shape[2]
-    passed_out[...] = passed[...]
 
     @pl.loop(0, rows // ROWS_STEP)
     def _(step):
@@ -88,7 +87,7 @@
 
 def applied(table, slots, row, blocks):
     vectors = jnp.concatenate([table[slots[s, row]] for s in range(blocks.shape[0])], axis=1)
-    return lax.dot_general(vectors, lanes(blocks), LAST, preferred_element_type=jnp.float32)
+    return lax.dot_general(lanes(blocks), vectors, LAST, preferred_element_type=jnp.float32).T
 
 
 def export_second_kernel(exports, slots, own, column, chip, other, degree, live, weights, out, table):
@@ -99,17 +98,17 @@
         out[i] = (product / degree[pl.ds(row, 1), :] * live[pl.ds(row, 1), :]).astype(jnp.bfloat16)
 
 
-def second_kernel(begin, slots, own, column, chip, other, degree, live, weights, passed, out, passed_out, table):
+def second_kernel(begin, slots, own, column, chip, other, degree, live, weights, *rest):
+    *passed, table = rest
+    out = passed.pop(len(passed) // 2)
+    if passed:
+        passed[1][...] = passed[0][...]
     fill_table(table, (own,), column, chip, other)
-    passed_out[...] = passed[...]
-
-    @pl.loop(0, out.shape[0] // ROWS_STEP)
-    def _(step):
-        for i in range(ROWS_STEP):
-            place = step * ROWS_STEP + i
-            row = begin + place
-            product = applied(table, slots, row, weights[row])
-            out[place] = (product / degree[pl.ds(row, 1), :] * live[pl.ds(row, 1), :]).astype(jnp.bfloat16)
+
+    for place in range(out.shape[0]):
+        row = begin + place
+        product = applied(table, slots, row, weights[row])
+        out[place] = (product / degree[row : row + 1, :] * live[row : row + 1, :]).astype(jnp.bfloat16)
 
 
 def halves(value):
@@ -117,33 +116,28 @@
     return high, (value - high.astype(jnp.float32)).astype(jnp.bfloat16)
 
 
-def sketch_kernel(slots, low_own, high_own, column, chip, other, degree, live, weights, sketch, gram, table, sums):
+def sketch_kernel(slots, low_own, high_own, column, chip, other, degree, live, weights, sketch, gram, table):
     fill_table(table, (low_own, high_own), column, chip, other)
     row_blocks, _, size, _ = weights.shape
     columns = table.shape[1]
-    sums[...] = jnp.zeros_like(sums)
-
-    @pl.loop(0, row_blocks // ROWS_STEP)
-    def _(step):
-        highs, lows = [], []
-        for i in range(ROWS_STEP):
-            row = step * ROWS_STEP + i
+    sums = jnp.zeros((2 * columns, columns), jnp.float32)
+    for start in range(0, row_blocks, ROWS_STEP):
+        for row in range(start, start + ROWS_STEP):
             product = applied(table, slots, row, weights[row])
-            value = product * lax.rsqrt(degree[pl.ds(row, 1), :]) * live[pl.ds(row, 1), :]
-            sketch[:, pl.ds(pl.multiple_of(row * size, size), size)] = value
+            value = product * lax.rsqrt(degree[row : row + 1, :]) * live[row : row + 1, :]
             high, low = halves(value)
-            highs.append(high)
-            lows.append(low)
-        high = jnp.concatenate(highs, axis=1)
-        both = jnp.concatenate([high, jnp.concatenate(lows, axis=1)], axis=0)
-        sums[...] += lax.dot_general(both, high, LAST, preferred_element_type=jnp.float32)
-
+            sketch[:columns, row * size : (row + 1) * size] = high
+            sketch[columns:, row * size : (row + 1) * size] = low
+        some = slice(start * size, (start + ROWS_STEP) * size)
+        sums = sums + lax.dot_general(
+            sketch[:, some], sketch[:columns, some], LAST, preferred_element_type=jnp.float32
+        )
     cross = sums[columns:]
     result = sums[:columns] + cross + cross.T
     gram[...] = jnp.concatenate([result[: columns // 2], result[columns // 2 :]], axis=1)
 
 
-def factor_kernel(scale, grams, sketch, out, inverse):
+def factor_kernel(scale, grams, sketch, out, inverse, result, sems):
     packed = grams[0]
     for i in range(1, grams.shape[0]):
         packed = packed + grams[i]
@@ -172,12 +166,20 @@
         if start + width < count:
             rest = rest[width:, :]
     high, low = halves(inverse[:, :count])
-    value_high, value_low = halves(sketch[...])
-    out[...] = (
-        jnp.dot(high, value_high, preferred_element_type=jnp.float32)
-        + jnp.dot(high, value_low, preferred_element_type=jnp.float32)
-        + jnp.dot(low, value_high, preferred_element_type=jnp.float32)
+    factors = jnp.concatenate(
+        [jnp.concatenate([high, high], axis=1), jnp.concatenate([low, jnp.zeros_like(low)], axis=1)], axis=0
     )
+    pieces = sems.shape[0]
+    length = result.shape[1] // pieces
+    copies = []
+    for i in range(pieces):
+        some = slice(i * length, (i + 1) * length)
+        both = jnp.dot(factors, sketch[:, some], preferred_element_type=jnp.float32)
+        result[:, some] = both[:count] + both[count:]
+        copies.append(pltpu.make_async_copy(result.at[:, some], out.at[:, some], sems.at[i]))
+        copies[i].start()
+    for copy in copies:
+        copy.wait()
 
 
 def cost(flops, moved):
@@ -228,21 +230,20 @@
             self.bytes_weights // 16,
         )(exports, count, in_hbm(probe), in_hbm(weights))
 
-    def first(self, count, probe, weights, passed):
+    def first(self, count, probe, weights):
         return plain(
             first_kernel,
-            [SMEM, VMEM, VMEM, VMEM],
-            [VMEM] * 4,
+            [SMEM, VMEM, VMEM],
+            [VMEM] * 3,
             [
                 jax.ShapeDtypeStruct((self.rb, self.bs), jnp.float32),
                 jax.ShapeDtypeStruct((self.rb, self.bs), jnp.float32),
                 jax.ShapeDtypeStruct((self.rb, self.k, self.bs), jnp.bfloat16),
-                jax.ShapeDtypeStruct(passed.shape, passed.dtype),
             ],
             [],
             self.flops,
             self.bytes_weights,
-        )(count, probe, weights, passed)
+        )(count, probe, weights)
 
     def export_second(self, exports, slots, tables, degree, live, weights):
         return plain(
@@ -255,19 +256,18 @@
             self.bytes_weights // 16,
         )(exports, slots, *tables, degree, live, weights)
 
-    def second(self, begin, rows, slots, tables, degree, live, weights, passed):
+    def second(self, begin, rows, slots, tables, degree, live, weights, *passed):
+        shapes = [jax.ShapeDtypeStruct((rows, self.k, self.bs), jnp.bfloat16)]
+        shapes += [jax.ShapeDtypeStruct(value.shape, value.dtype) for value in passed]
         return plain(
             functools.partial(second_kernel, begin),
-            [SMEM] + [VMEM] * 8,
-            [VMEM, VMEM],
-            [
-                jax.ShapeDtypeStruct((rows, self.k, self.bs), jnp.bfloat16),
-                jax.ShapeDtypeStruct(passed.shape, passed.dtype),
-            ],
+            [SMEM] + [VMEM] * (7 + len(passed)),
+            [VMEM] * len(shapes),
+            shapes,
             [self.table],
             self.flops // 2,
             self.bytes_weights // 2,
-        )(slots, *tables, degree, live, weights, passed)
+        )(slots, *tables, degree, live, weights, *passed)
 
     def sketch(self, slots, owns, halo, degree, live, weights):
         return plain(
@@ -275,23 +275,28 @@
             [SMEM] + [VMEM] * 8,
             [VMEM, VMEM],
             [
-                jax.ShapeDtypeStruct((self.k, self.rb * self.bs), jnp.float32),
+                jax.ShapeDtypeStruct((2 * self.k, self.rb * self.bs), jnp.bfloat16),
                 jax.ShapeDtypeStruct((self.k // 2, 2 * self.k), jnp.float32),
             ],
-            [self.table, pltpu.VMEM((2 * self.k, self.k), jnp.float32)],
+            [self.table],
             self.flops,
             self.bytes_weights,
         )(slots, *owns, *halo, degree, live, weights)
 
     def factor(self, scale, grams, sketch):
+        shape = (self.k, sketch.shape[1])
         return plain(
             functools.partial(factor_kernel, scale),
             [VMEM, VMEM],
-            VMEM,
-            jax.ShapeDtypeStruct(sketch.shape, jnp.float32),
-            [pltpu.VMEM((self.k, 2 * self.k), jnp.float32)],
+            ANY,
+            jax.ShapeDtypeStruct(shape, jnp.float32),
+            [
+                pltpu.VMEM((self.k, 2 * self.k), jnp.float32),
+                pltpu.VMEM(shape, jnp.float32),
+                pltpu.SemaphoreType.DMA((4,)),
+            ],
             6 * self.k * sketch.size,
-            8 * sketch.size,
+            4 * sketch.size,
         )(grams, sketch)
 
 
@@ -311,8 +316,8 @@
 def halo_blocks(before, exports, after):
     count = lax.axis_size("wide")
     column = jnp.concatenate([before, exports, after], axis=0)
+    other = swapped(column, "wide", lambda i: (i + 1) % count if i % 2 else (i - 1) % count)
     chip = swapped(column, "wide", lambda i: i ^ 1)
-    other = swapped(column, "wide", lambda i: (i + 1) % count if i % 2 else (i - 1) % count)
     return column, chip, other
 
 
@@ -338,14 +343,14 @@
 
     first_exports = kernels.export_first(exports, row_count, test_matrix, weights)
     before, after = along_narrow(first_exports)
-    degree, live, first_input, passed = kernels.first(row_count, test_matrix, weights, first_exports)
-    tables = (first_input, *halo_blocks(before, passed, after))
+    degree, live, first_input = kernels.first(row_count, test_matrix, weights)
+    tables = (first_input, *halo_blocks(before, first_exports, after))
     second_exports = kernels.export_second(exports, slots_of, tables, degree, live, weights)
     before, after = along_narrow(second_exports)
     half = row_blocks // 2
     low, passed = kernels.second(0, half, slots_of, tables, degree, live, weights, second_exports)
     halo = halo_blocks(before, passed, after)
-    high, _ = kernels.second(half, half, slots_of, tables, degree, live, weights, second_exports)
+    (high,) = kernels.second(half, half, slots_of, tables, degree, live, weights)
     sketch, gram = kernels.sketch(slots_of, (low, high), halo, degree, live, weights)
     grams = gathered_grams(gram)
     node_total = lax.axis_size(AXES) * row_blocks * size

time: 69.2 us -> 68.1 us (0.984)
  Pallas kernels: 19.2 us -> 17.2 us
  waiting for transfers between devices: 5.95 us -> 6.86 us
    ppermute x4, waiting for transfers between devices: 2.43 us -> 5.13 us  [shifted(): lax.ppermute(value, axis, [(i, (i + step) % count) for i in range(count)])]
    ppermute x5, waiting for transfers between devices: 3.53 us -> 1.73 us  [swapped(): lax.ppermute(value, axis, [(i, partner(i)) for i in range(lax.axis_size(a...]
    pallas_call x4, Pallas kernels: 11.1 us -> 9.87 us  [the longest x2 3.9 us: second(): plain(functools.partial(second_kernel, begin), [SMEM] + [VMEM] * (7 + len...]
    pallas_call x1, Pallas kernels: 4.81 us -> 4 us  [sketch(): plain(sketch_kernel, [SMEM] + [VMEM] * 8, [VMEM, VMEM], [jax.ShapeDtypeSt...]
  transfers between devices with their start and end apart: 9 -> 9, of which waited for: 3 -> 4; matrix products, arithmetic and copies ran while one was open for 0% -> 0% of each run, Pallas kernels for 11% -> 10%
where the time goes in v3:
time: 68.1 us; the launch traced here: 68 us
  blocking collectives  30 us (44%)
  Pallas kernels  17.2 us (25%)
  starting transfers between devices  12.7 us (19%)
  waiting for transfers between devices  6.86 us (10%)
  between operations  0.88 us (1%)
    all_to_all x2, blocking collectives, from_all(): lax.all_to_all(copies, axis, 0, 0, axis_index_groups=groups, tiled=True)  30 us
    ppermute x4, starting transfers between devices, shifted(): lax.ppermute(value, axis, [(i, (i + step) % count) for i in range(count)])  9.24 us
    ppermute x4, waiting for transfers between devices, shifted(): lax.ppermute(value, axis, [(i, (i + step) % count) for i in range(count)])  5.13 us
    pallas_call x1, Pallas kernels, sketch(): plain(sketch_kernel, [SMEM] + [VMEM] * 8, [VMEM, VMEM], [jax.ShapeDtypeSt...  4 us
    pallas_call x2, Pallas kernels, second(): plain(functools.partial(second_kernel, begin), [SMEM] + [VMEM] * (7 + len...  3.9 us
    ppermute x5, starting transfers between devices, swapped(): lax.ppermute(value, axis, [(i, partner(i)) for i in range(lax.axis_size(a...  3.43 us
    pallas_call x1, Pallas kernels, factor(): plain(functools.partial(factor_kernel, scale), [VMEM, VMEM], ANY, jax.Sha...  3.03 us
    pallas_call x1, Pallas kernels, first(): plain(first_kernel, [SMEM, VMEM, VMEM], [VMEM] * 3, [jax.ShapeDtypeStruct...  2.94 us
  transfers between devices with their start and end apart: 9, of which 4 were waited for; matrix products, arithmetic and copies ran while one was open for 0% of the time, Pallas kernels for 10%

profile of v3, /device:TPU:8, one launch (start us, length us, event | category | flops | bytes accessed | tf_op | source)
XLA Modules:
  0.0 68.0 jit_solution(15540838078632767607)
XLA Ops:
  0.7 0.0 copy-start.1
  0.7 0.2 dynamic-slice_reduce_fusion.exports
  0.9 2.3 %shard_map.56 = bf16[2,64,128]{2,1,0:T(8,128)(2,1)S(1)} custom-call(s32[2]{0:T(128)S(1)} %dynamic-slice_reduce_fusion.exports, s32[1]{0:T(128)S(6)} %copy.8.count, bf16[64,4096]{1,0:T(8,128)(2,1)} %probe.3, bf16[32,8,128,128]{3,2,1,0:T(8,128)(2,1)} %weights.11), custom_call_target="tpu_custom_call" | custom-call | flops 33554432 | bytes 524288 | tf_op jit(solution)/shard_map/pallas_call | solution.py:218
  3.3 5.9 %collective-permute-start.1 = (bf16[2,64,128]{2,1,0:T(8,128)(2,1)S(1)}, bf16[2,64,128]{2,1,0:T(8,128)(2,1)S(1)}, u32[]{:S(2)}, u32[]{:S(2)}) collective-permute-start(bf16[2,64,128]{2,1,0:T(8,128)(2,1)S(1)} %shard_map.56), channel_id=1, source_target_pairs={{0,7},{1,0},{2,1},{3,2},{4,3},{5,4},{6,5},{7,6},{8,15},{9,8},{10,9... | collective-permute-start | bytes 98312 | tf_op jit(solution)/shard_map/ppermute | solution.py:305
  9.2 1.6 %collective-permute-done.1 = bf16[2,64,128]{2,1,0:T(8,128)(2,1)S(1)} collective-permute-done((bf16[2,64,128]{2,1,0:T(8,128)(2,1)S(1)}, bf16[2,64,128]{2,1,0:T(8,128)(2,1)S(1)}, u32[]{:S(2)}, u32[]{:S(2)}) %collective-permute-start.1) | collective-permute-done | bytes 32800 | tf_op jit(solution)/shard_map/ppermute | solution.py:305
  10.8 3.5 %collective-permute-done = bf16[2,64,128]{2,1,0:T(8,128)(2,1)S(1)} collective-permute-done((bf16[2,64,128]{2,1,0:T(8,128)(2,1)S(1)}, bf16[2,64,128]{2,1,0:T(8,128)(2,1)S(1)}, u32[]{:S(2)}, u32[]{:S(2)}) %collective-permute-start) | collective-permute-done | bytes 32800 | tf_op jit(solution)/shard_map/ppermute | solution.py:305
  14.3 0.1 collective-permute-start.3
  14.4 1.7 %collective-permute-start.2 = (bf16[6,64,128]{2,1,0:T(8,128)(2,1)S(1)}, bf16[6,64,128]{2,1,0:T(8,128)(2,1)S(1)}, u32[]{:S(2)}, u32[]{:S(2)}) collective-permute-start(bf16[6,64,128]{2,1,0:T(8,128)(2,1)S(1)} %pad_maximum_fusion.column), channel_id=1, source_target_pairs={{0,8},{8,0},{16,24},{24,16},{32,40},{40,32},{48,56},{56,48},{64,72... | collective-permute-start | bytes 294920 | tf_op jit(solution)/shard_map/ppermute | solution.py:309
  16.1 2.9 %shard_map.55 = (f32[32,128]{1,0:T(8,128)S(1)}, f32[32,128]{1,0:T(8,128)S(1)}, bf16[32,64,128]{2,1,0:T(8,128)(2,1)S(1)}) custom-call(s32[1]{0:T(128)S(6)} %copy.8.count, bf16[64,4096]{1,0:T(8,128)(2,1)S(1)} %copy-done.2, bf16[32,8,128,128]{3,2,1,0:T(8,128)(2,1)S(1)} %copy-done.1), custom_call_target="tpu_custom_call" | custom-call | flops 536870912 | bytes 8388608 | tf_op jit(solution)/shard_map/pallas_call | solution.py:234
  19.1 0.0 collective-permute-done.2.chip
  19.1 1.0 %shard_map.57.rest_0_ = bf16[2,64,128]{2,1,0:T(8,128)(2,1)S(1)} custom-call(s32[2]{0:T(128)S(1)} %dynamic-slice_reduce_fusion.exports, s32[8,32]{1,0:T(8,128)S(1)} %bitcast.1, bf16[32,64,128]{2,1,0:T(8,128)(2,1)S(1)} %get-tuple-element.12.own, bf16[6,64,128]{2,1,0:T(8,128)(2,1)S(1)} %pad_maximum_fusion.column, ...), custom_call_target="tpu_custom_call" | custom-call | flops 33554432 | bytes 524288 | tf_op jit(solution)/shard_map/pallas_call | solution.py:249
  20.1 0.1 collective-permute-start.4
  20.2 3.2 %collective-permute-start.5 = (bf16[2,64,128]{2,1,0:T(8,128)(2,1)S(1)}, bf16[2,64,128]{2,1,0:T(8,128)(2,1)S(1)}, u32[]{:S(2)}, u32[]{:S(2)}) collective-permute-start(bf16[2,64,128]{2,1,0:T(8,128)(2,1)S(1)} %shard_map.57.rest_0_), channel_id=1, source_target_pairs={{0,7},{1,0},{2,1},{3,2},{4,3},{5,4},{6,5},{7,6},{8,15},{9,8},{10,9... | collective-permute-start | bytes 98312 | tf_op jit(solution)/shard_map/ppermute | solution.py:305
  23.4 1.9 %shard_map.58 = (bf16[16,64,128]{2,1,0:T(8,128)(2,1)S(1)}, bf16[2,64,128]{2,1,0:T(8,128)(2,1)S(1)}) custom-call(s32[8,32]{1,0:T(8,128)S(1)} %bitcast.2, bf16[32,64,128]{2,1,0:T(8,128)(2,1)S(1)} %get-tuple-element.12.own, bf16[6,64,128]{2,1,0:T(8,128)(2,1)S(1)} %pad_maximum_fusion.column, bf16[6,64,128]{2,1,0:T(8,128)(2,1)S(1)} %collective-permute-done.2.chip, ...), custom_call_target="tpu_custom_call" | custom-call | flops 268435456 | bytes 4194304 | tf_op jit(solution)/shard_map/pallas_call | solution.py:262
  25.4 1.6 %collective-permute-start.7 = (bf16[6,64,128]{2,1,0:T(8,128)(2,1)S(1)}, bf16[6,64,128]{2,1,0:T(8,128)(2,1)S(1)}, u32[]{:S(2)}, u32[]{:S(2)}) collective-permute-start(bf16[6,64,128]{2,1,0:T(8,128)(2,1)S(1)} %constant_dynamic-update-slice_fusion.column), channel_id=1, source_target_pairs={{0,248},{8,16},{16,8},{24,32},{32,24},{40,48},{48,40},{56,64},{64,... | collective-permute-start | bytes 294920 | tf_op jit(solution)/shard_map/ppermute | solution.py:309
  27.1 0.0 collective-permute-start.6
  27.1 1.9 %shard_map.59.high_own = bf16[16,64,128]{2,1,0:T(8,128)(2,1)S(1)} custom-call(s32[8,32]{1,0:T(8,128)S(1)} %bitcast.3, bf16[32,64,128]{2,1,0:T(8,128)(2,1)S(1)} %get-tuple-element.12.own, bf16[6,64,128]{2,1,0:T(8,128)(2,1)S(1)} %pad_maximum_fusion.column, bf16[6,64,128]{2,1,0:T(8,128)(2,1)S(1)} %collective-permute-done.2.chip, ...), custom_call_target="tpu_custom_call" | custom-call | flops 268435456 | bytes 4194304 | tf_op jit(solution)/shard_map/pallas_call | solution.py:262
  29.0 0.6 collective-permute-done.7.other
  29.6 4.0 %shard_map.60 = (bf16[128,4096]{1,0:T(8,128)(2,1)S(1)}, f32[32,128]{1,0:T(8,128)S(1)}) custom-call(s32[8,32]{1,0:T(8,128)S(1)} %bitcast.4, bf16[16,64,128]{2,1,0:T(8,128)(2,1)S(1)} %get-tuple-element.15.low_own, bf16[16,64,128]{2,1,0:T(8,128)(2,1)S(1)} %shard_map.59.high_own, bf16[6,64,128]{2,1,0:T(8,128)(2,1)S(1)} %constant_dynamic-update-slice_fusion.column, ...), custom_call_target="tpu_custom_call" | custom-call | flops 536870912 | bytes 8388608 | tf_op jit(solution)/shard_map/pallas_call | solution.py:273
  33.6 0.0 collective-permute-start.8
  33.6 1.2 %collective-permute-done.8 = f32[32,128]{1,0:T(8,128)S(1)} collective-permute-done((f32[32,128]{1,0:T(8,128)S(1)}, f32[32,128]{1,0:T(8,128)S(1)}, u32[]{:S(2)}, u32[]{:S(2)}) %collective-permute-start.8) | collective-permute-done | bytes 16416 | tf_op jit(solution)/shard_map/ppermute | solution.py:309
  34.8 17.7 %all_to_all.10 = f32[16,32,128]{2,1,0:T(8,128)S(1)} all-to-all(f32[16,32,128]{2,1,0:T(8,128)S(1)} %broadcast_in_dim.4), channel_id=1, replica_groups={{0,16,32,48,64,80,96,112,128,144,160,176,192,208,224,240},{8,24,40,56,7..., dimensions={0} | all-to-all | bytes 524288 | tf_op jit(solution)/shard_map/all_to_all | solution.py:327
  52.6 12.3 %all_to_all.11.grams = f32[8,32,128]{2,1,0:T(8,128)S(1)} all-to-all(f32[8,32,128]{2,1,0:T(8,128)S(1)} %broadcast_in_dim.5), channel_id=1, replica_groups=mesh['wide'=32,'narrow'=8] {'narrow'}, dimensions={0} | all-to-all | bytes 262144 | tf_op jit(solution)/shard_map/all_to_all | solution.py:327
  64.9 3.0 %shard_map.61 = f32[64,4096]{1,0:T(8,128)} custom-call(f32[8,32,128]{2,1,0:T(8,128)S(1)} %all_to_all.11.grams, bf16[128,4096]{1,0:T(8,128)(2,1)S(1)} %get-tuple-element.18.sketch), custom_call_target="tpu_custom_call" | custom-call | flops 201326592 | bytes 2097152 | tf_op jit(solution)/shard_map/pallas_call | solution.py:288
  (20 shorter events, 0.1 us)
Async XLA Ops:
  0.0 0.7 %copy-start = (s32[256,2]{0,1:T(2,128)S(1)}, s32[256,2]{0,1:T(2,128)}, u32[]{:S(2)}) copy-start(s32[256,2]{0,1:T(2,128)} %param.8) | copy-start | bytes 6148
  0.0 16.1 %copy-start.2 = (bf16[64,4096]{1,0:T(8,128)(2,1)S(1)}, bf16[64,4096]{1,0:T(8,128)(2,1)}, u32[]{:S(2)}) copy-start(bf16[64,4096]{1,0:T(8,128)(2,1)} %probe.3) | copy-start | bytes 1572868
  0.7 15.4 %copy-start.1 = (bf16[32,8,128,128]{3,2,1,0:T(8,128)(2,1)S(1)}, bf16[32,8,128,128]{3,2,1,0:T(8,128)(2,1)}, u32[]{:S(2)}) copy-start(bf16[32,8,128,128]{3,2,1,0:T(8,128)(2,1)} %weights.11) | copy-start | bytes 25165828
  0.9 18.2 %copy-start.3 = (s32[32,8]{0,1:T(8,128)S(1)}, s32[32,8]{0,1:T(8,128)}, u32[]{:S(2)}) copy-start(s32[32,8]{0,1:T(8,128)} %param.7) | copy-start | bytes 3076
  3.3 7.5 %collective-permute-start.1 = (bf16[2,64,128]{2,1,0:T(8,128)(2,1)S(1)}, bf16[2,64,128]{2,1,0:T(8,128)(2,1)S(1)}, u32[]{:S(2)}, u32[]{:S(2)}) collective-permute-start(bf16[2,64,128]{2,1,0:T(8,128)(2,1)S(1)} %shard_map.56), channel_id=1, source_target_pairs={{0,7},{1,0},{2,1},{3,2},{4,3},{5,4},{6,5},{7,6},{8,15},{9,8},{10,9... | collective-permute-start | bytes 98312 | tf_op jit(solution)/shard_map/ppermute | solution.py:305
  9.2 5.1 %collective-permute-start = (bf16[2,64,128]{2,1,0:T(8,128)(2,1)S(1)}, bf16[2,64,128]{2,1,0:T(8,128)(2,1)S(1)}, u32[]{:S(2)}, u32[]{:S(2)}) collective-permute-start(bf16[2,64,128]{2,1,0:T(8,128)(2,1)S(1)} %shard_map.56), channel_id=1, source_target_pairs={{0,1},{1,2},{2,3},{3,4},{4,5},{5,6},{6,7},{7,0},{8,9},{9,10},{10,1... | collective-permute-start | bytes 98312 | tf_op jit(solution)/shard_map/ppermute | solution.py:305
  14.3 4.7 %collective-permute-start.3 = (bf16[6,64,128]{2,1,0:T(8,128)(2,1)S(1)}, bf16[6,64,128]{2,1,0:T(8,128)(2,1)S(1)}, u32[]{:S(2)}, u32[]{:S(2)}) collective-permute-start(bf16[6,64,128]{2,1,0:T(8,128)(2,1)S(1)} %pad_maximum_fusion.column), channel_id=1, source_target_pairs={{0,248},{8,16},{16,8},{24,32},{32,24},{40,48},{48,40},{56,64},{64,... | collective-permute-start | bytes 294920 | tf_op jit(solution)/shard_map/ppermute | solution.py:309
  14.4 4.6 %collective-permute-start.2 = (bf16[6,64,128]{2,1,0:T(8,128)(2,1)S(1)}, bf16[6,64,128]{2,1,0:T(8,128)(2,1)S(1)}, u32[]{:S(2)}, u32[]{:S(2)}) collective-permute-start(bf16[6,64,128]{2,1,0:T(8,128)(2,1)S(1)} %pad_maximum_fusion.column), channel_id=1, source_target_pairs={{0,8},{8,0},{16,24},{24,16},{32,40},{40,32},{48,56},{56,48},{64,72... | collective-permute-start | bytes 294920 | tf_op jit(solution)/shard_map/ppermute | solution.py:309
  20.1 5.3 %collective-permute-start.4 = (bf16[2,64,128]{2,1,0:T(8,128)(2,1)S(1)}, bf16[2,64,128]{2,1,0:T(8,128)(2,1)S(1)}, u32[]{:S(2)}, u32[]{:S(2)}) collective-permute-start(bf16[2,64,128]{2,1,0:T(8,128)(2,1)S(1)} %shard_map.57.rest_0_), channel_id=1, source_target_pairs={{0,1},{1,2},{2,3},{3,4},{4,5},{5,6},{6,7},{7,0},{8,9},{9,10},{10,1... | collective-permute-start | bytes 98312 | tf_op jit(solution)/shard_map/ppermute | solution.py:305
  20.2 5.2 %collective-permute-start.5 = (bf16[2,64,128]{2,1,0:T(8,128)(2,1)S(1)}, bf16[2,64,128]{2,1,0:T(8,128)(2,1)S(1)}, u32[]{:S(2)}, u32[]{:S(2)}) collective-permute-start(bf16[2,64,128]{2,1,0:T(8,128)(2,1)S(1)} %shard_map.57.rest_0_), channel_id=1, source_target_pairs={{0,7},{1,0},{2,1},{3,2},{4,3},{5,4},{6,5},{7,6},{8,15},{9,8},{10,9... | collective-permute-start | bytes 98312 | tf_op jit(solution)/shard_map/ppermute | solution.py:305
  25.4 4.1 %collective-permute-start.7 = (bf16[6,64,128]{2,1,0:T(8,128)(2,1)S(1)}, bf16[6,64,128]{2,1,0:T(8,128)(2,1)S(1)}, u32[]{:S(2)}, u32[]{:S(2)}) collective-permute-start(bf16[6,64,128]{2,1,0:T(8,128)(2,1)S(1)} %constant_dynamic-update-slice_fusion.column), channel_id=1, source_target_pairs={{0,248},{8,16},{16,8},{24,32},{32,24},{40,48},{48,40},{56,64},{64,... | collective-permute-start | bytes 294920 | tf_op jit(solution)/shard_map/ppermute | solution.py:309
  27.1 2.5 %collective-permute-start.6 = (bf16[6,64,128]{2,1,0:T(8,128)(2,1)S(1)}, bf16[6,64,128]{2,1,0:T(8,128)(2,1)S(1)}, u32[]{:S(2)}, u32[]{:S(2)}) collective-permute-start(bf16[6,64,128]{2,1,0:T(8,128)(2,1)S(1)} %constant_dynamic-update-slice_fusion.column), channel_id=1, source_target_pairs={{0,8},{8,0},{16,24},{24,16},{32,40},{40,32},{48,56},{56,48},{64,72... | collective-permute-start | bytes 294920 | tf_op jit(solution)/shard_map/ppermute | solution.py:309
  33.6 1.2 %collective-permute-start.8 = (f32[32,128]{1,0:T(8,128)S(1)}, f32[32,128]{1,0:T(8,128)S(1)}, u32[]{:S(2)}, u32[]{:S(2)}) collective-permute-start(f32[32,128]{1,0:T(8,128)S(1)} %get-tuple-element.17), channel_id=1, source_target_pairs={{0,8},{8,0},{16,24},{24,16},{32,40},{40,32},{48,56},{56,48},{64,72... | collective-permute-start | bytes 49160 | tf_op jit(solution)/shard_map/ppermute | solution.py:309

commit v4 on v3

--- a/solution.py
+++ b/solution.py
@@ -116,6 +116,35 @@
     return high, (value - high.astype(jnp.float32)).astype(jnp.bfloat16)
 
 
+def grid(size):
+    shape = (size, size)
+    return lax.broadcasted_iota(jnp.int32, shape, 0), lax.broadcasted_iota(jnp.int32, shape, 1)
+
+
+def packed(square):
+    half = square.shape[0] // 2
+    down, along = grid(half)
+    first, mixed, last = square[:half, :half], square[half:, :half], square[half:, half:]
+    both = jnp.concatenate([mixed, jnp.where(down >= along, first, last)], axis=1)
+    lines = jnp.concatenate([both[: half // 2], both[half // 2 :]], axis=1)
+    diagonal = jnp.sum(jnp.where(down == along, last, 0.0), axis=0, keepdims=True)
+    diagonal = jnp.concatenate([diagonal] * (lines.shape[1] // half), axis=1)
+    return [lines[i : i + 1] for i in range(half // 2)] + [diagonal]
+
+
+def unpacked(lines, diagonal):
+    half = 2 * lines.shape[0]
+    down, along = grid(half)
+    both = jnp.concatenate([lines[:, : 2 * half], lines[:, 2 * half :]], axis=0)
+    mixed, triangles = both[:, :half], both[:, half:]
+    turned = triangles.T
+    first = jnp.where(down >= along, triangles, turned)
+    last = jnp.where(down < along, triangles, jnp.where(down > along, turned, diagonal[:, :half]))
+    return jnp.concatenate(
+        [jnp.concatenate([first, mixed.T], axis=1), jnp.concatenate([mixed, last], axis=1)], axis=0
+    )
+
+
 def sketch_kernel(slots, low_own, high_own, column, chip, other, degree, live, weights, sketch, gram, table):
     fill_table(table, (low_own, high_own), column, chip, other)
     row_blocks, _, size, _ = weights.shape
@@ -134,23 +163,24 @@
         )
     cross = sums[columns:]
     result = sums[:columns] + cross + cross.T
-    gram[...] = jnp.concatenate([result[: columns // 2], result[columns // 2 :]], axis=1)
-
-
-def factor_kernel(scale, grams, sketch, out, inverse, result, sems):
-    packed = grams[0]
+    for i, line in enumerate(packed(result)):
+        gram[:, i * size : (i + 1) * size] = line
+
+
+def factor_kernel(scale, grams, sketch, out, inverse, result, lines, sems):
+    sums = grams[0]
     for i in range(1, grams.shape[0]):
-        packed = packed + grams[i]
-    half = packed.shape[0]
-    count = 2 * half
-    total = jnp.concatenate([packed[:, :count], packed[:, count:]], axis=0)
-    identity = (
-        lax.broadcasted_iota(jnp.int32, (count, count), 0) == lax.broadcasted_iota(jnp.int32, (count, count), 1)
-    ).astype(jnp.float32)
-    rest = jnp.concatenate([identity, total], axis=1)
-    width = 8
+        sums = sums + grams[i]
+    size = lines.shape[1]
+    for i in range(lines.shape[0]):
+        lines[i : i + 1, :] = sums[:, i * size : (i + 1) * size]
+    last = lines.shape[0] - 1
+    total = unpacked(lines[:last], lines[last:])
+    count = total.shape[0]
+    down, along = grid(count)
+    rest = jnp.concatenate([(down == along).astype(jnp.float32), total], axis=1)
+    width = 16
     for start in range(0, count, width):
-        height = rest.shape[0]
         sides = [
             jnp.broadcast_to(rest[:, count + start + j : count + start + j + 1], rest.shape) for j in range(width)
         ]
@@ -276,7 +306,7 @@
             [VMEM, VMEM],
             [
                 jax.ShapeDtypeStruct((2 * self.k, self.rb * self.bs), jnp.bfloat16),
-                jax.ShapeDtypeStruct((self.k // 2, 2 * self.k), jnp.float32),
+                jax.ShapeDtypeStruct((1, (self.k // 4 + 1) * self.bs), jnp.float32),
             ],
             [self.table],
             self.flops,
@@ -293,6 +323,7 @@
             [
                 pltpu.VMEM((self.k, 2 * self.k), jnp.float32),
                 pltpu.VMEM(shape, jnp.float32),
+                pltpu.VMEM((self.k // 4 + 1, self.bs), jnp.float32),
                 pltpu.SemaphoreType.DMA((4,)),
             ],
             6 * self.k * sketch.size,

time: 68.1 us -> 67 us (0.984)
  blocking collectives: 30 us -> 28.4 us
    all_to_all x2, blocking collectives: 30 us -> 28.4 us  [from_all(): lax.all_to_all(copies, axis, 0, 0, axis_index_groups=groups, tiled=True)]
where the time goes in v4:
time: 67 us; the launch traced here: 66.8 us
  blocking collectives  28.4 us (42%)
  Pallas kernels  17.4 us (26%)
  starting transfers between devices  12.7 us (19%)
  waiting for transfers between devices  6.85 us (10%)
  between operations  0.89 us (1%)
    all_to_all x2, blocking collectives, from_all(): lax.all_to_all(copies, axis, 0, 0, axis_index_groups=groups, tiled=True)  28.4 us
    ppermute x4, starting transfers between devices, shifted(): lax.ppermute(value, axis, [(i, (i + step) % count) for i in range(count)])  9.24 us
    ppermute x4, waiting for transfers between devices, shifted(): lax.ppermute(value, axis, [(i, (i + step) % count) for i in range(count)])  5.13 us
    pallas_call x1, Pallas kernels, sketch(): plain(sketch_kernel, [SMEM] + [VMEM] * 8, [VMEM, VMEM], [jax.ShapeDtypeSt...  4.14 us
    pallas_call x2, Pallas kernels, second(): plain(functools.partial(second_kernel, begin), [SMEM] + [VMEM] * (7 + len...  3.88 us
    ppermute x5, starting transfers between devices, swapped(): lax.ppermute(value, axis, [(i, partner(i)) for i in range(lax.axis_size(a...  3.49 us
    pallas_call x1, Pallas kernels, factor(): plain(functools.partial(factor_kernel, scale), [VMEM, VMEM], ANY, jax.Sha...  3.17 us
    pallas_call x1, Pallas kernels, first(): plain(first_kernel, [SMEM, VMEM, VMEM], [VMEM] * 3, [jax.ShapeDtypeStruct...  2.94 us
  transfers between devices with their start and end apart: 9, of which 4 were waited for; matrix products, arithmetic and copies ran while one was open for 0% of the time, Pallas kernels for 10%

profile of v4, /device:TPU:8, one launch (start us, length us, event | category | flops | bytes accessed | tf_op | source)
XLA Modules:
  0.0 66.8 jit_solution(15471213746118703262)
XLA Ops:
  0.7 0.0 copy-start.1
  0.7 0.2 dynamic-slice_reduce_fusion.exports
  0.9 2.3 %shard_map.56 = bf16[2,64,128]{2,1,0:T(8,128)(2,1)S(1)} custom-call(s32[2]{0:T(128)S(1)} %dynamic-slice_reduce_fusion.exports, s32[1]{0:T(128)S(6)} %copy.10.count, bf16[64,4096]{1,0:T(8,128)(2,1)} %probe.3, bf16[32,8,128,128]{3,2,1,0:T(8,128)(2,1)} %weights.11), custom_call_target="tpu_custom_call" | custom-call | flops 33554432 | bytes 524288 | tf_op jit(solution)/shard_map/pallas_call | solution.py:248
  3.3 5.9 %collective-permute-start.1 = (bf16[2,64,128]{2,1,0:T(8,128)(2,1)S(1)}, bf16[2,64,128]{2,1,0:T(8,128)(2,1)S(1)}, u32[]{:S(2)}, u32[]{:S(2)}) collective-permute-start(bf16[2,64,128]{2,1,0:T(8,128)(2,1)S(1)} %shard_map.56), channel_id=1, source_target_pairs={{0,7},{1,0},{2,1},{3,2},{4,3},{5,4},{6,5},{7,6},{8,15},{9,8},{10,9... | collective-permute-start | bytes 98312 | tf_op jit(solution)/shard_map/ppermute | solution.py:336
  9.2 1.6 %collective-permute-done.1 = bf16[2,64,128]{2,1,0:T(8,128)(2,1)S(1)} collective-permute-done((bf16[2,64,128]{2,1,0:T(8,128)(2,1)S(1)}, bf16[2,64,128]{2,1,0:T(8,128)(2,1)S(1)}, u32[]{:S(2)}, u32[]{:S(2)}) %collective-permute-start.1) | collective-permute-done | bytes 32800 | tf_op jit(solution)/shard_map/ppermute | solution.py:336
  10.8 3.5 %collective-permute-done = bf16[2,64,128]{2,1,0:T(8,128)(2,1)S(1)} collective-permute-done((bf16[2,64,128]{2,1,0:T(8,128)(2,1)S(1)}, bf16[2,64,128]{2,1,0:T(8,128)(2,1)S(1)}, u32[]{:S(2)}, u32[]{:S(2)}) %collective-permute-start) | collective-permute-done | bytes 32800 | tf_op jit(solution)/shard_map/ppermute | solution.py:336
  14.3 0.1 collective-permute-start.3
  14.4 1.7 %collective-permute-start.2 = (bf16[6,64,128]{2,1,0:T(8,128)(2,1)S(1)}, bf16[6,64,128]{2,1,0:T(8,128)(2,1)S(1)}, u32[]{:S(2)}, u32[]{:S(2)}) collective-permute-start(bf16[6,64,128]{2,1,0:T(8,128)(2,1)S(1)} %pad_maximum_fusion.column), channel_id=1, source_target_pairs={{0,8},{8,0},{16,24},{24,16},{32,40},{40,32},{48,56},{56,48},{64,72... | collective-permute-start | bytes 294920 | tf_op jit(solution)/shard_map/ppermute | solution.py:340
  16.1 2.9 %shard_map.55 = (f32[32,128]{1,0:T(8,128)S(1)}, f32[32,128]{1,0:T(8,128)S(1)}, bf16[32,64,128]{2,1,0:T(8,128)(2,1)S(1)}) custom-call(s32[1]{0:T(128)S(6)} %copy.10.count, bf16[64,4096]{1,0:T(8,128)(2,1)S(1)} %copy-done.2, bf16[32,8,128,128]{3,2,1,0:T(8,128)(2,1)S(1)} %copy-done.1), custom_call_target="tpu_custom_call" | custom-call | flops 536870912 | bytes 8388608 | tf_op jit(solution)/shard_map/pallas_call | solution.py:264
  19.1 1.0 %shard_map.57.rest_0_ = bf16[2,64,128]{2,1,0:T(8,128)(2,1)S(1)} custom-call(s32[2]{0:T(128)S(1)} %dynamic-slice_reduce_fusion.exports, s32[8,32]{1,0:T(8,128)S(1)} %bitcast.1, bf16[32,64,128]{2,1,0:T(8,128)(2,1)S(1)} %get-tuple-element.12.own, bf16[6,64,128]{2,1,0:T(8,128)(2,1)S(1)} %pad_maximum_fusion.column, ...), custom_call_target="tpu_custom_call" | custom-call | flops 33554432 | bytes 524288 | tf_op jit(solution)/shard_map/pallas_call | solution.py:279
  20.1 0.1 collective-permute-start.4
  20.2 3.2 %collective-permute-start.5 = (bf16[2,64,128]{2,1,0:T(8,128)(2,1)S(1)}, bf16[2,64,128]{2,1,0:T(8,128)(2,1)S(1)}, u32[]{:S(2)}, u32[]{:S(2)}) collective-permute-start(bf16[2,64,128]{2,1,0:T(8,128)(2,1)S(1)} %shard_map.57.rest_0_), channel_id=1, source_target_pairs={{0,7},{1,0},{2,1},{3,2},{4,3},{5,4},{6,5},{7,6},{8,15},{9,8},{10,9... | collective-permute-start | bytes 98312 | tf_op jit(solution)/shard_map/ppermute | solution.py:336
  23.4 1.9 %shard_map.58 = (bf16[16,64,128]{2,1,0:T(8,128)(2,1)S(1)}, bf16[2,64,128]{2,1,0:T(8,128)(2,1)S(1)}) custom-call(s32[8,32]{1,0:T(8,128)S(1)} %bitcast.2, bf16[32,64,128]{2,1,0:T(8,128)(2,1)S(1)} %get-tuple-element.12.own, bf16[6,64,128]{2,1,0:T(8,128)(2,1)S(1)} %pad_maximum_fusion.column, bf16[6,64,128]{2,1,0:T(8,128)(2,1)S(1)} %collective-permute-done.2.chip, ...), custom_call_target="tpu_custom_call" | custom-call | flops 268435456 | bytes 4194304 | tf_op jit(solution)/shard_map/pallas_call | solution.py:292
  25.4 1.6 %collective-permute-start.7 = (bf16[6,64,128]{2,1,0:T(8,128)(2,1)S(1)}, bf16[6,64,128]{2,1,0:T(8,128)(2,1)S(1)}, u32[]{:S(2)}, u32[]{:S(2)}) collective-permute-start(bf16[6,64,128]{2,1,0:T(8,128)(2,1)S(1)} %constant_dynamic-update-slice_fusion.column), channel_id=1, source_target_pairs={{0,248},{8,16},{16,8},{24,32},{32,24},{40,48},{48,40},{56,64},{64,... | collective-permute-start | bytes 294920 | tf_op jit(solution)/shard_map/ppermute | solution.py:340
  27.1 1.9 %shard_map.59.high_own = bf16[16,64,128]{2,1,0:T(8,128)(2,1)S(1)} custom-call(s32[8,32]{1,0:T(8,128)S(1)} %bitcast.3, bf16[32,64,128]{2,1,0:T(8,128)(2,1)S(1)} %get-tuple-element.12.own, bf16[6,64,128]{2,1,0:T(8,128)(2,1)S(1)} %pad_maximum_fusion.column, bf16[6,64,128]{2,1,0:T(8,128)(2,1)S(1)} %collective-permute-done.2.chip, ...), custom_call_target="tpu_custom_call" | custom-call | flops 268435456 | bytes 4194304 | tf_op jit(solution)/shard_map/pallas_call | solution.py:292
  29.0 0.6 collective-permute-done.7.other
  29.6 4.1 %shard_map.60 = (bf16[128,4096]{1,0:T(8,128)(2,1)S(1)}, f32[1,2176]{1,0:T(1,128)S(1)}) custom-call(s32[8,32]{1,0:T(8,128)S(1)} %bitcast.4, bf16[16,64,128]{2,1,0:T(8,128)(2,1)S(1)} %get-tuple-element.15.low_own, bf16[16,64,128]{2,1,0:T(8,128)(2,1)S(1)} %shard_map.59.high_own, bf16[6,64,128]{2,1,0:T(8,128)(2,1)S(1)} %constant_dynamic-update-slice_fusion.column, ...), custom_call_target="tpu_custom_call" | custom-call | flops 536870912 | bytes 8388608 | tf_op jit(solution)/shard_map/pallas_call | solution.py:303
  33.7 0.1 collective-permute-start.8
  33.8 1.2 %collective-permute-done.8 = f32[1,2176]{1,0:T(1,128)S(1)} collective-permute-done((f32[1,2176]{1,0:T(1,128)S(1)}, f32[1,2176]{1,0:T(1,128)S(1)}, u32[]{:S(2)}, u32[]{:S(2)}) %collective-permute-start.8) | collective-permute-done | bytes 8736 | tf_op jit(solution)/shard_map/ppermute | solution.py:340
  35.0 0.1 broadcast_in_dim.7
  35.1 16.8 %all_to_all.10 = f32[16,1,2176]{2,1,0:T(1,128)S(1)} all-to-all(f32[16,1,2176]{2,1,0:T(1,128)S(1)} %broadcast_in_dim.7), channel_id=1, replica_groups={{0,16,32,48,64,80,96,112,128,144,160,176,192,208,224,240},{8,24,40,56,7..., dimensions={0} | all-to-all | bytes 278528 | tf_op jit(solution)/shard_map/all_to_all | solution.py:358
  51.9 0.1 reduce_sum.9
  52.0 11.7 %all_to_all.11.grams = f32[8,1,2176]{2,1,0:T(1,128)S(1)} all-to-all(f32[8,1,2176]{2,1,0:T(1,128)S(1)} %broadcast_in_dim.16), channel_id=1, replica_groups=mesh['wide'=32,'narrow'=8] {'narrow'}, dimensions={0} | all-to-all | bytes 139264 | tf_op jit(solution)/shard_map/all_to_all | solution.py:358
  63.7 3.2 %shard_map.61 = f32[64,4096]{1,0:T(8,128)} custom-call(f32[8,1,2176]{2,1,0:T(1,128)S(1)} %all_to_all.11.grams, bf16[128,4096]{1,0:T(8,128)(2,1)S(1)} %get-tuple-element.18.sketch), custom_call_target="tpu_custom_call" | custom-call | flops 201326592 | bytes 2097152 | tf_op jit(solution)/shard_map/pallas_call | solution.py:318
  (20 shorter events, 0.1 us)
Async XLA Ops:
  0.0 0.7 %copy-start = (s32[256,2]{0,1:T(2,128)S(1)}, s32[256,2]{0,1:T(2,128)}, u32[]{:S(2)}) copy-start(s32[256,2]{0,1:T(2,128)} %param.8) | copy-start | bytes 6148
  0.0 16.1 %copy-start.2 = (bf16[64,4096]{1,0:T(8,128)(2,1)S(1)}, bf16[64,4096]{1,0:T(8,128)(2,1)}, u32[]{:S(2)}) copy-start(bf16[64,4096]{1,0:T(8,128)(2,1)} %probe.3) | copy-start | bytes 1572868
  0.7 15.4 %copy-start.1 = (bf16[32,8,128,128]{3,2,1,0:T(8,128)(2,1)S(1)}, bf16[32,8,128,128]{3,2,1,0:T(8,128)(2,1)}, u32[]{:S(2)}) copy-start(bf16[32,8,128,128]{3,2,1,0:T(8,128)(2,1)} %weights.11) | copy-start | bytes 25165828
  0.9 18.2 %copy-start.3 = (s32[32,8]{0,1:T(8,128)S(1)}, s32[32,8]{0,1:T(8,128)}, u32[]{:S(2)}) copy-start(s32[32,8]{0,1:T(8,128)} %param.7) | copy-start | bytes 3076
  3.3 7.5 %collective-permute-start.1 = (bf16[2,64,128]{2,1,0:T(8,128)(2,1)S(1)}, bf16[2,64,128]{2,1,0:T(8,128)(2,1)S(1)}, u32[]{:S(2)}, u32[]{:S(2)}) collective-permute-start(bf16[2,64,128]{2,1,0:T(8,128)(2,1)S(1)} %shard_map.56), channel_id=1, source_target_pairs={{0,7},{1,0},{2,1},{3,2},{4,3},{5,4},{6,5},{7,6},{8,15},{9,8},{10,9... | collective-permute-start | bytes 98312 | tf_op jit(solution)/shard_map/ppermute | solution.py:336
  9.2 5.1 %collective-permute-start = (bf16[2,64,128]{2,1,0:T(8,128)(2,1)S(1)}, bf16[2,64,128]{2,1,0:T(8,128)(2,1)S(1)}, u32[]{:S(2)}, u32[]{:S(2)}) collective-permute-start(bf16[2,64,128]{2,1,0:T(8,128)(2,1)S(1)} %shard_map.56), channel_id=1, source_target_pairs={{0,1},{1,2},{2,3},{3,4},{4,5},{5,6},{6,7},{7,0},{8,9},{9,10},{10,1... | collective-permute-start | bytes 98312 | tf_op jit(solution)/shard_map/ppermute | solution.py:336
  14.3 4.7 %collective-permute-start.3 = (bf16[6,64,128]{2,1,0:T(8,128)(2,1)S(1)}, bf16[6,64,128]{2,1,0:T(8,128)(2,1)S(1)}, u32[]{:S(2)}, u32[]{:S(2)}) collective-permute-start(bf16[6,64,128]{2,1,0:T(8,128)(2,1)S(1)} %pad_maximum_fusion.column), channel_id=1, source_target_pairs={{0,248},{8,16},{16,8},{24,32},{32,24},{40,48},{48,40},{56,64},{64,... | collective-permute-start | bytes 294920 | tf_op jit(solution)/shard_map/ppermute | solution.py:340
  14.4 4.6 %collective-permute-start.2 = (bf16[6,64,128]{2,1,0:T(8,128)(2,1)S(1)}, bf16[6,64,128]{2,1,0:T(8,128)(2,1)S(1)}, u32[]{:S(2)}, u32[]{:S(2)}) collective-permute-start(bf16[6,64,128]{2,1,0:T(8,128)(2,1)S(1)} %pad_maximum_fusion.column), channel_id=1, source_target_pairs={{0,8},{8,0},{16,24},{24,16},{32,40},{40,32},{48,56},{56,48},{64,72... | collective-permute-start | bytes 294920 | tf_op jit(solution)/shard_map/ppermute | solution.py:340
  20.1 5.3 %collective-permute-start.4 = (bf16[2,64,128]{2,1,0:T(8,128)(2,1)S(1)}, bf16[2,64,128]{2,1,0:T(8,128)(2,1)S(1)}, u32[]{:S(2)}, u32[]{:S(2)}) collective-permute-start(bf16[2,64,128]{2,1,0:T(8,128)(2,1)S(1)} %shard_map.57.rest_0_), channel_id=1, source_target_pairs={{0,1},{1,2},{2,3},{3,4},{4,5},{5,6},{6,7},{7,0},{8,9},{9,10},{10,1... | collective-permute-start | bytes 98312 | tf_op jit(solution)/shard_map/ppermute | solution.py:336
  20.2 5.2 %collective-permute-start.5 = (bf16[2,64,128]{2,1,0:T(8,128)(2,1)S(1)}, bf16[2,64,128]{2,1,0:T(8,128)(2,1)S(1)}, u32[]{:S(2)}, u32[]{:S(2)}) collective-permute-start(bf16[2,64,128]{2,1,0:T(8,128)(2,1)S(1)} %shard_map.57.rest_0_), channel_id=1, source_target_pairs={{0,7},{1,0},{2,1},{3,2},{4,3},{5,4},{6,5},{7,6},{8,15},{9,8},{10,9... | collective-permute-start | bytes 98312 | tf_op jit(solution)/shard_map/ppermute | solution.py:336
  25.4 4.1 %collective-permute-start.7 = (bf16[6,64,128]{2,1,0:T(8,128)(2,1)S(1)}, bf16[6,64,128]{2,1,0:T(8,128)(2,1)S(1)}, u32[]{:S(2)}, u32[]{:S(2)}) collective-permute-start(bf16[6,64,128]{2,1,0:T(8,128)(2,1)S(1)} %constant_dynamic-update-slice_fusion.column), channel_id=1, source_target_pairs={{0,248},{8,16},{16,8},{24,32},{32,24},{40,48},{48,40},{56,64},{64,... | collective-permute-start | bytes 294920 | tf_op jit(solution)/shard_map/ppermute | solution.py:340
  27.1 2.5 %collective-permute-start.6 = (bf16[6,64,128]{2,1,0:T(8,128)(2,1)S(1)}, bf16[6,64,128]{2,1,0:T(8,128)(2,1)S(1)}, u32[]{:S(2)}, u32[]{:S(2)}) collective-permute-start(bf16[6,64,128]{2,1,0:T(8,128)(2,1)S(1)} %constant_dynamic-update-slice_fusion.column), channel_id=1, source_target_pairs={{0,8},{8,0},{16,24},{24,16},{32,40},{40,32},{48,56},{56,48},{64,72... | collective-permute-start | bytes 294920 | tf_op jit(solution)/shard_map/ppermute | solution.py:340
  33.7 1.3 %collective-permute-start.8 = (f32[1,2176]{1,0:T(1,128)S(1)}, f32[1,2176]{1,0:T(1,128)S(1)}, u32[]{:S(2)}, u32[]{:S(2)}) collective-permute-start(f32[1,2176]{1,0:T(1,128)S(1)} %get-tuple-element.17), channel_id=1, source_target_pairs={{0,8},{8,0},{16,24},{24,16},{32,40},{40,32},{48,56},{56,48},{64,72... | collective-permute-start | bytes 26120 | tf_op jit(solution)/shard_map/ppermute | solution.py:340

commit v5 on v4

--- a/solution.py
+++ b/solution.py
@@ -73,11 +73,9 @@
             out[row] = scaled(probe[:, pl.ds(pl.multiple_of(row * size, size), size)], degree, live)
 
 
-def fill_table(table, owns, column, chip, other):
-    start = 0
-    for own in owns:
-        table[start : start + own.shape[0]] = own[...]
-        start += own.shape[0]
+def fill_table(table, own, column, chip, other):
+    start = own.shape[0]
+    table[:start] = own[...]
     group = column.shape[0]
     odd = lax.axis_index("wide") & 1
     table[start + group : start + 2 * group] = column[...]
@@ -91,24 +89,18 @@
 
 
 def export_second_kernel(exports, slots, own, column, chip, other, degree, live, weights, out, table):
-    fill_table(table, (own,), column, chip, other)
+    fill_table(table, own, column, chip, other)
     for i in range(out.shape[0]):
         row = exports[i]
         product = applied(table, slots, row, weights[row])
         out[i] = (product / degree[pl.ds(row, 1), :] * live[pl.ds(row, 1), :]).astype(jnp.bfloat16)
 
 
-def second_kernel(begin, slots, own, column, chip, other, degree, live, weights, *rest):
-    *passed, table = rest
-    out = passed.pop(len(passed) // 2)
-    if passed:
-        passed[1][...] = passed[0][...]
-    fill_table(table, (own,), column, chip, other)
-
-    for place in range(out.shape[0]):
-        row = begin + place
+def second_kernel(slots, own, column, chip, other, degree, live, weights, out, table):
+    fill_table(table, own, column, chip, other)
+    for row in range(out.shape[0]):
         product = applied(table, slots, row, weights[row])
-        out[place] = (product / degree[row : row + 1, :] * live[row : row + 1, :]).astype(jnp.bfloat16)
+        out[row] = (product / degree[row : row + 1, :] * live[row : row + 1, :]).astype(jnp.bfloat16)
 
 
 def halves(value):
@@ -145,8 +137,8 @@
     )
 
 
-def sketch_kernel(slots, low_own, high_own, column, chip, other, degree, live, weights, sketch, gram, table):
-    fill_table(table, (low_own, high_own), column, chip, other)
+def sketch_kernel(slots, own, column, chip, other, degree, live, weights, sketch, gram, table):
+    fill_table(table, own, column, chip, other)
     row_blocks, _, size, _ = weights.shape
     columns = table.shape[1]
     sums = jnp.zeros((2 * columns, columns), jnp.float32)
@@ -286,23 +278,21 @@
             self.bytes_weights // 16,
         )(exports, slots, *tables, degree, live, weights)
 
-    def second(self, begin, rows, slots, tables, degree, live, weights, *passed):
-        shapes = [jax.ShapeDtypeStruct((rows, self.k, self.bs), jnp.bfloat16)]
-        shapes += [jax.ShapeDtypeStruct(value.shape, value.dtype) for value in passed]
-        return plain(
-            functools.partial(second_kernel, begin),
-            [SMEM] + [VMEM] * (7 + len(passed)),
-            [VMEM] * len(shapes),
-            shapes,
+    def second(self, slots, tables, degree, live, weights):
+        return plain(
+            second_kernel,
+            [SMEM] + [VMEM] * 7,
+            VMEM,
+            jax.ShapeDtypeStruct((self.rb, self.k, self.bs), jnp.bfloat16),
             [self.table],
-            self.flops // 2,
-            self.bytes_weights // 2,
-        )(slots, *tables, degree, live, weights, *passed)
-
-    def sketch(self, slots, owns, halo, degree, live, weights):
+            self.flops,
+            self.bytes_weights,
+        )(slots, *tables, degree, live, weights)
+
+    def sketch(self, slots, own, halo, degree, live, weights):
         return plain(
             sketch_kernel,
-            [SMEM] + [VMEM] * 8,
+            [SMEM] + [VMEM] * 7,
             [VMEM, VMEM],
             [
                 jax.ShapeDtypeStruct((2 * self.k, self.rb * self.bs), jnp.bfloat16),
@@ -311,7 +301,7 @@
             [self.table],
             self.flops,
             self.bytes_weights,
-        )(slots, *owns, *halo, degree, live, weights)
+        )(slots, own, *halo, degree, live, weights)
 
     def factor(self, scale, grams, sketch):
         shape = (self.k, sketch.shape[1])
@@ -324,7 +314,7 @@
                 pltpu.VMEM((self.k, 2 * self.k), jnp.float32),
                 pltpu.VMEM(shape, jnp.float32),
                 pltpu.VMEM((self.k // 4 + 1, self.bs), jnp.float32),
-                pltpu.SemaphoreType.DMA((4,)),
+                pltpu.SemaphoreType.DMA((8,)),
             ],
             6 * self.k * sketch.size,
             4 * sketch.size,
@@ -378,11 +368,9 @@
     tables = (first_input, *halo_blocks(before, first_exports, after))
     second_exports = kernels.export_second(exports, slots_of, tables, degree, live, weights)
     before, after = along_narrow(second_exports)
-    half = row_blocks // 2
-    low, passed = kernels.second(0, half, slots_of, tables, degree, live, weights, second_exports)
-    halo = halo_blocks(before, passed, after)
-    (high,) = kernels.second(half, half, slots_of, tables, degree, live, weights)
-    sketch, gram = kernels.sketch(slots_of, (low, high), halo, degree, live, weights)
+    halo = halo_blocks(before, second_exports, after)
+    second_input = kernels.second(slots_of, tables, degree, live, weights)
+    sketch, gram = kernels.sketch(slots_of, second_input, halo, degree, live, weights)
     grams = gathered_grams(gram)
     node_total = lax.axis_size(AXES) * row_blocks * size
     return kernels.factor(math.sqrt(node_total), grams, sketch)

time: 67 us -> 65.9 us (0.984)
  waiting for transfers between devices: 6.85 us -> 9.44 us
  blocking collectives: 28.4 us -> 27 us
  starting transfers between devices: 12.7 us -> 11.4 us
  Pallas kernels: 17.4 us -> 16.6 us
    ppermute x4, waiting for transfers between devices: 5.13 us -> 8.31 us  [shifted(): lax.ppermute(value, axis, [(i, (i + step) % count) for i in range(count)])]
    all_to_all x2, blocking collectives: 28.4 us -> 27 us  [from_all(): lax.all_to_all(copies, axis, 0, 0, axis_index_groups=groups, tiled=True)]
    ppermute x4, starting transfers between devices: 9.24 us -> 8.03 us  [shifted(): lax.ppermute(value, axis, [(i, (i + step) % count) for i in range(count)])]
    pallas_call x3 -> x2, Pallas kernels: 8.02 us -> 7.18 us  [the longest x1 4.14 us: sketch(): plain(sketch_kernel, [SMEM] + [VMEM] * 7, [VMEM, VMEM], [jax.ShapeDtypeSt...]
  transfers between devices with their start and end apart: 9 -> 9, of which waited for: 4 -> 5; matrix products, arithmetic and copies ran while one was open for 0% -> 0% of each run, Pallas kernels for 10% -> 9%
where the time goes in v5:
time: 65.9 us; the launch traced here: 65.8 us
  blocking collectives  27 us (41%)
  Pallas kernels  16.6 us (25%)
  starting transfers between devices  11.4 us (17%)
  waiting for transfers between devices  9.44 us (14%)
  between operations  0.87 us (1%)
    all_to_all x2, blocking collectives, from_all(): lax.all_to_all(copies, axis, 0, 0, axis_index_groups=groups, tiled=True)  27 us
    ppermute x4, waiting for transfers between devices, shifted(): lax.ppermute(value, axis, [(i, (i + step) % count) for i in range(count)])  8.31 us
    ppermute x4, starting transfers between devices, shifted(): lax.ppermute(value, axis, [(i, (i + step) % count) for i in range(count)])  8.03 us
    pallas_call x1, Pallas kernels, sketch(): plain(sketch_kernel, [SMEM] + [VMEM] * 7, [VMEM, VMEM], [jax.ShapeDtypeSt...  4.14 us
    ppermute x5, starting transfers between devices, swapped(): lax.ppermute(value, axis, [(i, partner(i)) for i in range(lax.axis_size(a...  3.4 us
    pallas_call x1, Pallas kernels, factor(): plain(functools.partial(factor_kernel, scale), [VMEM, VMEM], ANY, jax.Sha...  3.15 us
    pallas_call x1, Pallas kernels, second(): plain(second_kernel, [SMEM] + [VMEM] * 7, VMEM, jax.ShapeDtypeStruct((sel...  3.04 us
    pallas_call x1, Pallas kernels, first(): plain(first_kernel, [SMEM, VMEM, VMEM], [VMEM] * 3, [jax.ShapeDtypeStruct...  2.94 us
  transfers between devices with their start and end apart: 9, of which 5 were waited for; matrix products, arithmetic and copies ran while one was open for 0% of the time, Pallas kernels for 9%

profile of v5, /device:TPU:8, one launch (start us, length us, event | category | flops | bytes accessed | tf_op | source)
XLA Modules:
  0.0 65.8 jit_solution(10610171455279364985)
XLA Ops:
  0.7 0.2 dynamic-slice_reduce_fusion.exports
  0.9 2.3 %shard_map.56 = bf16[2,64,128]{2,1,0:T(8,128)(2,1)S(1)} custom-call(s32[2]{0:T(128)S(1)} %dynamic-slice_reduce_fusion.exports, s32[1]{0:T(128)S(6)} %copy.8.count, bf16[64,4096]{1,0:T(8,128)(2,1)} %probe.3, bf16[32,8,128,128]{3,2,1,0:T(8,128)(2,1)} %weights.9), custom_call_target="tpu_custom_call" | custom-call | flops 33554432 | bytes 524288 | tf_op jit(solution)/shard_map/pallas_call | solution.py:240
  3.3 5.9 %collective-permute-start.1 = (bf16[2,64,128]{2,1,0:T(8,128)(2,1)S(1)}, bf16[2,64,128]{2,1,0:T(8,128)(2,1)S(1)}, u32[]{:S(2)}, u32[]{:S(2)}) collective-permute-start(bf16[2,64,128]{2,1,0:T(8,128)(2,1)S(1)} %shard_map.56), channel_id=1, source_target_pairs={{0,7},{1,0},{2,1},{3,2},{4,3},{5,4},{6,5},{7,6},{8,15},{9,8},{10,9... | collective-permute-start | bytes 98312 | tf_op jit(solution)/shard_map/ppermute | solution.py:326
  9.2 1.6 %collective-permute-done.1 = bf16[2,64,128]{2,1,0:T(8,128)(2,1)S(1)} collective-permute-done((bf16[2,64,128]{2,1,0:T(8,128)(2,1)S(1)}, bf16[2,64,128]{2,1,0:T(8,128)(2,1)S(1)}, u32[]{:S(2)}, u32[]{:S(2)}) %collective-permute-start.1) | collective-permute-done | bytes 32800 | tf_op jit(solution)/shard_map/ppermute | solution.py:326
  10.8 3.5 %collective-permute-done = bf16[2,64,128]{2,1,0:T(8,128)(2,1)S(1)} collective-permute-done((bf16[2,64,128]{2,1,0:T(8,128)(2,1)S(1)}, bf16[2,64,128]{2,1,0:T(8,128)(2,1)S(1)}, u32[]{:S(2)}, u32[]{:S(2)}) %collective-permute-start) | collective-permute-done | bytes 32800 | tf_op jit(solution)/shard_map/ppermute | solution.py:326
  14.3 0.1 collective-permute-start.3
  14.4 1.7 %collective-permute-start.2 = (bf16[6,64,128]{2,1,0:T(8,128)(2,1)S(1)}, bf16[6,64,128]{2,1,0:T(8,128)(2,1)S(1)}, u32[]{:S(2)}, u32[]{:S(2)}) collective-permute-start(bf16[6,64,128]{2,1,0:T(8,128)(2,1)S(1)} %pad_maximum_fusion.column), channel_id=1, source_target_pairs={{0,8},{8,0},{16,24},{24,16},{32,40},{40,32},{48,56},{56,48},{64,72... | collective-permute-start | bytes 294920 | tf_op jit(solution)/shard_map/ppermute | solution.py:330
  16.1 2.9 %shard_map.55 = (f32[32,128]{1,0:T(8,128)S(1)}, f32[32,128]{1,0:T(8,128)S(1)}, bf16[32,64,128]{2,1,0:T(8,128)(2,1)S(1)}) custom-call(s32[1]{0:T(128)S(6)} %copy.8.count, bf16[64,4096]{1,0:T(8,128)(2,1)S(1)} %copy-done.2, bf16[32,8,128,128]{3,2,1,0:T(8,128)(2,1)S(1)} %copy-done.1), custom_call_target="tpu_custom_call" | custom-call | flops 536870912 | bytes 8388608 | tf_op jit(solution)/shard_map/pallas_call | solution.py:256
  19.1 1.0 %shard_map.58 = bf16[2,64,128]{2,1,0:T(8,128)(2,1)S(1)} custom-call(s32[2]{0:T(128)S(1)} %dynamic-slice_reduce_fusion.exports, s32[8,32]{1,0:T(8,128)S(1)} %bitcast.1, bf16[32,64,128]{2,1,0:T(8,128)(2,1)S(1)} %get-tuple-element.10.own, bf16[6,64,128]{2,1,0:T(8,128)(2,1)S(1)} %pad_maximum_fusion.column, bf16[6,64,128]{2,1,0:T(8,128)(2,1)S(1)} %collective-permute-done.2.chip, ...), custom_call_target="tpu_custom_call" | custom-call | flops 33554432 | bytes 524288 | tf_op jit(solution)/shard_map/pallas_call | solution.py:271
  20.1 0.1 collective-permute-start.5
  20.2 2.0 %collective-permute-start.4 = (bf16[2,64,128]{2,1,0:T(8,128)(2,1)S(1)}, bf16[2,64,128]{2,1,0:T(8,128)(2,1)S(1)}, u32[]{:S(2)}, u32[]{:S(2)}) collective-permute-start(bf16[2,64,128]{2,1,0:T(8,128)(2,1)S(1)} %shard_map.58), channel_id=1, source_target_pairs={{0,1},{1,2},{2,3},{3,4},{4,5},{5,6},{6,7},{7,0},{8,9},{9,10},{10,1... | collective-permute-start | bytes 98312 | tf_op jit(solution)/shard_map/ppermute | solution.py:326
  22.2 1.9 %collective-permute-done.5 = bf16[2,64,128]{2,1,0:T(8,128)(2,1)S(1)} collective-permute-done((bf16[2,64,128]{2,1,0:T(8,128)(2,1)S(1)}, bf16[2,64,128]{2,1,0:T(8,128)(2,1)S(1)}, u32[]{:S(2)}, u32[]{:S(2)}) %collective-permute-start.5) | collective-permute-done | bytes 32800 | tf_op jit(solution)/shard_map/ppermute | solution.py:326
  24.1 1.3 %collective-permute-done.4 = bf16[2,64,128]{2,1,0:T(8,128)(2,1)S(1)} collective-permute-done((bf16[2,64,128]{2,1,0:T(8,128)(2,1)S(1)}, bf16[2,64,128]{2,1,0:T(8,128)(2,1)S(1)}, u32[]{:S(2)}, u32[]{:S(2)}) %collective-permute-start.4) | collective-permute-done | bytes 32800 | tf_op jit(solution)/shard_map/ppermute | solution.py:326
  25.4 1.0 %collective-permute-start.7 = (bf16[6,64,128]{2,1,0:T(8,128)(2,1)S(1)}, bf16[6,64,128]{2,1,0:T(8,128)(2,1)S(1)}, u32[]{:S(2)}, u32[]{:S(2)}) collective-permute-start(bf16[6,64,128]{2,1,0:T(8,128)(2,1)S(1)} %pad_maximum_fusion.1.column), channel_id=1, source_target_pairs={{0,248},{8,16},{16,8},{24,32},{32,24},{40,48},{48,40},{56,64},{64,... | collective-permute-start | bytes 294920 | tf_op jit(solution)/shard_map/ppermute | solution.py:330
  26.4 0.5 collective-permute-start.6
  26.9 3.0 %shard_map.57.own = bf16[32,64,128]{2,1,0:T(8,128)(2,1)S(1)} custom-call(s32[8,32]{1,0:T(8,128)S(1)} %bitcast.2, bf16[32,64,128]{2,1,0:T(8,128)(2,1)S(1)} %get-tuple-element.10.own, bf16[6,64,128]{2,1,0:T(8,128)(2,1)S(1)} %pad_maximum_fusion.column, bf16[6,64,128]{2,1,0:T(8,128)(2,1)S(1)} %collective-permute-done.2.chip, ...), custom_call_target="tpu_custom_call" | custom-call | flops 536870912 | bytes 8388608 | tf_op jit(solution)/shard_map/pallas_call | solution.py:282
  30.0 4.1 %shard_map.59 = (bf16[128,4096]{1,0:T(8,128)(2,1)S(1)}, f32[1,2176]{1,0:T(1,128)S(1)}) custom-call(s32[8,32]{1,0:T(8,128)S(1)} %bitcast.3, bf16[32,64,128]{2,1,0:T(8,128)(2,1)S(1)} %shard_map.57.own, bf16[6,64,128]{2,1,0:T(8,128)(2,1)S(1)} %pad_maximum_fusion.1.column, bf16[6,64,128]{2,1,0:T(8,128)(2,1)S(1)} %collective-permute-done.6.chip, ...), custom_call_target="tpu_custom_call" | custom-call | flops 536870912 | bytes 8388608 | tf_op jit(solution)/shard_map/pallas_call | solution.py:293
  34.1 0.1 collective-permute-start.8
  34.3 1.1 %collective-permute-done.8 = f32[1,2176]{1,0:T(1,128)S(1)} collective-permute-done((f32[1,2176]{1,0:T(1,128)S(1)}, f32[1,2176]{1,0:T(1,128)S(1)}, u32[]{:S(2)}, u32[]{:S(2)}) %collective-permute-start.8) | collective-permute-done | bytes 8736 | tf_op jit(solution)/shard_map/ppermute | solution.py:330
  35.4 0.1 broadcast_in_dim.7
  35.5 15.8 %all_to_all.10 = f32[16,1,2176]{2,1,0:T(1,128)S(1)} all-to-all(f32[16,1,2176]{2,1,0:T(1,128)S(1)} %broadcast_in_dim.7), channel_id=1, replica_groups={{0,16,32,48,64,80,96,112,128,144,160,176,192,208,224,240},{8,24,40,56,7..., dimensions={0} | all-to-all | bytes 278528 | tf_op jit(solution)/shard_map/all_to_all | solution.py:348
  51.3 0.1 reduce_sum.9
  51.4 11.2 %all_to_all.11.grams = f32[8,1,2176]{2,1,0:T(1,128)S(1)} all-to-all(f32[8,1,2176]{2,1,0:T(1,128)S(1)} %broadcast_in_dim.16), channel_id=1, replica_groups=mesh['wide'=32,'narrow'=8] {'narrow'}, dimensions={0} | all-to-all | bytes 139264 | tf_op jit(solution)/shard_map/all_to_all | solution.py:348
  62.6 3.2 %shard_map.60 = f32[64,4096]{1,0:T(8,128)} custom-call(f32[8,1,2176]{2,1,0:T(1,128)S(1)} %all_to_all.11.grams, bf16[128,4096]{1,0:T(8,128)(2,1)S(1)} %get-tuple-element.14.sketch), custom_call_target="tpu_custom_call" | custom-call | flops 201326592 | bytes 2097152 | tf_op jit(solution)/shard_map/pallas_call | solution.py:308
  (17 shorter events, 0.1 us)
Async XLA Ops:
  0.0 0.7 %copy-start = (s32[256,2]{0,1:T(2,128)S(1)}, s32[256,2]{0,1:T(2,128)}, u32[]{:S(2)}) copy-start(s32[256,2]{0,1:T(2,128)} %param.8) | copy-start | bytes 6148
  0.0 16.1 %copy-start.2 = (bf16[64,4096]{1,0:T(8,128)(2,1)S(1)}, bf16[64,4096]{1,0:T(8,128)(2,1)}, u32[]{:S(2)}) copy-start(bf16[64,4096]{1,0:T(8,128)(2,1)} %probe.3) | copy-start | bytes 1572868
  0.7 15.4 %copy-start.1 = (bf16[32,8,128,128]{3,2,1,0:T(8,128)(2,1)S(1)}, bf16[32,8,128,128]{3,2,1,0:T(8,128)(2,1)}, u32[]{:S(2)}) copy-start(bf16[32,8,128,128]{3,2,1,0:T(8,128)(2,1)} %weights.9) | copy-start | bytes 25165828
  0.9 18.2 %copy-start.3 = (s32[32,8]{0,1:T(8,128)S(1)}, s32[32,8]{0,1:T(8,128)}, u32[]{:S(2)}) copy-start(s32[32,8]{0,1:T(8,128)} %param.7) | copy-start | bytes 3076
  3.3 7.5 %collective-permute-start.1 = (bf16[2,64,128]{2,1,0:T(8,128)(2,1)S(1)}, bf16[2,64,128]{2,1,0:T(8,128)(2,1)S(1)}, u32[]{:S(2)}, u32[]{:S(2)}) collective-permute-start(bf16[2,64,128]{2,1,0:T(8,128)(2,1)S(1)} %shard_map.56), channel_id=1, source_target_pairs={{0,7},{1,0},{2,1},{3,2},{4,3},{5,4},{6,5},{7,6},{8,15},{9,8},{10,9... | collective-permute-start | bytes 98312 | tf_op jit(solution)/shard_map/ppermute | solution.py:326
  9.2 5.1 %collective-permute-start = (bf16[2,64,128]{2,1,0:T(8,128)(2,1)S(1)}, bf16[2,64,128]{2,1,0:T(8,128)(2,1)S(1)}, u32[]{:S(2)}, u32[]{:S(2)}) collective-permute-start(bf16[2,64,128]{2,1,0:T(8,128)(2,1)S(1)} %shard_map.56), channel_id=1, source_target_pairs={{0,1},{1,2},{2,3},{3,4},{4,5},{5,6},{6,7},{7,0},{8,9},{9,10},{10,1... | collective-permute-start | bytes 98312 | tf_op jit(solution)/shard_map/ppermute | solution.py:326
  14.3 4.7 %collective-permute-start.3 = (bf16[6,64,128]{2,1,0:T(8,128)(2,1)S(1)}, bf16[6,64,128]{2,1,0:T(8,128)(2,1)S(1)}, u32[]{:S(2)}, u32[]{:S(2)}) collective-permute-start(bf16[6,64,128]{2,1,0:T(8,128)(2,1)S(1)} %pad_maximum_fusion.column), channel_id=1, source_target_pairs={{0,248},{8,16},{16,8},{24,32},{32,24},{40,48},{48,40},{56,64},{64,... | collective-permute-start | bytes 294920 | tf_op jit(solution)/shard_map/ppermute | solution.py:330
  14.4 4.6 %collective-permute-start.2 = (bf16[6,64,128]{2,1,0:T(8,128)(2,1)S(1)}, bf16[6,64,128]{2,1,0:T(8,128)(2,1)S(1)}, u32[]{:S(2)}, u32[]{:S(2)}) collective-permute-start(bf16[6,64,128]{2,1,0:T(8,128)(2,1)S(1)} %pad_maximum_fusion.column), channel_id=1, source_target_pairs={{0,8},{8,0},{16,24},{24,16},{32,40},{40,32},{48,56},{56,48},{64,72... | collective-permute-start | bytes 294920 | tf_op jit(solution)/shard_map/ppermute | solution.py:330
  20.1 4.0 %collective-permute-start.5 = (bf16[2,64,128]{2,1,0:T(8,128)(2,1)S(1)}, bf16[2,64,128]{2,1,0:T(8,128)(2,1)S(1)}, u32[]{:S(2)}, u32[]{:S(2)}) collective-permute-start(bf16[2,64,128]{2,1,0:T(8,128)(2,1)S(1)} %shard_map.58), channel_id=1, source_target_pairs={{0,7},{1,0},{2,1},{3,2},{4,3},{5,4},{6,5},{7,6},{8,15},{9,8},{10,9... | collective-permute-start | bytes 98312 | tf_op jit(solution)/shard_map/ppermute | solution.py:326
  20.2 5.2 %collective-permute-start.4 = (bf16[2,64,128]{2,1,0:T(8,128)(2,1)S(1)}, bf16[2,64,128]{2,1,0:T(8,128)(2,1)S(1)}, u32[]{:S(2)}, u32[]{:S(2)}) collective-permute-start(bf16[2,64,128]{2,1,0:T(8,128)(2,1)S(1)} %shard_map.58), channel_id=1, source_target_pairs={{0,1},{1,2},{2,3},{3,4},{4,5},{5,6},{6,7},{7,0},{8,9},{9,10},{10,1... | collective-permute-start | bytes 98312 | tf_op jit(solution)/shard_map/ppermute | solution.py:326
  25.4 4.5 %collective-permute-start.7 = (bf16[6,64,128]{2,1,0:T(8,128)(2,1)S(1)}, bf16[6,64,128]{2,1,0:T(8,128)(2,1)S(1)}, u32[]{:S(2)}, u32[]{:S(2)}) collective-permute-start(bf16[6,64,128]{2,1,0:T(8,128)(2,1)S(1)} %pad_maximum_fusion.1.column), channel_id=1, source_target_pairs={{0,248},{8,16},{16,8},{24,32},{32,24},{40,48},{48,40},{56,64},{64,... | collective-permute-start | bytes 294920 | tf_op jit(solution)/shard_map/ppermute | solution.py:330
  26.4 3.5 %collective-permute-start.6 = (bf16[6,64,128]{2,1,0:T(8,128)(2,1)S(1)}, bf16[6,64,128]{2,1,0:T(8,128)(2,1)S(1)}, u32[]{:S(2)}, u32[]{:S(2)}) collective-permute-start(bf16[6,64,128]{2,1,0:T(8,128)(2,1)S(1)} %pad_maximum_fusion.1.column), channel_id=1, source_target_pairs={{0,8},{8,0},{16,24},{24,16},{32,40},{40,32},{48,56},{56,48},{64,72... | collective-permute-start | bytes 294920 | tf_op jit(solution)/shard_map/ppermute | solution.py:330
  34.1 1.3 %collective-permute-start.8 = (f32[1,2176]{1,0:T(1,128)S(1)}, f32[1,2176]{1,0:T(1,128)S(1)}, u32[]{:S(2)}, u32[]{:S(2)}) collective-permute-start(f32[1,2176]{1,0:T(1,128)S(1)} %get-tuple-element.13), channel_id=1, source_target_pairs={{0,8},{8,0},{16,24},{24,16},{32,40},{40,32},{48,56},{56,48},{64,72... | collective-permute-start | bytes 26120 | tf_op jit(solution)/shard_map/ppermute | solution.py:330

commit v6 on v5

--- a/solution.py
+++ b/solution.py
@@ -349,10 +349,11 @@
 
 
 def gathered_grams(gram):
-    chip = gram + swapped(gram, "wide", lambda i: i ^ 1)
-    count = lax.axis_size("wide")
-    groups = [list(range(core, count, 2)) for core in range(2)]
-    return from_all(jnp.sum(from_all(chip, "wide", groups), axis=0), "narrow")
+    wide, narrow = lax.axis_size("wide"), lax.axis_size("narrow")
+    groups = [list(range(core, wide, 2)) for core in range(2)]
+    plane = jnp.sum(from_all(gram, "wide", groups), axis=0)
+    lines = [[(2 * i + core) * narrow + j for core in range(2) for j in range(narrow)] for i in range(wide // 2)]
+    return from_all(plane, AXES, lines)
 
 
 def local(test_matrix, weights, block_cols, export_rows, row_count):

time: 65.9 us -> 65.7 us (level)
  the two profiles are of different devices: /device:TPU:8 before, /device:TPU:1 now
where the time goes in v6:
time: 65.7 us; the launch traced here: 65.5 us
  blocking collectives  23.1 us (35%)
  starting transfers between devices  17.9 us (27%)
  Pallas kernels  16.6 us (25%)
  waiting for transfers between devices  6.58 us (10%)
  between operations  0.86 us (1%)
    all_to_all x2, blocking collectives, from_all(): lax.all_to_all(copies, axis, 0, 0, axis_index_groups=groups, tiled=True)  23.1 us
    ppermute x4, starting transfers between devices, swapped(): lax.ppermute(value, axis, [(i, partner(i)) for i in range(lax.axis_size(a...  9.88 us
    ppermute x4, starting transfers between devices, shifted(): lax.ppermute(value, axis, [(i, (i + step) % count) for i in range(count)])  8.02 us
    ppermute x4, waiting for transfers between devices, shifted(): lax.ppermute(value, axis, [(i, (i + step) % count) for i in range(count)])  6.57 us
    pallas_call x1, Pallas kernels, sketch(): plain(sketch_kernel, [SMEM] + [VMEM] * 7, [VMEM, VMEM], [jax.ShapeDtypeSt...  4.14 us
    pallas_call x1, Pallas kernels, factor(): plain(functools.partial(factor_kernel, scale), [VMEM, VMEM], ANY, jax.Sha...  3.17 us
    pallas_call x1, Pallas kernels, second(): plain(second_kernel, [SMEM] + [VMEM] * 7, VMEM, jax.ShapeDtypeStruct((sel...  3.04 us
    pallas_call x1, Pallas kernels, first(): plain(first_kernel, [SMEM, VMEM, VMEM], [VMEM] * 3, [jax.ShapeDtypeStruct...  2.94 us
  transfers between devices with their start and end apart: 8, of which 4 were waited for; matrix products, arithmetic and copies ran while one was open for 0% of the time, Pallas kernels for 9%

profile of v6, /device:TPU:1, one launch (start us, length us, event | category | flops | bytes accessed | tf_op | source)
XLA Modules:
  0.0 65.5 jit_solution(12304921875127048311)
XLA Ops:
  0.7 0.0 copy-start.1
  0.7 0.2 dynamic-slice_reduce_fusion.exports
  0.9 2.3 %shard_map.56 = bf16[2,64,128]{2,1,0:T(8,128)(2,1)S(1)} custom-call(s32[2]{0:T(128)S(1)} %dynamic-slice_reduce_fusion.exports, s32[1]{0:T(128)S(6)} %copy.8.count, bf16[64,4096]{1,0:T(8,128)(2,1)} %probe.3, bf16[32,8,128,128]{3,2,1,0:T(8,128)(2,1)} %weights.9), custom_call_target="tpu_custom_call" | custom-call | flops 33554432 | bytes 524288 | tf_op jit(solution)/shard_map/pallas_call | solution.py:240
  3.3 6.5 %collective-permute-start.1 = (bf16[2,64,128]{2,1,0:T(8,128)(2,1)S(1)}, bf16[2,64,128]{2,1,0:T(8,128)(2,1)S(1)}, u32[]{:S(2)}, u32[]{:S(2)}) collective-permute-start(bf16[2,64,128]{2,1,0:T(8,128)(2,1)S(1)} %shard_map.56), channel_id=1, source_target_pairs={{0,7},{1,0},{2,1},{3,2},{4,3},{5,4},{6,5},{7,6},{8,15},{9,8},{10,9... | collective-permute-start | bytes 98312 | tf_op jit(solution)/shard_map/ppermute | solution.py:326
  9.8 1.0 %collective-permute-done.1 = bf16[2,64,128]{2,1,0:T(8,128)(2,1)S(1)} collective-permute-done((bf16[2,64,128]{2,1,0:T(8,128)(2,1)S(1)}, bf16[2,64,128]{2,1,0:T(8,128)(2,1)S(1)}, u32[]{:S(2)}, u32[]{:S(2)}) %collective-permute-start.1) | collective-permute-done | bytes 32800 | tf_op jit(solution)/shard_map/ppermute | solution.py:326
  10.8 3.0 %collective-permute-done = bf16[2,64,128]{2,1,0:T(8,128)(2,1)S(1)} collective-permute-done((bf16[2,64,128]{2,1,0:T(8,128)(2,1)S(1)}, bf16[2,64,128]{2,1,0:T(8,128)(2,1)S(1)}, u32[]{:S(2)}, u32[]{:S(2)}) %collective-permute-start) | collective-permute-done | bytes 32800 | tf_op jit(solution)/shard_map/ppermute | solution.py:326
  13.7 3.4 %collective-permute-start.3 = (bf16[6,64,128]{2,1,0:T(8,128)(2,1)S(1)}, bf16[6,64,128]{2,1,0:T(8,128)(2,1)S(1)}, u32[]{:S(2)}, u32[]{:S(2)}) collective-permute-start(bf16[6,64,128]{2,1,0:T(8,128)(2,1)S(1)} %pad_maximum_fusion.column), channel_id=1, source_target_pairs={{0,248},{8,16},{16,8},{24,32},{32,24},{40,48},{48,40},{56,64},{64,... | collective-permute-start | bytes 294920 | tf_op jit(solution)/shard_map/ppermute | solution.py:330
  17.1 2.0 %collective-permute-start.2 = (bf16[6,64,128]{2,1,0:T(8,128)(2,1)S(1)}, bf16[6,64,128]{2,1,0:T(8,128)(2,1)S(1)}, u32[]{:S(2)}, u32[]{:S(2)}) collective-permute-start(bf16[6,64,128]{2,1,0:T(8,128)(2,1)S(1)} %pad_maximum_fusion.column), channel_id=1, source_target_pairs={{0,8},{8,0},{16,24},{24,16},{32,40},{40,32},{48,56},{56,48},{64,72... | collective-permute-start | bytes 294920 | tf_op jit(solution)/shard_map/ppermute | solution.py:330
  19.2 2.9 %shard_map.55 = (f32[32,128]{1,0:T(8,128)S(1)}, f32[32,128]{1,0:T(8,128)S(1)}, bf16[32,64,128]{2,1,0:T(8,128)(2,1)S(1)}) custom-call(s32[1]{0:T(128)S(6)} %copy.8.count, bf16[64,4096]{1,0:T(8,128)(2,1)S(1)} %copy-done.2, bf16[32,8,128,128]{3,2,1,0:T(8,128)(2,1)S(1)} %copy-done.1), custom_call_target="tpu_custom_call" | custom-call | flops 536870912 | bytes 8388608 | tf_op jit(solution)/shard_map/pallas_call | solution.py:256
  22.1 1.0 %shard_map.58 = bf16[2,64,128]{2,1,0:T(8,128)(2,1)S(1)} custom-call(s32[2]{0:T(128)S(1)} %dynamic-slice_reduce_fusion.exports, s32[8,32]{1,0:T(8,128)S(1)} %bitcast.1, bf16[32,64,128]{2,1,0:T(8,128)(2,1)S(1)} %get-tuple-element.10.own, bf16[6,64,128]{2,1,0:T(8,128)(2,1)S(1)} %pad_maximum_fusion.column, bf16[6,64,128]{2,1,0:T(8,128)(2,1)S(1)} %collective-permute-done.2.chip, ...), custom_call_target="tpu_custom_call" | custom-call | flops 33554432 | bytes 524288 | tf_op jit(solution)/shard_map/pallas_call | solution.py:271
  23.1 0.1 collective-permute-start.5
  23.2 1.5 %collective-permute-start.4 = (bf16[2,64,128]{2,1,0:T(8,128)(2,1)S(1)}, bf16[2,64,128]{2,1,0:T(8,128)(2,1)S(1)}, u32[]{:S(2)}, u32[]{:S(2)}) collective-permute-start(bf16[2,64,128]{2,1,0:T(8,128)(2,1)S(1)} %shard_map.58), channel_id=1, source_target_pairs={{0,1},{1,2},{2,3},{3,4},{4,5},{5,6},{6,7},{7,0},{8,9},{9,10},{10,1... | collective-permute-start | bytes 98312 | tf_op jit(solution)/shard_map/ppermute | solution.py:326
  24.7 1.3 %collective-permute-done.5 = bf16[2,64,128]{2,1,0:T(8,128)(2,1)S(1)} collective-permute-done((bf16[2,64,128]{2,1,0:T(8,128)(2,1)S(1)}, bf16[2,64,128]{2,1,0:T(8,128)(2,1)S(1)}, u32[]{:S(2)}, u32[]{:S(2)}) %collective-permute-start.5) | collective-permute-done | bytes 32800 | tf_op jit(solution)/shard_map/ppermute | solution.py:326
  26.0 1.3 %collective-permute-done.4 = bf16[2,64,128]{2,1,0:T(8,128)(2,1)S(1)} collective-permute-done((bf16[2,64,128]{2,1,0:T(8,128)(2,1)S(1)}, bf16[2,64,128]{2,1,0:T(8,128)(2,1)S(1)}, u32[]{:S(2)}, u32[]{:S(2)}) %collective-permute-start.4) | collective-permute-done | bytes 32800 | tf_op jit(solution)/shard_map/ppermute | solution.py:326
  27.3 0.9 %collective-permute-start.7 = (bf16[6,64,128]{2,1,0:T(8,128)(2,1)S(1)}, bf16[6,64,128]{2,1,0:T(8,128)(2,1)S(1)}, u32[]{:S(2)}, u32[]{:S(2)}) collective-permute-start(bf16[6,64,128]{2,1,0:T(8,128)(2,1)S(1)} %pad_maximum_fusion.1.column), channel_id=1, source_target_pairs={{0,248},{8,16},{16,8},{24,32},{32,24},{40,48},{48,40},{56,64},{64,... | collective-permute-start | bytes 294920 | tf_op jit(solution)/shard_map/ppermute | solution.py:330
  28.2 3.6 %collective-permute-start.6 = (bf16[6,64,128]{2,1,0:T(8,128)(2,1)S(1)}, bf16[6,64,128]{2,1,0:T(8,128)(2,1)S(1)}, u32[]{:S(2)}, u32[]{:S(2)}) collective-permute-start(bf16[6,64,128]{2,1,0:T(8,128)(2,1)S(1)} %pad_maximum_fusion.1.column), channel_id=1, source_target_pairs={{0,8},{8,0},{16,24},{24,16},{32,40},{40,32},{48,56},{56,48},{64,72... | collective-permute-start | bytes 294920 | tf_op jit(solution)/shard_map/ppermute | solution.py:330
  31.8 3.0 %shard_map.57.own = bf16[32,64,128]{2,1,0:T(8,128)(2,1)S(1)} custom-call(s32[8,32]{1,0:T(8,128)S(1)} %bitcast.2, bf16[32,64,128]{2,1,0:T(8,128)(2,1)S(1)} %get-tuple-element.10.own, bf16[6,64,128]{2,1,0:T(8,128)(2,1)S(1)} %pad_maximum_fusion.column, bf16[6,64,128]{2,1,0:T(8,128)(2,1)S(1)} %collective-permute-done.2.chip, ...), custom_call_target="tpu_custom_call" | custom-call | flops 536870912 | bytes 8388608 | tf_op jit(solution)/shard_map/pallas_call | solution.py:282
  34.8 4.1 %shard_map.59 = (bf16[128,4096]{1,0:T(8,128)(2,1)S(1)}, f32[1,2176]{1,0:T(1,128)S(1)}) custom-call(s32[8,32]{1,0:T(8,128)S(1)} %bitcast.3, bf16[32,64,128]{2,1,0:T(8,128)(2,1)S(1)} %shard_map.57.own, bf16[6,64,128]{2,1,0:T(8,128)(2,1)S(1)} %pad_maximum_fusion.1.column, bf16[6,64,128]{2,1,0:T(8,128)(2,1)S(1)} %collective-permute-done.6.chip, ...), custom_call_target="tpu_custom_call" | custom-call | flops 536870912 | bytes 8388608 | tf_op jit(solution)/shard_map/pallas_call | solution.py:293
  39.0 0.1 broadcast_in_dim.7
  39.1 12.3 %all_to_all.10 = f32[16,1,2176]{2,1,0:T(1,128)S(1)} all-to-all(f32[16,1,2176]{2,1,0:T(1,128)S(1)} %broadcast_in_dim.7), channel_id=1, replica_groups={{0,16,32,48,64,80,96,112,128,144,160,176,192,208,224,240},{8,24,40,56,7..., dimensions={0} | all-to-all | bytes 278528 | tf_op jit(solution)/shard_map/all_to_all | solution.py:348
  51.4 0.1 reduce_sum.9
  51.5 0.1 broadcast_in_dim.16
  51.6 10.7 %all_to_all.11.grams = f32[16,1,2176]{2,1,0:T(1,128)S(1)} all-to-all(f32[16,1,2176]{2,1,0:T(1,128)S(1)} %broadcast_in_dim.16), channel_id=1, replica_groups={{0,1,2,3,4,5,6,7,8,9,10,11,12,13,14,15},{16,17,18,19,20,21,22,23,24,25,..., dimensions={0} | all-to-all | bytes 278528 | tf_op jit(solution)/shard_map/all_to_all | solution.py:348
  62.4 3.2 %shard_map.60 = f32[64,4096]{1,0:T(8,128)} custom-call(f32[16,1,2176]{2,1,0:T(1,128)S(1)} %all_to_all.11.grams, bf16[128,4096]{1,0:T(8,128)(2,1)S(1)} %get-tuple-element.14.sketch), custom_call_target="tpu_custom_call" | custom-call | flops 201326592 | bytes 2097152 | tf_op jit(solution)/shard_map/pallas_call | solution.py:308
  (15 shorter events, 0.1 us)
Async XLA Ops:
  0.0 0.7 %copy-start = (s32[256,2]{0,1:T(2,128)S(1)}, s32[256,2]{0,1:T(2,128)}, u32[]{:S(2)}) copy-start(s32[256,2]{0,1:T(2,128)} %param.8) | copy-start | bytes 6148
  0.0 19.2 %copy-start.2 = (bf16[64,4096]{1,0:T(8,128)(2,1)S(1)}, bf16[64,4096]{1,0:T(8,128)(2,1)}, u32[]{:S(2)}) copy-start(bf16[64,4096]{1,0:T(8,128)(2,1)} %probe.3) | copy-start | bytes 1572868
  0.7 18.4 %copy-start.1 = (bf16[32,8,128,128]{3,2,1,0:T(8,128)(2,1)S(1)}, bf16[32,8,128,128]{3,2,1,0:T(8,128)(2,1)}, u32[]{:S(2)}) copy-start(bf16[32,8,128,128]{3,2,1,0:T(8,128)(2,1)} %weights.9) | copy-start | bytes 25165828
  0.9 21.2 %copy-start.3 = (s32[32,8]{0,1:T(8,128)S(1)}, s32[32,8]{0,1:T(8,128)}, u32[]{:S(2)}) copy-start(s32[32,8]{0,1:T(8,128)} %param.7) | copy-start | bytes 3076
  3.3 7.5 %collective-permute-start.1 = (bf16[2,64,128]{2,1,0:T(8,128)(2,1)S(1)}, bf16[2,64,128]{2,1,0:T(8,128)(2,1)S(1)}, u32[]{:S(2)}, u32[]{:S(2)}) collective-permute-start(bf16[2,64,128]{2,1,0:T(8,128)(2,1)S(1)} %shard_map.56), channel_id=1, source_target_pairs={{0,7},{1,0},{2,1},{3,2},{4,3},{5,4},{6,5},{7,6},{8,15},{9,8},{10,9... | collective-permute-start | bytes 98312 | tf_op jit(solution)/shard_map/ppermute | solution.py:326
  9.8 4.0 %collective-permute-start = (bf16[2,64,128]{2,1,0:T(8,128)(2,1)S(1)}, bf16[2,64,128]{2,1,0:T(8,128)(2,1)S(1)}, u32[]{:S(2)}, u32[]{:S(2)}) collective-permute-start(bf16[2,64,128]{2,1,0:T(8,128)(2,1)S(1)} %shard_map.56), channel_id=1, source_target_pairs={{0,1},{1,2},{2,3},{3,4},{4,5},{5,6},{6,7},{7,0},{8,9},{9,10},{10,1... | collective-permute-start | bytes 98312 | tf_op jit(solution)/shard_map/ppermute | solution.py:326
  13.7 8.4 %collective-permute-start.3 = (bf16[6,64,128]{2,1,0:T(8,128)(2,1)S(1)}, bf16[6,64,128]{2,1,0:T(8,128)(2,1)S(1)}, u32[]{:S(2)}, u32[]{:S(2)}) collective-permute-start(bf16[6,64,128]{2,1,0:T(8,128)(2,1)S(1)} %pad_maximum_fusion.column), channel_id=1, source_target_pairs={{0,248},{8,16},{16,8},{24,32},{32,24},{40,48},{48,40},{56,64},{64,... | collective-permute-start | bytes 294920 | tf_op jit(solution)/shard_map/ppermute | solution.py:330
  17.1 5.0 %collective-permute-start.2 = (bf16[6,64,128]{2,1,0:T(8,128)(2,1)S(1)}, bf16[6,64,128]{2,1,0:T(8,128)(2,1)S(1)}, u32[]{:S(2)}, u32[]{:S(2)}) collective-permute-start(bf16[6,64,128]{2,1,0:T(8,128)(2,1)S(1)} %pad_maximum_fusion.column), channel_id=1, source_target_pairs={{0,8},{8,0},{16,24},{24,16},{32,40},{40,32},{48,56},{56,48},{64,72... | collective-permute-start | bytes 294920 | tf_op jit(solution)/shard_map/ppermute | solution.py:330
  23.1 2.8 %collective-permute-start.5 = (bf16[2,64,128]{2,1,0:T(8,128)(2,1)S(1)}, bf16[2,64,128]{2,1,0:T(8,128)(2,1)S(1)}, u32[]{:S(2)}, u32[]{:S(2)}) collective-permute-start(bf16[2,64,128]{2,1,0:T(8,128)(2,1)S(1)} %shard_map.58), channel_id=1, source_target_pairs={{0,7},{1,0},{2,1},{3,2},{4,3},{5,4},{6,5},{7,6},{8,15},{9,8},{10,9... | collective-permute-start | bytes 98312 | tf_op jit(solution)/shard_map/ppermute | solution.py:326
  23.2 4.1 %collective-permute-start.4 = (bf16[2,64,128]{2,1,0:T(8,128)(2,1)S(1)}, bf16[2,64,128]{2,1,0:T(8,128)(2,1)S(1)}, u32[]{:S(2)}, u32[]{:S(2)}) collective-permute-start(bf16[2,64,128]{2,1,0:T(8,128)(2,1)S(1)} %shard_map.58), channel_id=1, source_target_pairs={{0,1},{1,2},{2,3},{3,4},{4,5},{5,6},{6,7},{7,0},{8,9},{9,10},{10,1... | collective-permute-start | bytes 98312 | tf_op jit(solution)/shard_map/ppermute | solution.py:326
  27.3 7.5 %collective-permute-start.7 = (bf16[6,64,128]{2,1,0:T(8,128)(2,1)S(1)}, bf16[6,64,128]{2,1,0:T(8,128)(2,1)S(1)}, u32[]{:S(2)}, u32[]{:S(2)}) collective-permute-start(bf16[6,64,128]{2,1,0:T(8,128)(2,1)S(1)} %pad_maximum_fusion.1.column), channel_id=1, source_target_pairs={{0,248},{8,16},{16,8},{24,32},{32,24},{40,48},{48,40},{56,64},{64,... | collective-permute-start | bytes 294920 | tf_op jit(solution)/shard_map/ppermute | solution.py:330
  28.2 6.6 %collective-permute-start.6 = (bf16[6,64,128]{2,1,0:T(8,128)(2,1)S(1)}, bf16[6,64,128]{2,1,0:T(8,128)(2,1)S(1)}, u32[]{:S(2)}, u32[]{:S(2)}) collective-permute-start(bf16[6,64,128]{2,1,0:T(8,128)(2,1)S(1)} %pad_maximum_fusion.1.column), channel_id=1, source_target_pairs={{0,8},{8,0},{16,24},{24,16},{32,40},{40,32},{48,56},{56,48},{64,72... | collective-permute-start | bytes 294920 | tf_op jit(solution)/shard_map/ppermute | solution.py:330

commit v7 on v5

--- a/solution.py
+++ b/solution.py
@@ -62,25 +62,26 @@
 def first_kernel(count, probe, weights, degree_out, live_out, out):
     rows, size = weights.shape[0], weights.shape[2]
 
-    @pl.loop(0, rows // ROWS_STEP)
-    def _(step):
-        for i in range(ROWS_STEP):
-            row = step * ROWS_STEP + i
-            degree = block_degree(weights[row])
-            degree_out[pl.ds(row, 1), :] = degree
-            live = live_mask(row, size, count[0])
-            live_out[pl.ds(row, 1), :] = live
-            out[row] = scaled(probe[:, pl.ds(pl.multiple_of(row * size, size), size)], degree, live)
+    for row in range(rows):
+        degree = block_degree(weights[row])
+        degree_out[row : row + 1, :] = degree
+        live = live_mask(row, size, count[0])
+        live_out[row : row + 1, :] = live
+        out[row] = scaled(probe[:, row * size : (row + 1) * size], degree, live)
 
 
 def fill_table(table, own, column, chip, other):
     start = own.shape[0]
     table[:start] = own[...]
     group = column.shape[0]
-    odd = lax.axis_index("wide") & 1
-    table[start + group : start + 2 * group] = column[...]
-    table[pl.ds(start + 2 * group * (1 - odd), group)] = chip[...]
-    table[pl.ds(start + 2 * group * odd, group)] = other[...]
+    each = group // 3
+    odd, narrow_odd = lax.axis_index("wide") & 1, lax.axis_index("narrow") & 1
+    sources = ((column, group), (chip, 2 * group * (1 - odd)), (other, 2 * group * odd))
+    for source, place in sources:
+        place = start + place
+        table[pl.ds(place + 2 * each * (1 - narrow_odd), each)] = source[:each]
+        table[pl.ds(place + each, each)] = source[each : 2 * each]
+        table[pl.ds(place + 2 * each * narrow_odd, each)] = source[2 * each :]
 
 
 def applied(table, slots, row, blocks):
@@ -236,7 +237,7 @@
         self.table = pltpu.VMEM((row_blocks + halo, columns, size), jnp.bfloat16)
 
     def export_first(self, exports, count, probe, weights):
-        pieces = 4
+        pieces = 1
         return plain(
             export_first_kernel,
             [SMEM, SMEM, ANY, ANY],
@@ -321,17 +322,15 @@
         )(grams, sketch)
 
 
-def shifted(value, axis, step):
-    count = lax.axis_size(axis)
-    return lax.ppermute(value, axis, [(i, (i + step) % count) for i in range(count)])
-
-
 def swapped(value, axis, partner):
     return lax.ppermute(value, axis, [(i, partner(i)) for i in range(lax.axis_size(axis))])
 
 
 def along_narrow(exports):
-    return shifted(exports, "narrow", 1), shifted(exports, "narrow", -1)
+    count = lax.axis_size("narrow")
+    near = swapped(exports, "narrow", lambda i: i ^ 1)
+    far = swapped(exports, "narrow", lambda i: (i + 1) % count if i % 2 else (i - 1) % count)
+    return near, far
 
 
 def halo_blocks(before, exports, after):

time: 65.9 us -> 66 us (level)
  blocking collectives: 27 us -> 28.7 us
    ppermute x4 -> x0, waiting for transfers between devices: 8.31 us -> none  [shifted(): lax.ppermute(value, axis, [(i, (i + step) % count) for i in range(count)])]
    ppermute x4 -> x0, starting transfers between devices: 8.03 us -> none  [shifted(): lax.ppermute(value, axis, [(i, (i + step) % count) for i in range(count)])]
    ppermute x5 -> x9, waiting for transfers between devices: 1.13 us -> 8.99 us  [swapped(): lax.ppermute(value, axis, [(i, partner(i)) for i in range(lax.axis_size(a...]
    ppermute x5 -> x9, starting transfers between devices: 3.4 us -> 10.8 us  [swapped(): lax.ppermute(value, axis, [(i, partner(i)) for i in range(lax.axis_size(a...]
    all_to_all x2, blocking collectives: 27 us -> 28.7 us  [from_all(): lax.all_to_all(copies, axis, 0, 0, axis_index_groups=groups, tiled=True)]
  transfers between devices with their start and end apart: 9 -> 9, of which waited for: 5 -> 4; matrix products, arithmetic and copies ran while one was open for 0% -> 0% of each run, Pallas kernels for 9% -> 8%
where the time goes in v7:
time: 66 us; the launch traced here: 65.8 us
  blocking collectives  28.7 us (43%)
  Pallas kernels  16 us (24%)
  starting transfers between devices  10.8 us (16%)
  waiting for transfers between devices  8.99 us (14%)
  between operations  0.87 us (1%)
    all_to_all x2, blocking collectives, from_all(): lax.all_to_all(copies, axis, 0, 0, axis_index_groups=groups, tiled=True)  28.7 us
    ppermute x9, starting transfers between devices, swapped(): lax.ppermute(value, axis, [(i, partner(i)) for i in range(lax.axis_size(a...  10.8 us
    ppermute x9, waiting for transfers between devices, swapped(): lax.ppermute(value, axis, [(i, partner(i)) for i in range(lax.axis_size(a...  8.99 us
    pallas_call x1, Pallas kernels, sketch(): plain(sketch_kernel, [SMEM] + [VMEM] * 7, [VMEM, VMEM], [jax.ShapeDtypeSt...  4.14 us
    pallas_call x1, Pallas kernels, factor(): plain(functools.partial(factor_kernel, scale), [VMEM, VMEM], ANY, jax.Sha...  3.16 us
    pallas_call x1, Pallas kernels, second(): plain(second_kernel, [SMEM] + [VMEM] * 7, VMEM, jax.ShapeDtypeStruct((sel...  3.04 us
    pallas_call x1, Pallas kernels, first(): plain(first_kernel, [SMEM, VMEM, VMEM], [VMEM] * 3, [jax.ShapeDtypeStruct...  2.4 us
    pallas_call x1, Pallas kernels, export_first(): plain(export_first_kernel, [SMEM, SMEM, ANY, ANY], VMEM, jax.ShapeDtypeSt...  2.27 us
  transfers between devices with their start and end apart: 9, of which 4 were waited for; matrix products, arithmetic and copies ran while one was open for 0% of the time, Pallas kernels for 8%

profile of v7, /device:TPU:8, one launch (start us, length us, event | category | flops | bytes accessed | tf_op | source)
XLA Modules:
  0.0 65.8 jit_solution(7246991918420500717)
XLA Ops:
  0.7 0.0 copy-start.1
  0.7 0.2 dynamic-slice_reduce_fusion.exports
  0.9 2.3 %shard_map.56 = bf16[2,64,128]{2,1,0:T(8,128)(2,1)S(1)} custom-call(s32[2]{0:T(128)S(1)} %dynamic-slice_reduce_fusion.exports, s32[1]{0:T(128)S(6)} %copy.8.count, bf16[64,4096]{1,0:T(8,128)(2,1)} %probe.3, bf16[32,8,128,128]{3,2,1,0:T(8,128)(2,1)} %weights.9), custom_call_target="tpu_custom_call" | custom-call | flops 33554432 | bytes 524288 | tf_op jit(solution)/shard_map/pallas_call | solution.py:241
  3.2 5.9 %collective-permute-start.1 = (bf16[2,64,128]{2,1,0:T(8,128)(2,1)S(1)}, bf16[2,64,128]{2,1,0:T(8,128)(2,1)S(1)}, u32[]{:S(2)}, u32[]{:S(2)}) collective-permute-start(bf16[2,64,128]{2,1,0:T(8,128)(2,1)S(1)} %shard_map.56), channel_id=1, source_target_pairs={{0,7},{1,2},{2,1},{3,4},{4,3},{5,6},{6,5},{7,0},{8,15},{9,10},{10,... | collective-permute-start | bytes 98312 | tf_op jit(solution)/shard_map/ppermute | solution.py:326
  9.2 0.0 collective-permute-start
  9.2 1.9 %collective-permute-done.1 = bf16[2,64,128]{2,1,0:T(8,128)(2,1)S(1)} collective-permute-done((bf16[2,64,128]{2,1,0:T(8,128)(2,1)S(1)}, bf16[2,64,128]{2,1,0:T(8,128)(2,1)S(1)}, u32[]{:S(2)}, u32[]{:S(2)}) %collective-permute-start.1) | collective-permute-done | bytes 32800 | tf_op jit(solution)/shard_map/ppermute | solution.py:326
  11.0 2.0 %collective-permute-done = bf16[2,64,128]{2,1,0:T(8,128)(2,1)S(1)} collective-permute-done((bf16[2,64,128]{2,1,0:T(8,128)(2,1)S(1)}, bf16[2,64,128]{2,1,0:T(8,128)(2,1)S(1)}, u32[]{:S(2)}, u32[]{:S(2)}) %collective-permute-start) | collective-permute-done | bytes 32800 | tf_op jit(solution)/shard_map/ppermute | solution.py:326
  13.1 0.1 collective-permute-start.3
  13.2 1.7 %collective-permute-start.2 = (bf16[6,64,128]{2,1,0:T(8,128)(2,1)S(1)}, bf16[6,64,128]{2,1,0:T(8,128)(2,1)S(1)}, u32[]{:S(2)}, u32[]{:S(2)}) collective-permute-start(bf16[6,64,128]{2,1,0:T(8,128)(2,1)S(1)} %pad_maximum_fusion.column), channel_id=1, source_target_pairs={{0,8},{8,0},{16,24},{24,16},{32,40},{40,32},{48,56},{56,48},{64,72... | collective-permute-start | bytes 294920 | tf_op jit(solution)/shard_map/ppermute | solution.py:326
  14.9 2.4 %shard_map.55 = (f32[32,128]{1,0:T(8,128)S(1)}, f32[32,128]{1,0:T(8,128)S(1)}, bf16[32,64,128]{2,1,0:T(8,128)(2,1)S(1)}) custom-call(s32[1]{0:T(128)S(6)} %copy.8.count, bf16[64,4096]{1,0:T(8,128)(2,1)S(1)} %copy-done.2, bf16[32,8,128,128]{3,2,1,0:T(8,128)(2,1)S(1)} %copy-done.1), custom_call_target="tpu_custom_call" | custom-call | flops 536870912 | bytes 8388608 | tf_op jit(solution)/shard_map/pallas_call | solution.py:257
  17.3 1.0 %shard_map.58 = bf16[2,64,128]{2,1,0:T(8,128)(2,1)S(1)} custom-call(s32[2]{0:T(128)S(1)} %dynamic-slice_reduce_fusion.exports, s32[8,32]{1,0:T(8,128)S(1)} %bitcast.1, bf16[32,64,128]{2,1,0:T(8,128)(2,1)S(1)} %get-tuple-element.10.own, bf16[6,64,128]{2,1,0:T(8,128)(2,1)S(1)} %pad_maximum_fusion.column, bf16[6,64,128]{2,1,0:T(8,128)(2,1)S(1)} %collective-permute-done.2.chip, ...), custom_call_target="tpu_custom_call" | custom-call | flops 33554432 | bytes 524288 | tf_op jit(solution)/shard_map/pallas_call | solution.py:272
  18.3 1.3 %collective-permute-start.5 = (bf16[2,64,128]{2,1,0:T(8,128)(2,1)S(1)}, bf16[2,64,128]{2,1,0:T(8,128)(2,1)S(1)}, u32[]{:S(2)}, u32[]{:S(2)}) collective-permute-start(bf16[2,64,128]{2,1,0:T(8,128)(2,1)S(1)} %shard_map.58), channel_id=1, source_target_pairs={{0,7},{1,2},{2,1},{3,4},{4,3},{5,6},{6,5},{7,0},{8,15},{9,10},{10,... | collective-permute-start | bytes 98312 | tf_op jit(solution)/shard_map/ppermute | solution.py:326
  19.6 3.9 %collective-permute-done.5 = bf16[2,64,128]{2,1,0:T(8,128)(2,1)S(1)} collective-permute-done((bf16[2,64,128]{2,1,0:T(8,128)(2,1)S(1)}, bf16[2,64,128]{2,1,0:T(8,128)(2,1)S(1)}, u32[]{:S(2)}, u32[]{:S(2)}) %collective-permute-start.5) | collective-permute-done | bytes 32800 | tf_op jit(solution)/shard_map/ppermute | solution.py:326
  23.5 1.0 %collective-permute-start.7 = (bf16[6,64,128]{2,1,0:T(8,128)(2,1)S(1)}, bf16[6,64,128]{2,1,0:T(8,128)(2,1)S(1)}, u32[]{:S(2)}, u32[]{:S(2)}) collective-permute-start(bf16[6,64,128]{2,1,0:T(8,128)(2,1)S(1)} %pad_maximum_fusion.1.column), channel_id=1, source_target_pairs={{0,248},{8,16},{16,8},{24,32},{32,24},{40,48},{48,40},{56,64},{64,... | collective-permute-start | bytes 294920 | tf_op jit(solution)/shard_map/ppermute | solution.py:326
  24.6 0.7 %collective-permute-start.6 = (bf16[6,64,128]{2,1,0:T(8,128)(2,1)S(1)}, bf16[6,64,128]{2,1,0:T(8,128)(2,1)S(1)}, u32[]{:S(2)}, u32[]{:S(2)}) collective-permute-start(bf16[6,64,128]{2,1,0:T(8,128)(2,1)S(1)} %pad_maximum_fusion.1.column), channel_id=1, source_target_pairs={{0,8},{8,0},{16,24},{24,16},{32,40},{40,32},{48,56},{56,48},{64,72... | collective-permute-start | bytes 294920 | tf_op jit(solution)/shard_map/ppermute | solution.py:326
  25.2 3.0 %shard_map.57.own = bf16[32,64,128]{2,1,0:T(8,128)(2,1)S(1)} custom-call(s32[8,32]{1,0:T(8,128)S(1)} %bitcast.2, bf16[32,64,128]{2,1,0:T(8,128)(2,1)S(1)} %get-tuple-element.10.own, bf16[6,64,128]{2,1,0:T(8,128)(2,1)S(1)} %pad_maximum_fusion.column, bf16[6,64,128]{2,1,0:T(8,128)(2,1)S(1)} %collective-permute-done.2.chip, ...), custom_call_target="tpu_custom_call" | custom-call | flops 536870912 | bytes 8388608 | tf_op jit(solution)/shard_map/pallas_call | solution.py:283
  28.3 4.1 %shard_map.59 = (bf16[128,4096]{1,0:T(8,128)(2,1)S(1)}, f32[1,2176]{1,0:T(1,128)S(1)}) custom-call(s32[8,32]{1,0:T(8,128)S(1)} %bitcast.3, bf16[32,64,128]{2,1,0:T(8,128)(2,1)S(1)} %shard_map.57.own, bf16[6,64,128]{2,1,0:T(8,128)(2,1)S(1)} %pad_maximum_fusion.1.column, bf16[6,64,128]{2,1,0:T(8,128)(2,1)S(1)} %collective-permute-done.6.chip, ...), custom_call_target="tpu_custom_call" | custom-call | flops 536870912 | bytes 8388608 | tf_op jit(solution)/shard_map/pallas_call | solution.py:294
  32.5 0.1 collective-permute-start.8
  32.6 1.2 %collective-permute-done.8 = f32[1,2176]{1,0:T(1,128)S(1)} collective-permute-done((f32[1,2176]{1,0:T(1,128)S(1)}, f32[1,2176]{1,0:T(1,128)S(1)}, u32[]{:S(2)}, u32[]{:S(2)}) %collective-permute-start.8) | collective-permute-done | bytes 8736 | tf_op jit(solution)/shard_map/ppermute | solution.py:326
  33.7 0.1 broadcast_in_dim.7
  33.8 16.1 %all_to_all.10 = f32[16,1,2176]{2,1,0:T(1,128)S(1)} all-to-all(f32[16,1,2176]{2,1,0:T(1,128)S(1)} %broadcast_in_dim.7), channel_id=1, replica_groups={{0,16,32,48,64,80,96,112,128,144,160,176,192,208,224,240},{8,24,40,56,7..., dimensions={0} | all-to-all | bytes 278528 | tf_op jit(solution)/shard_map/all_to_all | solution.py:347
  49.9 0.1 reduce_sum.9
  50.1 12.6 %all_to_all.11.grams = f32[8,1,2176]{2,1,0:T(1,128)S(1)} all-to-all(f32[8,1,2176]{2,1,0:T(1,128)S(1)} %broadcast_in_dim.16), channel_id=1, replica_groups=mesh['wide'=32,'narrow'=8] {'narrow'}, dimensions={0} | all-to-all | bytes 139264 | tf_op jit(solution)/shard_map/all_to_all | solution.py:347
  62.6 3.2 %shard_map.60 = f32[64,4096]{1,0:T(8,128)} custom-call(f32[8,1,2176]{2,1,0:T(1,128)S(1)} %all_to_all.11.grams, bf16[128,4096]{1,0:T(8,128)(2,1)S(1)} %get-tuple-element.14.sketch), custom_call_target="tpu_custom_call" | custom-call | flops 201326592 | bytes 2097152 | tf_op jit(solution)/shard_map/pallas_call | solution.py:309
  (17 shorter events, 0.1 us)
Async XLA Ops:
  0.0 0.7 %copy-start = (s32[256,2]{0,1:T(2,128)S(1)}, s32[256,2]{0,1:T(2,128)}, u32[]{:S(2)}) copy-start(s32[256,2]{0,1:T(2,128)} %param.8) | copy-start | bytes 6148
  0.0 14.9 %copy-start.2 = (bf16[64,4096]{1,0:T(8,128)(2,1)S(1)}, bf16[64,4096]{1,0:T(8,128)(2,1)}, u32[]{:S(2)}) copy-start(bf16[64,4096]{1,0:T(8,128)(2,1)} %probe.3) | copy-start | bytes 1572868
  0.7 14.1 %copy-start.1 = (bf16[32,8,128,128]{3,2,1,0:T(8,128)(2,1)S(1)}, bf16[32,8,128,128]{3,2,1,0:T(8,128)(2,1)}, u32[]{:S(2)}) copy-start(bf16[32,8,128,128]{3,2,1,0:T(8,128)(2,1)} %weights.9) | copy-start | bytes 25165828
  0.9 16.4 %copy-start.3 = (s32[32,8]{0,1:T(8,128)S(1)}, s32[32,8]{0,1:T(8,128)}, u32[]{:S(2)}) copy-start(s32[32,8]{0,1:T(8,128)} %param.7) | copy-start | bytes 3076
  3.2 7.8 %collective-permute-start.1 = (bf16[2,64,128]{2,1,0:T(8,128)(2,1)S(1)}, bf16[2,64,128]{2,1,0:T(8,128)(2,1)S(1)}, u32[]{:S(2)}, u32[]{:S(2)}) collective-permute-start(bf16[2,64,128]{2,1,0:T(8,128)(2,1)S(1)} %shard_map.56), channel_id=1, source_target_pairs={{0,7},{1,2},{2,1},{3,4},{4,3},{5,6},{6,5},{7,0},{8,15},{9,10},{10,... | collective-permute-start | bytes 98312 | tf_op jit(solution)/shard_map/ppermute | solution.py:326
  9.2 3.9 %collective-permute-start = (bf16[2,64,128]{2,1,0:T(8,128)(2,1)S(1)}, bf16[2,64,128]{2,1,0:T(8,128)(2,1)S(1)}, u32[]{:S(2)}, u32[]{:S(2)}) collective-permute-start(bf16[2,64,128]{2,1,0:T(8,128)(2,1)S(1)} %shard_map.56), channel_id=1, source_target_pairs={{0,1},{1,0},{2,3},{3,2},{4,5},{5,4},{6,7},{7,6},{8,9},{9,8},{10,11... | collective-permute-start | bytes 98312 | tf_op jit(solution)/shard_map/ppermute | solution.py:326
  13.1 4.2 %collective-permute-start.3 = (bf16[6,64,128]{2,1,0:T(8,128)(2,1)S(1)}, bf16[6,64,128]{2,1,0:T(8,128)(2,1)S(1)}, u32[]{:S(2)}, u32[]{:S(2)}) collective-permute-start(bf16[6,64,128]{2,1,0:T(8,128)(2,1)S(1)} %pad_maximum_fusion.column), channel_id=1, source_target_pairs={{0,248},{8,16},{16,8},{24,32},{32,24},{40,48},{48,40},{56,64},{64,... | collective-permute-start | bytes 294920 | tf_op jit(solution)/shard_map/ppermute | solution.py:326
  13.2 4.1 %collective-permute-start.2 = (bf16[6,64,128]{2,1,0:T(8,128)(2,1)S(1)}, bf16[6,64,128]{2,1,0:T(8,128)(2,1)S(1)}, u32[]{:S(2)}, u32[]{:S(2)}) collective-permute-start(bf16[6,64,128]{2,1,0:T(8,128)(2,1)S(1)} %pad_maximum_fusion.column), channel_id=1, source_target_pairs={{0,8},{8,0},{16,24},{24,16},{32,40},{40,32},{48,56},{56,48},{64,72... | collective-permute-start | bytes 294920 | tf_op jit(solution)/shard_map/ppermute | solution.py:326
  18.3 5.2 %collective-permute-start.5 = (bf16[2,64,128]{2,1,0:T(8,128)(2,1)S(1)}, bf16[2,64,128]{2,1,0:T(8,128)(2,1)S(1)}, u32[]{:S(2)}, u32[]{:S(2)}) collective-permute-start(bf16[2,64,128]{2,1,0:T(8,128)(2,1)S(1)} %shard_map.58), channel_id=1, source_target_pairs={{0,7},{1,2},{2,1},{3,4},{4,3},{5,6},{6,5},{7,0},{8,15},{9,10},{10,... | collective-permute-start | bytes 98312 | tf_op jit(solution)/shard_map/ppermute | solution.py:326
  19.6 3.9 %collective-permute-start.4 = (bf16[2,64,128]{2,1,0:T(8,128)(2,1)S(1)}, bf16[2,64,128]{2,1,0:T(8,128)(2,1)S(1)}, u32[]{:S(2)}, u32[]{:S(2)}) collective-permute-start(bf16[2,64,128]{2,1,0:T(8,128)(2,1)S(1)} %shard_map.58), channel_id=1, source_target_pairs={{0,1},{1,0},{2,3},{3,2},{4,5},{5,4},{6,7},{7,6},{8,9},{9,8},{10,11... | collective-permute-start | bytes 98312 | tf_op jit(solution)/shard_map/ppermute | solution.py:326
  23.5 4.7 %collective-permute-start.7 = (bf16[6,64,128]{2,1,0:T(8,128)(2,1)S(1)}, bf16[6,64,128]{2,1,0:T(8,128)(2,1)S(1)}, u32[]{:S(2)}, u32[]{:S(2)}) collective-permute-start(bf16[6,64,128]{2,1,0:T(8,128)(2,1)S(1)} %pad_maximum_fusion.1.column), channel_id=1, source_target_pairs={{0,248},{8,16},{16,8},{24,32},{32,24},{40,48},{48,40},{56,64},{64,... | collective-permute-start | bytes 294920 | tf_op jit(solution)/shard_map/ppermute | solution.py:326
  24.6 3.7 %collective-permute-start.6 = (bf16[6,64,128]{2,1,0:T(8,128)(2,1)S(1)}, bf16[6,64,128]{2,1,0:T(8,128)(2,1)S(1)}, u32[]{:S(2)}, u32[]{:S(2)}) collective-permute-start(bf16[6,64,128]{2,1,0:T(8,128)(2,1)S(1)} %pad_maximum_fusion.1.column), channel_id=1, source_target_pairs={{0,8},{8,0},{16,24},{24,16},{32,40},{40,32},{48,56},{56,48},{64,72... | collective-permute-start | bytes 294920 | tf_op jit(solution)/shard_map/ppermute | solution.py:326
  32.5 1.3 %collective-permute-start.8 = (f32[1,2176]{1,0:T(1,128)S(1)}, f32[1,2176]{1,0:T(1,128)S(1)}, u32[]{:S(2)}, u32[]{:S(2)}) collective-permute-start(f32[1,2176]{1,0:T(1,128)S(1)} %get-tuple-element.13), channel_id=1, source_target_pairs={{0,8},{8,0},{16,24},{24,16},{32,40},{40,32},{48,56},{56,48},{64,72... | collective-permute-start | bytes 26120 | tf_op jit(solution)/shard_map/ppermute | solution.py:326
